TPU v7x, 32 devices: a whole 2x2x4 slice. The times are simulated.
32 devices in a mesh: dp: 2 (over y), tile: 16 (over z, x, core).
Axes of the slice: x: 2, y: 2, z: 4, core: 2. Of those that a mesh axis runs over, the one named last changes fastest.
Arguments:
- videos: bfloat16 [2, 16, 32, 64, 512], P('dp', 'tile'), may hold values from -6 to 6
- spatial_filter: bfloat16 [9, 512, 512], P(None, 'dp'), may hold values from -0.09375 to 0.09375
- temporal_filter: bfloat16 [3, 512, 512], P(None, 'dp'), may hold values from -0.15625 to 0.15625
- spatial_bias: float32 [512], replicated, may hold values from -3 to 3
- temporal_bias: float32 [512], replicated, may hold values from -3 to 3
Outputs:
- output: bfloat16 [2, 16, 32, 64, 512], P('dp', 'tile')
All inputs are finite; a program needn't handle non-finite values.
Results may differ from a plain program's by a relative error of at most 0.0044.
Values may be sent and summed in bfloat16 or wider, within the bound.
No kernel may reach another device: no remote copies, remote signals or barrier semaphores. Data moves between devices by JAX's collectives and lax.ppermute only.
A program may use at most 128 MiB of HBM per device.

v0:
```python
import jax
import jax.numpy as jnp
from jax import lax
from jax.sharding import PartitionSpec as P


def padded_2(block, sides, width):
    for axis, dim in sides:
        count = lax.axis_size(axis)
        forward = [(i, i + 1) for i in range(count - 1)]
        backward = [(target, source) for source, target in forward]
        low = lax.ppermute(
            lax.slice_in_dim(block, block.shape[dim] - width, None, axis=dim), axis, forward
        )
        high = lax.ppermute(lax.slice_in_dim(block, 0, width, axis=dim), axis, backward)
        block = jnp.concatenate([low, block, high], axis=dim)
    return block


def spatial_term(padded, weight_piece):
    width = weight_piece.shape[1]
    height = padded.shape[2] - 2
    breadth = padded.shape[3] - 2
    columns = jnp.concatenate(
        [
            padded[:, :, row_off : row_off + height, col_off : col_off + breadth, :]
            for row_off in range(3)
            for col_off in range(3)
        ],
        axis=4,
    )
    matrix = weight_piece.reshape(9 * width, weight_piece.shape[2])
    return jnp.dot(columns.reshape(-1, 9 * width), matrix, preferred_element_type=jnp.float32)


def temporal_term(framed, weight_piece):
    width = weight_piece.shape[1]
    frames = framed.shape[1] - 2
    columns = jnp.concatenate([framed[:, lag : lag + frames] for lag in range(3)], axis=4)
    matrix = weight_piece.reshape(3 * width, weight_piece.shape[2])
    return jnp.dot(columns.reshape(-1, 3 * width), matrix, preferred_element_type=jnp.float32)


def per_device(videos, spatial_filter, temporal_filter, spatial_bias, temporal_bias):
    samples, frames, height, breadth, channels = videos.shape
    count_frames = videos.shape[1]
    padded = jnp.pad(videos, ((0, 0), (0, 0), (1, 1), (1, 1), (0, 0)))
    summed = spatial_term(padded, lax.all_gather(spatial_filter, "dp", axis=1, tiled=True))
    activated = jax.nn.silu(summed + spatial_bias).astype(jnp.bfloat16)
    hidden = activated.reshape(samples, count_frames, height, breadth, channels)
    framed = padded_2(hidden, (("tile", 1),), 1)
    result = temporal_term(framed, lax.all_gather(temporal_filter, "dp", axis=1, tiled=True))
    return (result + temporal_bias).astype(jnp.bfloat16).reshape(videos.shape)


def solution(mesh):
    return jax.shard_map(
        per_device,
        mesh=mesh,
        in_specs=(
            P("dp", "tile", None, None, None),
            P(None, "dp", None),
            P(None, "dp", None),
            P(),
            P(),
        ),
        out_specs=P("dp", "tile", None, None, None),
        check_vma=False,
    )
```

profile of v0, /device:TPU:1, one launch (start us, length us, event | category | flops | bytes accessed | tf_op | source)
XLA Modules:
  0.0 152.8 jit_solution(8099898863406536119)
XLA Ops:
  6.5 0.0 copy-start
  6.5 0.0 all-gather.3.cloned.1.call-start
  6.5 0.7 all-gather.3.cloned.1.call-update
  7.3 0.0 all-gather.5.cloned.1.call-start
  7.3 3.5 %slice_dynamic-update-slice_fusion.7 = bf16[1,1,32,64,4608]{4,3,2,1,0:T(8,128)(2,1)} fusion(bf16[1,1,32,64,512]{4,3,2,1,0:T(8,128)(2,1)} %param.5), kind=kLoop, calls=%fused_computation.15 | loop fusion | bytes 4194304
  10.8 0.0 copy-done
  10.8 1.6 %slice_dynamic-update-slice_fusion.6 = bf16[1,1,32,64,4608]{4,3,2,1,0:T(8,128)(2,1)} fusion(bf16[1,1,32,64,4608]{4,3,2,1,0:T(8,128)(2,1)} %slice_dynamic-update-slice_fusion.7, bf16[1,1,32,64,512]{4,3,2,1,0:T(8,128)(2,1)S(1)} %copy-done), kind=kLoop, calls=%fused_computation.14 | loop fusion | bytes 4194304
  12.4 2.5 %slice_dynamic-update-slice_fusion.5 = bf16[1,1,32,64,4608]{4,3,2,1,0:T(8,128)(2,1)} fusion(bf16[1,1,32,64,4608]{4,3,2,1,0:T(8,128)(2,1)} %slice_dynamic-update-slice_fusion.6, bf16[1,1,32,64,512]{4,3,2,1,0:T(8,128)(2,1)S(1)} %copy-done), kind=kLoop, calls=%fused_computation.13 | loop fusion | bytes 4194304
  15.0 2.7 %slice_dynamic-update-slice_fusion.4 = bf16[1,1,32,64,4608]{4,3,2,1,0:T(8,128)(2,1)} fusion(bf16[1,1,32,64,4608]{4,3,2,1,0:T(8,128)(2,1)} %slice_dynamic-update-slice_fusion.5, bf16[1,1,32,64,512]{4,3,2,1,0:T(8,128)(2,1)S(1)} %copy-done), kind=kLoop, calls=%fused_computation.12 | loop fusion | bytes 4194304
  17.6 1.6 %constant_dynamic-update-slice_fusion = bf16[1,1,32,64,4608]{4,3,2,1,0:T(8,128)(2,1)} fusion(bf16[1,1,32,64,4608]{4,3,2,1,0:T(8,128)(2,1)} %slice_dynamic-update-slice_fusion.4, bf16[1,1,32,64,512]{4,3,2,1,0:T(8,128)(2,1)S(1)} %copy-done), kind=kLoop, calls=%fused_computation.16 | loop fusion | bytes 4194304
  19.2 2.5 %slice_dynamic-update-slice_fusion.3 = bf16[1,1,32,64,4608]{4,3,2,1,0:T(8,128)(2,1)} fusion(bf16[1,1,32,64,4608]{4,3,2,1,0:T(8,128)(2,1)} %constant_dynamic-update-slice_fusion, bf16[1,1,32,64,512]{4,3,2,1,0:T(8,128)(2,1)S(1)} %copy-done), kind=kLoop, calls=%fused_computation.11 | loop fusion | bytes 4194304
  21.8 2.7 %slice_dynamic-update-slice_fusion.2 = bf16[1,1,32,64,4608]{4,3,2,1,0:T(8,128)(2,1)} fusion(bf16[1,1,32,64,4608]{4,3,2,1,0:T(8,128)(2,1)} %slice_dynamic-update-slice_fusion.3, bf16[1,1,32,64,512]{4,3,2,1,0:T(8,128)(2,1)S(1)} %copy-done), kind=kLoop, calls=%fused_computation.10 | loop fusion | bytes 4194304
  24.4 0.0 copy-start.1
  24.4 1.6 %slice_dynamic-update-slice_fusion.1 = bf16[1,1,32,64,4608]{4,3,2,1,0:T(8,128)(2,1)} fusion(bf16[1,1,32,64,4608]{4,3,2,1,0:T(8,128)(2,1)} %slice_dynamic-update-slice_fusion.2, bf16[1,1,32,64,512]{4,3,2,1,0:T(8,128)(2,1)S(1)} %copy-done), kind=kLoop, calls=%fused_computation.9 | loop fusion | bytes 4194304
  26.1 2.6 %slice_dynamic-update-slice_fusion = bf16[1,1,32,64,4608]{4,3,2,1,0:T(8,128)(2,1)} fusion(bf16[1,1,32,64,4608]{4,3,2,1,0:T(8,128)(2,1)} %slice_dynamic-update-slice_fusion.1, bf16[1,1,32,64,512]{4,3,2,1,0:T(8,128)(2,1)S(1)} %copy-done), kind=kLoop, calls=%fused_computation.8 | loop fusion | bytes 4194304 | tf_op jit(solution)/shard_map/concatenate | solution.py:24
  28.6 45.0 %all-gather.3.cloned.1.call-done = bf16[9,512,512]{2,1,0:T(8,128)(2,1)} async-done(((bf16[9,256,512]{2,1,0:T(8,128)(2,1)}), bf16[9,512,512]{2,1,0:T(8,128)(2,1)}) %all-gather.3.cloned.1.call-update) | async-done | bytes 4718608 | tf_op jit(solution)/shard_map/all_gather | solution.py:48
  73.7 0.0 copy-done.1
  73.7 0.0 copy-start.2
  73.7 15.8 %multiply_convert_fusion = bf16[2048,512]{1,0:T(8,128)(2,1)S(1)} fusion(bf16[2048,4608]{1,0:T(8,128)(2,1)} %bitcast, bf16[4608,512]{1,0:T(8,128)(2,1)} %bitcast.10, f32[512]{0:T(512)S(1)} %copy-done.1), kind=kOutput, calls=%fused_computation.7 | convolution fusion | flops 9669967872 | bytes 25692160 | tf_op jit(solution)/shard_map/dot_general | solution.py:33
  89.5 3.7 %collective-permute-start = (bf16[1,1,32,64,512]{4,3,2,1,0:T(8,128)(2,1)S(1)}, bf16[1,1,32,64,512]{4,3,2,1,0:T(8,128)(2,1)}, u32[]{:S(2)}, u32[]{:S(2)}) collective-permute-start(bf16[1,1,32,64,512]{4,3,2,1,0:T(8,128)(2,1)S(1)} %bitcast.11), channel_id=1, source_target_pairs={{0,1},{1,2},{2,3},{3,4},{4,5},{5,6},{6,7},{7,8},{8,9},{9,10},{10,1... | collective-permute-start | bytes 6291464 | tf_op jit(solution)/shard_map/ppermute | solution.py:12
  93.1 2.2 %collective-permute-start.1 = (bf16[1,1,32,64,512]{4,3,2,1,0:T(8,128)(2,1)S(1)}, bf16[1,1,32,64,512]{4,3,2,1,0:T(8,128)(2,1)}, u32[]{:S(2)}, u32[]{:S(2)}) collective-permute-start(bf16[1,1,32,64,512]{4,3,2,1,0:T(8,128)(2,1)S(1)} %bitcast.12), channel_id=1, source_target_pairs={{1,0},{2,1},{3,2},{4,3},{5,4},{6,5},{7,6},{8,7},{9,8},{10,9},{11,1... | collective-permute-start | bytes 6291464 | tf_op jit(solution)/shard_map/ppermute | solution.py:15
  95.3 0.0 all-gather.5.cloned.1.call-update
  95.3 27.3 %all-gather.5.cloned.1.call-done = bf16[3,512,512]{2,1,0:T(8,128)(2,1)} async-done(((bf16[3,256,512]{2,1,0:T(8,128)(2,1)}), bf16[3,512,512]{2,1,0:T(8,128)(2,1)}) %all-gather.5.cloned.1.call-update) | async-done | bytes 1572880 | tf_op jit(solution)/shard_map/all_gather | solution.py:52
  122.6 15.9 %collective-permute-done = bf16[1,1,32,64,512]{4,3,2,1,0:T(8,128)(2,1)} collective-permute-done((bf16[1,1,32,64,512]{4,3,2,1,0:T(8,128)(2,1)S(1)}, bf16[1,1,32,64,512]{4,3,2,1,0:T(8,128)(2,1)}, u32[]{:S(2)}, u32[]{:S(2)}) %collective-permute-start) | collective-permute-done | bytes 2097184 | tf_op jit(solution)/shard_map/ppermute | solution.py:12
  138.6 0.0 collective-permute-done.1
  138.6 0.0 copy-done.2
  138.6 7.4 %add_convert_fusion = bf16[2048,512]{1,0:T(8,128)(2,1)} fusion(bf16[1536,512]{1,0:T(8,128)(2,1)} %bitcast.13, bf16[2048,512]{1,0:T(8,128)(2,1)} %bitcast.4, bf16[2048,512]{1,0:T(8,128)(2,1)S(1)} %multiply_convert_fusion, bf16[2048,512]{1,0:T(8,128)(2,1)} %bitcast.3, f32[512]{0:T(512)S(1)} %copy-done.2), kind=kOutput, calls=%fused_computation.6 | convolution fusion | flops 3242196992 | bytes 9963520 | tf_op jit(solution)/shard_map/dot_general | solution.py:41
Async XLA Ops:
  6.5 4.3 %copy-start = (bf16[1,1,32,64,512]{4,3,2,1,0:T(8,128)(2,1)S(1)}, bf16[1,1,32,64,512]{4,3,2,1,0:T(8,128)(2,1)}, u32[]{:S(2)}) copy-start(bf16[1,1,32,64,512]{4,3,2,1,0:T(8,128)(2,1)} %param.5) | copy-start | bytes 6291460
  6.5 67.1 %all-gather.3.cloned.1.call-start = ((), (), s32[]{:S(2)}) async-start(), calls=%async_computation | async-start | bytes 7077888 | tf_op jit(solution)/shard_map/all_gather | solution.py:48
  7.3 115.4 %all-gather.5.cloned.1.call-start = ((), (), s32[]{:S(2)}) async-start(), calls=%async_computation.1 | async-start | bytes 2359296 | tf_op jit(solution)/shard_map/all_gather | solution.py:52
  24.4 49.2 %copy-start.1 = (f32[512]{0:T(512)S(1)}, f32[512]{0:T(512)}, u32[]{:S(2)}) copy-start(f32[512]{0:T(512)} %param.8) | copy-start | bytes 6148
  73.7 64.9 %copy-start.2 = (f32[512]{0:T(512)S(1)}, f32[512]{0:T(512)}, u32[]{:S(2)}) copy-start(f32[512]{0:T(512)} %param.9) | copy-start | bytes 6148
  89.5 49.1 %collective-permute-start = (bf16[1,1,32,64,512]{4,3,2,1,0:T(8,128)(2,1)S(1)}, bf16[1,1,32,64,512]{4,3,2,1,0:T(8,128)(2,1)}, u32[]{:S(2)}, u32[]{:S(2)}) collective-permute-start(bf16[1,1,32,64,512]{4,3,2,1,0:T(8,128)(2,1)S(1)} %bitcast.11), channel_id=1, source_target_pairs={{0,1},{1,2},{2,3},{3,4},{4,5},{5,6},{6,7},{7,8},{8,9},{9,10},{10,1... | collective-permute-start | bytes 6291464 | tf_op jit(solution)/shard_map/ppermute | solution.py:12
  93.1 45.4 %collective-permute-start.1 = (bf16[1,1,32,64,512]{4,3,2,1,0:T(8,128)(2,1)S(1)}, bf16[1,1,32,64,512]{4,3,2,1,0:T(8,128)(2,1)}, u32[]{:S(2)}, u32[]{:S(2)}) collective-permute-start(bf16[1,1,32,64,512]{4,3,2,1,0:T(8,128)(2,1)S(1)} %bitcast.12), channel_id=1, source_target_pairs={{1,0},{2,1},{3,2},{4,3},{5,4},{6,5},{7,6},{8,7},{9,8},{10,9},{11,1... | collective-permute-start | bytes 6291464 | tf_op jit(solution)/shard_map/ppermute | solution.py:15
Sparse Core Ops, SparseCore 0:
  8.9 64.7 all-gather.2
  95.4 27.1 all-gather.4
where the time goes:
time: 154 us; the launch traced here: 153 us
  waiting for transfers between devices  89 us (58%)
  matrix products  23.2 us (15%)
  local copies, waits for them, and re-layouts  21.3 us (14%)
  between operations  13.4 us (9%)
  starting transfers between devices  5.86 us (4%)
    all_gather x1, waiting for transfers between devices, per_device(): lax.all_gather(spatial_filter, 'dp', axis=1, tiled=True)  45 us
    all_gather x1, waiting for transfers between devices, per_device(): lax.all_gather(temporal_filter, 'dp', axis=1, tiled=True)  27.3 us
    unnamed x14, local copies, waits for them, and re-layouts  18.7 us
    ppermute x1, waiting for transfers between devices, padded_2(): lax.ppermute(lax.slice_in_dim(block, block.shape[dim] - width, None, axis...  15.9 us
    dot_general x1, matrix products, spatial_term(): jnp.dot(columns.reshape(-1, 9 * width), matrix, preferred_element_type=jn...  15.8 us
    dot_general x1, matrix products, temporal_term(): jnp.dot(columns.reshape(-1, 3 * width), matrix, preferred_element_type=jn...  7.43 us
    ppermute x1, starting transfers between devices, padded_2(): lax.ppermute(lax.slice_in_dim(block, block.shape[dim] - width, None, axis...  3.66 us
  transfers between devices with their start and end apart: 4, of which 3 were waited for; matrix products, arithmetic and copies ran while one was open for 14% of the time, Pallas kernels for 0%

commit v1 on v0

--- a/solution.py
+++ b/solution.py
@@ -1,7 +1,322 @@
+import functools
+
 import jax
 import jax.numpy as jnp
 from jax import lax
+from jax.experimental import pallas as pl
+from jax.experimental.pallas import tpu as pltpu
 from jax.sharding import PartitionSpec as P
+
+TAPS = (1, 4, 7, 0, 3, 6, 2, 5, 8)
+VMEM = 60 * 2**20
+
+
+def dot(a, b):
+    return jnp.dot(a, b, preferred_element_type=jnp.float32)
+
+
+def silu(v):
+    return v / (1 + jnp.exp(-v))
+
+
+def rows_conv(padded, weights, first, rows, breadth, columns, ready=None):
+    count = rows * breadth
+    place = lax.rem(lax.broadcasted_iota(jnp.int32, (count, 1), 0), breadth)
+    depth = padded.shape[2]
+    lines = jnp.concatenate(
+        [padded[pl.ds(first + dy, rows)].reshape(count, depth) for dy in range(3)], axis=1
+    )
+
+    def side(dx):
+        if ready is not None:
+            ready(dx)
+        matrix = jnp.concatenate([weights[3 * dy + dx, :, columns] for dy in range(3)], axis=0)
+        return dot(lines, matrix)
+
+    total = side(1)
+    total += jnp.where(place == 0, 0.0, pltpu.roll(side(0), 1, 0))
+    total += jnp.where(place == breadth - 1, 0.0, pltpu.roll(side(2), count - 1, 0))
+    return total
+
+
+def halves(width):
+    cut = width // 2
+    return [slice(0, cut), slice(cut, width)]
+
+
+def conv_kernel(rows, pieces, has_base, activate, at_ref, *refs):
+    video = refs[0]
+    parts = refs[1 : 1 + pieces]
+    rest = refs[1 + pieces :]
+    base = rest[0] if has_base else None
+    bias, out, padded, weights, video_sem, part_sem = rest[1 if has_base else 0 :]
+    height, breadth = video.shape[0], video.shape[1]
+    depth = padded.shape[2]
+    steps = height // rows
+    i = pl.program_id(0)
+
+    def video_copy(j):
+        channels = pl.ds(pl.multiple_of(at_ref[0], 128), depth)
+        return pltpu.make_async_copy(
+            video.at[pl.ds(j * rows, rows), :, channels], padded.at[pl.ds(j * rows + 1, rows)], video_sem.at[j]
+        )
+
+    def part_copy(p, tap):
+        deep = parts[p].shape[1]
+        begin = 0 if pieces == 1 else pl.multiple_of(at_ref[1 + p], 64)
+        return pltpu.make_async_copy(
+            parts[p].at[tap], weights.at[tap, pl.ds(begin, deep)], part_sem.at[p, tap]
+        )
+
+    @pl.when(i == 0)
+    def _():
+        video_copy(0).start()
+        for tap in TAPS[:3]:
+            for p in range(pieces):
+                part_copy(p, tap).start()
+        if steps > 1:
+            video_copy(1).start()
+        for tap in TAPS[3:]:
+            for p in range(pieces):
+                part_copy(p, tap).start()
+        for j in range(2, steps):
+            video_copy(j).start()
+        padded[0] = jnp.zeros(padded.shape[1:], padded.dtype)
+        padded[height + 1] = jnp.zeros(padded.shape[1:], padded.dtype)
+        video_copy(0).wait()
+        for tap in TAPS:
+            for p in range(pieces):
+                part_copy(p, tap).wait()
+
+    @pl.when(i + 1 < steps)
+    def _():
+        video_copy(i + 1).wait()
+
+    for columns in halves(out.shape[2]):
+        total = rows_conv(padded, weights, i * rows, rows, breadth, columns)
+        if has_base:
+            total += base[:, :, columns].reshape(total.shape)
+        if activate:
+            total = silu(total + bias[:, columns])
+        out[:, :, columns] = total.astype(out.dtype).reshape(rows, breadth, -1)
+
+
+def conv_call(video, parts, at, base, bias, depth, rows, activate):
+    height, breadth, channels = video.shape
+    width = parts[0].shape[2]
+    steps = height // rows
+    has_base = base is not None
+    row_spec = pl.BlockSpec((rows, breadth, width), lambda i, at: (i, 0, 0))
+    any_spec = pl.BlockSpec(memory_space=pl.ANY)
+    operands = [video, *parts] + ([base] if has_base else []) + [bias]
+    return pl.pallas_call(
+        functools.partial(conv_kernel, rows, len(parts), has_base, activate),
+        grid_spec=pltpu.PrefetchScalarGridSpec(
+            num_scalar_prefetch=1,
+            grid=(steps,),
+            in_specs=[any_spec] * (1 + len(parts))
+            + ([row_spec] if has_base else [])
+            + [pl.BlockSpec((1, width), lambda i, at: (0, 0))],
+            out_specs=row_spec,
+            scratch_shapes=[
+                pltpu.VMEM((height + 2, breadth, depth), video.dtype),
+                pltpu.VMEM((9, depth, width), video.dtype),
+                pltpu.SemaphoreType.DMA((steps,)),
+                pltpu.SemaphoreType.DMA((len(parts), 9)),
+            ],
+        ),
+        out_shape=jax.ShapeDtypeStruct((height, breadth, width), jnp.bfloat16 if activate else jnp.float32),
+        cost_estimate=pl.CostEstimate(
+            flops=2 * height * breadth * 9 * depth * width, bytes_accessed=12 * 2**20, transcendentals=0
+        ),
+        compiler_params=pltpu.CompilerParams(vmem_limit_bytes=VMEM),
+    )(at, *operands)
+
+
+def far_kernel(rows, top, begin, pieces, at_ref, *refs):
+    blocks = refs[:top]
+    parts = refs[top : top + pieces]
+    bias, out, padded, weights, video_sem, part_sem = refs[top + pieces :]
+    breadth = out.shape[1]
+    steps = pl.num_programs(0)
+    i = pl.program_id(0)
+    need = padded.shape[0]
+
+    def video_copies():
+        copies, at = [], 0
+        low = begin - 1
+        for p, block in enumerate(blocks):
+            size = block.shape[0]
+            start, end = max(low, at), min(low + need, at + size)
+            if end > start:
+                copies.append(
+                    pltpu.make_async_copy(
+                        block.at[pl.ds(start - at, end - start)],
+                        padded.at[pl.ds(start - low, end - start)],
+                        video_sem.at[p],
+                    )
+                )
+            at += size
+        return copies
+
+    def part_copy(p, tap):
+        deep = parts[p].shape[1]
+        first = 0 if pieces == 1 else pl.multiple_of(at_ref[1 + p], 64)
+        return pltpu.make_async_copy(
+            parts[p].at[tap], weights.at[tap, pl.ds(first, deep)], part_sem.at[p, tap]
+        )
+
+    @pl.when(i == 0)
+    def _():
+        for copy in video_copies():
+            copy.start()
+        for tap in TAPS:
+            for p in range(pieces):
+                part_copy(p, tap).start()
+        if begin == 0:
+            padded[0] = jnp.zeros(padded.shape[1:], padded.dtype)
+        for copy in video_copies():
+            copy.wait()
+        for tap in TAPS:
+            for p in range(pieces):
+                part_copy(p, tap).wait()
+
+    for columns in halves(out.shape[2]):
+        total = rows_conv(padded, weights, i * rows, rows, breadth, columns)
+        total = silu(total + bias[:, columns])
+        out[:, :, columns] = total.astype(out.dtype).reshape(rows, breadth, -1)
+
+
+def far_call(blocks, parts, at, bias, begin, count, rows):
+    breadth, channels = blocks[0].shape[1:]
+    width = parts[0].shape[2]
+    any_spec = pl.BlockSpec(memory_space=pl.ANY)
+    return pl.pallas_call(
+        functools.partial(far_kernel, rows, len(blocks), begin, len(parts)),
+        grid_spec=pltpu.PrefetchScalarGridSpec(
+            num_scalar_prefetch=1,
+            grid=(count // rows,),
+            in_specs=[any_spec] * (len(blocks) + len(parts)) + [pl.BlockSpec((1, width), lambda i, at: (0, 0))],
+            out_specs=pl.BlockSpec((rows, breadth, width), lambda i, at: (i, 0, 0)),
+            scratch_shapes=[
+                pltpu.VMEM((count + 2, breadth, channels), blocks[0].dtype),
+                pltpu.VMEM((9, channels, width), blocks[0].dtype),
+                pltpu.SemaphoreType.DMA((len(blocks),)),
+                pltpu.SemaphoreType.DMA((len(parts), 9)),
+            ],
+        ),
+        out_shape=jax.ShapeDtypeStruct((count, breadth, width), jnp.bfloat16),
+        cost_estimate=pl.CostEstimate(
+            flops=2 * count * breadth * 9 * channels * width, bytes_accessed=8 * 2**20, transcendentals=0
+        ),
+        compiler_params=pltpu.CompilerParams(vmem_limit_bytes=VMEM),
+    )(at, *blocks, *parts, bias)
+
+
+def mix_kernel(pieces, aliased, at_ref, own, mate, far, *refs):
+    parts = refs[:pieces]
+    bias, out, weights, part_sem = refs[pieces + aliased :]
+    rows, breadth, width = out.shape
+    depth = weights.shape[1]
+    i = pl.program_id(0)
+
+    def part_copy(p):
+        deep = parts[p].shape[1]
+        first = 0 if pieces == 1 else pl.multiple_of(at_ref[3 + p], 64)
+        return pltpu.make_async_copy(parts[p], weights.at[:, pl.ds(first, deep)], part_sem.at[p])
+
+    @pl.when(i == 0)
+    def _():
+        for p in range(pieces):
+            part_copy(p).start()
+        for p in range(pieces):
+            part_copy(p).wait()
+
+    count = rows * breadth
+    lines = [ref[...].reshape(count, depth) for ref in (own, mate, far)]
+    lines[2] = jnp.where(at_ref[2] > 0, lines[2], jnp.zeros_like(lines[2]))
+    for columns in halves(width):
+        total = dot(lines[0], weights[1, :, columns])
+        total += dot(lines[1], weights[at_ref[0], :, columns])
+        total += dot(lines[2], weights[at_ref[1], :, columns])
+        total += bias[:, columns]
+        out[:, :, columns] = total.astype(out.dtype).reshape(rows, breadth, -1)
+
+
+def mix_call(own, mate, far, parts, at, bias, before, begin, rows):
+    height, breadth, depth = own.shape
+    width = parts[0].shape[2]
+    count = far.shape[0]
+    any_spec = pl.BlockSpec(memory_space=pl.ANY)
+    there = pl.BlockSpec((rows, breadth, depth), lambda i, at: (i + begin // rows, 0, 0))
+    aliased = 0 if before is None else 1
+    return pl.pallas_call(
+        functools.partial(mix_kernel, len(parts), aliased),
+        grid_spec=pltpu.PrefetchScalarGridSpec(
+            num_scalar_prefetch=1,
+            grid=(count // rows,),
+            in_specs=[there, there, pl.BlockSpec((rows, breadth, depth), lambda i, at: (i, 0, 0))]
+            + [any_spec] * (len(parts) + aliased)
+            + [pl.BlockSpec((1, width), lambda i, at: (0, 0))],
+            out_specs=pl.BlockSpec((rows, breadth, width), lambda i, at: (i + begin // rows, 0, 0)),
+            scratch_shapes=[
+                pltpu.VMEM((3, depth, width), own.dtype),
+                pltpu.SemaphoreType.DMA((len(parts),)),
+            ],
+        ),
+        out_shape=jax.ShapeDtypeStruct((height, breadth, width), jnp.bfloat16),
+        input_output_aliases={4 + len(parts): 0} if aliased else {},
+        cost_estimate=pl.CostEstimate(
+            flops=2 * count * breadth * 3 * depth * width, bytes_accessed=6 * 2**20, transcendentals=0
+        ),
+        compiler_params=pltpu.CompilerParams(vmem_limit_bytes=VMEM),
+    )(at, own, mate, far, *parts, *([before] if aliased else []), bias)
+
+
+def near_device(videos, spatial_filter, temporal_filter, spatial_bias, temporal_bias):
+    height, breadth, channels = videos.shape[2:]
+    video = videos.reshape(height, breadth, channels)
+    spatial_bias = spatial_bias.reshape(1, -1)
+    temporal_bias = temporal_bias.reshape(1, -1)
+    tiles = lax.axis_size("tile")
+    group, tile = lax.axis_index("dp"), lax.axis_index("tile")
+    core = lax.rem(tile, 2)
+    depth = spatial_filter.shape[1]
+    part = depth // 2
+    swap = [(0, 1), (1, 0)]
+    mates = [(i, i ^ 1) for i in range(tiles)]
+    across = [pair for i in range(1, tiles - 1, 2) for pair in ((i, i + 1), (i + 1, i))]
+
+    first, second = height // 2, 3 * height // 4
+    far_a = lax.ppermute(video[: first + 1], "tile", across)
+    mine = lax.dynamic_slice_in_dim(spatial_filter, core * part, part, axis=1)
+    spatial_y = lax.ppermute(mine, "dp", swap)
+    mine = lax.dynamic_slice_in_dim(temporal_filter, core * part, part, axis=1)
+    temporal_y = lax.ppermute(mine, "dp", swap)
+    far_b = lax.ppermute(video[first + 1 : second + 1], "tile", across)
+    spatial_m = lax.ppermute(spatial_y, "tile", mates)
+    temporal_m = lax.ppermute(temporal_y, "tile", mates)
+
+    here, there = group * depth, (1 - group) * depth
+    local = conv_call(
+        video, [spatial_filter], jnp.stack([here]), None, spatial_bias, depth, 8, False
+    )
+    at = jnp.stack([there, core * part, (1 - core) * part])
+    hidden = conv_call(video, [spatial_y, spatial_m], at, local, spatial_bias, depth, 8, True)
+    mate = lax.ppermute(hidden, "tile", mates)
+    far_c = lax.ppermute(hidden[second:], "tile", across)
+    places = [here, there + core * part, there + (1 - core) * part]
+    at = jnp.stack([here, *places])
+    parts = [spatial_filter, spatial_y, spatial_m]
+    hidden_a = far_call([far_a], parts, at, spatial_bias, 0, first, 8)
+    hidden_b = far_call([far_a, far_b], parts, at, spatial_bias, first, second - first, 8)
+    present = jnp.where(core == 0, tile > 0, tile < tiles - 1).astype(jnp.int32)
+    at = jnp.stack([2 - 2 * core, 2 * core, present, *places])
+    parts = [temporal_filter, temporal_y, temporal_m]
+    out = mix_call(hidden, mate, hidden_a, parts, at, temporal_bias, None, 0, 8)
+    out = mix_call(hidden, mate, hidden_b, parts, at, temporal_bias, out, first, 8)
+    out = mix_call(hidden, mate, far_c, parts, at, temporal_bias, out, second, 8)
+    return out.reshape(videos.shape)
 
 
 def padded_2(block, sides, width):
@@ -41,16 +356,26 @@
     return jnp.dot(columns.reshape(-1, 3 * width), matrix, preferred_element_type=jnp.float32)
 
 
-def per_device(videos, spatial_filter, temporal_filter, spatial_bias, temporal_bias):
+def any_device(videos, spatial_filter, temporal_filter, spatial_bias, temporal_bias):
     samples, frames, height, breadth, channels = videos.shape
-    count_frames = videos.shape[1]
     padded = jnp.pad(videos, ((0, 0), (0, 0), (1, 1), (1, 1), (0, 0)))
     summed = spatial_term(padded, lax.all_gather(spatial_filter, "dp", axis=1, tiled=True))
     activated = jax.nn.silu(summed + spatial_bias).astype(jnp.bfloat16)
-    hidden = activated.reshape(samples, count_frames, height, breadth, channels)
+    hidden = activated.reshape(samples, frames, height, breadth, channels)
     framed = padded_2(hidden, (("tile", 1),), 1)
     result = temporal_term(framed, lax.all_gather(temporal_filter, "dp", axis=1, tiled=True))
     return (result + temporal_bias).astype(jnp.bfloat16).reshape(videos.shape)
+
+
+def per_device(videos, *rest):
+    near = (
+        videos.shape[0] == 1
+        and videos.shape[1] == 1
+        and videos.shape[2] % 32 == 0
+        and lax.axis_size("dp") == 2
+        and lax.axis_size("tile") % 2 == 0
+    )
+    return (near_device if near else any_device)(videos, *rest)
 
 
 def solution(mesh):

time: 154 us -> 133 us (0.86)
  Pallas kernels: 0 us -> 55.4 us
  waiting for transfers between devices: 89 us -> 49.1 us
  matrix products: 23.2 us -> 0 us
  between operations: 13.4 us -> 0.23 us
  local copies, waits for them, and re-layouts: 21.3 us -> 10.7 us
  starting transfers between devices: 5.86 us -> 15.2 us
    all_gather x2 -> x0, waiting for transfers between devices: 72.3 us -> none  [the longest x1 45 us: per_device(): lax.all_gather(spatial_filter, 'dp', axis=1, tiled=True)]
    pallas_call x0 -> x7, Pallas kernels: none -> 55.4 us  [the longest x2 20.4 us: conv_call(): pl.pallas_call(functools.partial(conv_kernel, rows, len(parts), has_base,...]
    ppermute x2 -> x8, waiting for transfers between devices: 15.9 us -> 49.1 us  [the longest x1 25.7 us: near_device(): spatial_y = lax.ppermute(mine, 'dp', swap)]
    dot_general x2 -> x0, matrix products: 23.2 us -> none  [the longest x1 15.8 us: spatial_term(): jnp.dot(columns.reshape(-1, 9 * width), matrix, preferred_element_type=jn...]
    unnamed x14, local copies, waits for them, and re-layouts: 18.7 us -> 3.25 us
    ppermute x2 -> x8, starting transfers between devices: 5.82 us -> 15.2 us  [the longest x1 4.32 us: near_device(): far_c = lax.ppermute(hidden[second:], 'tile', across)]
    slice x0 -> x3, local copies, waits for them, and re-layouts: none -> 5.5 us  [the longest x1 2.41 us: near_device(): far_a = lax.ppermute(video[:first + 1], 'tile', across)]
    concatenate x1 -> x0, local copies, waits for them, and re-layouts: 2.58 us -> none  [spatial_term(): jnp.concatenate([padded[:, :, row_off:row_off + height, col_off:col_off +...]
  transfers between devices with their start and end apart: 4 -> 8, of which waited for: 3 -> 3; matrix products, arithmetic and copies ran while one was open for 14% -> 6% of each run, Pallas kernels for 0% -> 30%
where the time goes in v1:
time: 133 us; the launch traced here: 132 us
  Pallas kernels  55.4 us (42%)
  waiting for transfers between devices  49.1 us (37%)
  starting transfers between devices  15.2 us (11%)
  local copies, waits for them, and re-layouts  10.7 us (8%)
    ppermute x1, waiting for transfers between devices, near_device(): spatial_y = lax.ppermute(mine, 'dp', swap)  25.7 us
    pallas_call x2, Pallas kernels, conv_call(): pl.pallas_call(functools.partial(conv_kernel, rows, len(parts), has_base,...  20.4 us
    ppermute x1, waiting for transfers between devices, near_device(): far_a = lax.ppermute(video[:first + 1], 'tile', across)  19.7 us
    pallas_call x2, Pallas kernels, far_call(): pl.pallas_call(functools.partial(far_kernel, rows, len(blocks), begin, le...  18.2 us
    pallas_call x3, Pallas kernels, mix_call(): pl.pallas_call(functools.partial(mix_kernel, len(parts), aliased), grid_s...  16.7 us
    ppermute x1, starting transfers between devices, near_device(): far_c = lax.ppermute(hidden[second:], 'tile', across)  4.32 us
    ppermute x1, waiting for transfers between devices, near_device(): temporal_y = lax.ppermute(mine, 'dp', swap)  3.66 us
    ppermute x1, starting transfers between devices, near_device(): far_a = lax.ppermute(video[:first + 1], 'tile', across)  3.56 us
  transfers between devices with their start and end apart: 8, of which 3 were waited for; matrix products, arithmetic and copies ran while one was open for 6% of the time, Pallas kernels for 30%

profile of v1, /device:TPU:1, one launch (start us, length us, event | category | flops | bytes accessed | tf_op | source)
XLA Modules:
  0.0 131.9 jit_solution(13413726998588076455)
XLA Ops:
  0.0 1.3 %constant_dynamic-slice_fusion.1 = bf16[9,128,512]{2,1,0:T(8,128)(2,1)S(1)} fusion(bf16[9,256,512]{2,1,0:T(8,128)(2,1)} %refs_1_.3, s32[]{:T(128)S(6)} %select_n.9), kind=kLoop, calls=%fused_computation.5 | loop fusion | bytes 2359300 | tf_op jit(solution)/shard_map/dynamic_slice | solution.py:292
  1.4 2.1 %collective-permute-start = (bf16[9,128,512]{2,1,0:T(8,128)(2,1)S(1)}, bf16[9,128,512]{2,1,0:T(8,128)(2,1)S(1)}, u32[]{:S(2)}, u32[]{:S(2)}) collective-permute-start(bf16[9,128,512]{2,1,0:T(8,128)(2,1)S(1)} %constant_dynamic-slice_fusion.1), channel_id=1, source_target_pairs={{0,16},{16,0},{1,17},{17,1},{2,18},{18,2},{3,19},{19,3},{4,20},{20... | collective-permute-start | bytes 3538952 | tf_op jit(solution)/shard_map/ppermute | solution.py:293
  3.5 25.7 %collective-permute-done.refs_1_.refs_3_.refs_2_ = bf16[9,128,512]{2,1,0:T(8,128)(2,1)S(1)} collective-permute-done((bf16[9,128,512]{2,1,0:T(8,128)(2,1)S(1)}, bf16[9,128,512]{2,1,0:T(8,128)(2,1)S(1)}, u32[]{:S(2)}, u32[]{:S(2)}) %collective-permute-start) | collective-permute-done | bytes 1179680 | tf_op jit(solution)/shard_map/ppermute | solution.py:293
  29.2 0.0 copy-start.5
  29.2 1.2 collective-permute-start.1
  30.4 0.7 pad_add_fusion.at_ref
  31.1 9.3 %shard_map.55.refs_3_ = f32[32,64,512]{2,1,0:T(8,128)} custom-call(s32[1]{0:T(128)} %bitcast.3.at_ref, bf16[32,64,512]{2,1,0:T(8,128)(2,1)} %bitcast.17, bf16[9,256,512]{2,1,0:T(8,128)(2,1)} %refs_1_.3, f32[1,512]{1,0:T(1,128)} %bitcast.22), custom_call_target="tpu_custom_call" | custom-call | flops 4831838208 | bytes 12582912 | tf_op jit(solution)/shard_map/pallas_call | solution.py:112
  40.4 0.0 copy-done.5
  40.4 0.0 collective-permute-done.1.refs_2_.refs_4_.refs_3_
  40.4 0.0 copy-start.6
  40.4 1.0 copy-done.6
  41.4 11.1 %shard_map.56.own = bf16[32,64,512]{2,1,0:T(8,128)(2,1)} custom-call(s32[3]{0:T(128)} %pad_add_fusion.at_ref, bf16[32,64,512]{2,1,0:T(8,128)(2,1)} %bitcast.18, bf16[9,128,512]{2,1,0:T(8,128)(2,1)} %copy-done.5, bf16[9,128,512]{2,1,0:T(8,128)(2,1)} %copy-done.6, f32[32,64,512]{2,1,0:T(8,128)} %shard_map.55.refs_3_, f32[1,512]{1,0:T(1,128)} %bitcast.23), custom_call_target="tpu_custom_call" | custom-call | flops 4831838208 | bytes 12582912 | tf_op jit(solution)/shard_map/pallas_call | solution.py:112
  52.5 0.0 copy-start.1
  52.5 0.2 collective-permute-start.2
  52.7 2.4 %slice_bitcast_fusion = bf16[17,64,512]{2,1,0:T(8,128)(2,1)} fusion(bf16[1,1,32,64,512]{4,3,2,1,0:T(8,128)(2,1)} %param.5), kind=kLoop, calls=%fused_computation | loop fusion | bytes 2228224 | tf_op jit(solution)/shard_map/slice | solution.py:291
  55.1 3.6 %collective-permute-start.6 = (bf16[17,64,512]{2,1,0:T(8,128)(2,1)}, bf16[17,64,512]{2,1,0:T(8,128)(2,1)}, u32[]{:S(2)}, u32[]{:S(2)}) collective-permute-start(bf16[17,64,512]{2,1,0:T(8,128)(2,1)} %slice_bitcast_fusion), channel_id=1, source_target_pairs={{1,2},{2,1},{3,4},{4,3},{5,6},{6,5},{7,8},{8,7},{9,10},{10,9},{11,... | collective-permute-start | bytes 3342344 | tf_op jit(solution)/shard_map/ppermute | solution.py:291
  58.7 0.0 copy-done.1
  58.7 1.3 collective-permute-start.4
  60.0 1.1 slice_bitcast_fusion.1
  61.1 2.5 %collective-permute-start.7 = (bf16[8,64,512]{2,1,0:T(8,128)(2,1)S(1)}, bf16[8,64,512]{2,1,0:T(8,128)(2,1)}, u32[]{:S(2)}, u32[]{:S(2)}) collective-permute-start(bf16[8,64,512]{2,1,0:T(8,128)(2,1)S(1)} %slice_bitcast_fusion.1), channel_id=1, source_target_pairs={{1,2},{2,1},{3,4},{4,3},{5,6},{6,5},{7,8},{8,7},{9,10},{10,9},{11,... | collective-permute-start | bytes 1572872 | tf_op jit(solution)/shard_map/ppermute | solution.py:296
  63.6 0.6 stack.51.at_ref
  64.2 0.6 pad_add_fusion.1.at_ref
  64.8 3.7 %collective-permute-done.4.refs_1_ = bf16[3,128,512]{2,1,0:T(8,128)(2,1)S(1)} collective-permute-done((bf16[3,128,512]{2,1,0:T(8,128)(2,1)S(1)}, bf16[3,128,512]{2,1,0:T(8,128)(2,1)S(1)}, u32[]{:S(2)}, u32[]{:S(2)}) %collective-permute-start.4) | collective-permute-done | bytes 393248 | tf_op jit(solution)/shard_map/ppermute | solution.py:295
  68.5 0.0 copy-start.2
  68.5 0.0 collective-permute-start.5
  68.5 2.0 %slice.20 = bf16[8,64,512]{2,1,0:T(8,128)(2,1)} slice(bf16[32,64,512]{2,1,0:T(8,128)(2,1)} %shard_map.56.own), slice={[24:32], [0:64], [0:512]} | slice | bytes 1048576 | tf_op jit(solution)/shard_map/slice | solution.py:307
  70.5 4.3 %collective-permute-start.3 = (bf16[8,64,512]{2,1,0:T(8,128)(2,1)}, bf16[8,64,512]{2,1,0:T(8,128)(2,1)S(1)}, u32[]{:S(2)}, u32[]{:S(2)}) collective-permute-start(bf16[8,64,512]{2,1,0:T(8,128)(2,1)} %slice.20), channel_id=1, source_target_pairs={{1,2},{2,1},{3,4},{4,3},{5,6},{6,5},{7,8},{8,7},{9,10},{10,9},{11,... | collective-permute-start | bytes 1572872 | tf_op jit(solution)/shard_map/ppermute | solution.py:307
  74.9 19.7 %collective-permute-done.6.refs_0_ = bf16[17,64,512]{2,1,0:T(8,128)(2,1)} collective-permute-done((bf16[17,64,512]{2,1,0:T(8,128)(2,1)}, bf16[17,64,512]{2,1,0:T(8,128)(2,1)}, u32[]{:S(2)}, u32[]{:S(2)}) %collective-permute-start.6) | collective-permute-done | bytes 1114144 | tf_op jit(solution)/shard_map/ppermute | solution.py:291
  94.6 10.6 %shard_map.58.far = bf16[16,64,512]{2,1,0:T(8,128)(2,1)} custom-call(s32[4]{0:T(128)} %pad_add_fusion.1.at_ref, bf16[17,64,512]{2,1,0:T(8,128)(2,1)} %collective-permute-done.6.refs_0_, bf16[9,256,512]{2,1,0:T(8,128)(2,1)} %refs_1_.3, bf16[9,128,512]{2,1,0:T(8,128)(2,1)} %copy-done.5, bf16[9,128,512]{2,1,0:T(8,128)(2,1)} %copy-done.6, f32[1,512]{1,0:T(1,128)} %bitcast.24), custom_call_target="tpu_custom_call" | custom-call | flops 4831838208 | bytes 8388608 | tf_op jit(solution)/shard_map/pallas_call | solution.py:194
  105.2 0.0 copy-done.2
  105.2 0.0 collective-permute-done.7.refs_1_
  105.2 7.7 %shard_map.57.far = bf16[8,64,512]{2,1,0:T(8,128)(2,1)} custom-call(s32[4]{0:T(128)} %pad_add_fusion.1.at_ref, bf16[17,64,512]{2,1,0:T(8,128)(2,1)} %collective-permute-done.6.refs_0_, bf16[8,64,512]{2,1,0:T(8,128)(2,1)} %collective-permute-done.7.refs_1_, bf16[9,256,512]{2,1,0:T(8,128)(2,1)} %refs_1_.3, bf16[9,128,512]{2,1,0:T(8,128)(2,1)} %copy-done.5, ...), custom_call_target="tpu_custom_call" | custom-call | flops 2415919104 | bytes 8388608 | tf_op jit(solution)/shard_map/pallas_call | solution.py:194
  112.9 0.0 collective-permute-done.5.refs_2_
  112.9 0.0 copy-start.3
  112.9 0.0 collective-permute-done.2.mate
  112.9 0.0 copy-start
  112.9 0.7 copy-done.3
  113.6 0.7 copy-done
  114.3 6.4 %shard_map.59.refs_3_ = bf16[32,64,512]{2,1,0:T(8,128)(2,1)} custom-call(s32[6]{0:T(128)} %stack.51.at_ref, bf16[32,64,512]{2,1,0:T(8,128)(2,1)} %shard_map.56.own, bf16[32,64,512]{2,1,0:T(8,128)(2,1)} %copy-done, bf16[16,64,512]{2,1,0:T(8,128)(2,1)} %shard_map.58.far, bf16[3,256,512]{2,1,0:T(8,128)(2,1)} %refs_0_.5, bf16[3,128,512]{2,1,0:T(8,128)(2,1)} %copy-done.2, ...), custom_call_target="tpu_custom_call" | custom-call | flops 1610612736 | bytes 6291456 | tf_op jit(solution)/shard_map/pallas_call | solution.py:253
  120.7 5.2 %shard_map.60.refs_3_ = bf16[32,64,512]{2,1,0:T(8,128)(2,1)} custom-call(s32[6]{0:T(128)} %stack.51.at_ref, bf16[32,64,512]{2,1,0:T(8,128)(2,1)} %shard_map.56.own, bf16[32,64,512]{2,1,0:T(8,128)(2,1)} %copy-done, bf16[8,64,512]{2,1,0:T(8,128)(2,1)} %shard_map.57.far, bf16[3,256,512]{2,1,0:T(8,128)(2,1)} %refs_0_.5, ...), custom_call_target="tpu_custom_call", output_to_operand_aliasing={{}: (7, {})} | custom-call | flops 805306368 | bytes 6291456 | tf_op jit(solution)/shard_map/pallas_call | solution.py:253
  125.9 0.0 collective-permute-done.3.far
  125.9 0.0 copy-start.4
  125.9 0.8 copy-done.4
  126.7 5.2 %shard_map.61 = bf16[32,64,512]{2,1,0:T(8,128)(2,1)} custom-call(s32[6]{0:T(128)} %stack.51.at_ref, bf16[32,64,512]{2,1,0:T(8,128)(2,1)} %shard_map.56.own, bf16[32,64,512]{2,1,0:T(8,128)(2,1)} %copy-done, bf16[8,64,512]{2,1,0:T(8,128)(2,1)} %copy-done.4, bf16[3,256,512]{2,1,0:T(8,128)(2,1)} %refs_0_.5, ...), custom_call_target="tpu_custom_call", output_to_operand_aliasing={{}: (7, {})} | custom-call | flops 805306368 | bytes 6291456 | tf_op jit(solution)/shard_map/pallas_call | solution.py:253
  (1 shorter events, 0.0 us)
Async XLA Ops:
  1.4 27.8 %collective-permute-start = (bf16[9,128,512]{2,1,0:T(8,128)(2,1)S(1)}, bf16[9,128,512]{2,1,0:T(8,128)(2,1)S(1)}, u32[]{:S(2)}, u32[]{:S(2)}) collective-permute-start(bf16[9,128,512]{2,1,0:T(8,128)(2,1)S(1)} %constant_dynamic-slice_fusion.1), channel_id=1, source_target_pairs={{0,16},{16,0},{1,17},{17,1},{2,18},{18,2},{3,19},{19,3},{4,20},{20... | collective-permute-start | bytes 3538952 | tf_op jit(solution)/shard_map/ppermute | solution.py:293
  29.2 11.2 %copy-start.5 = (bf16[9,128,512]{2,1,0:T(8,128)(2,1)}, bf16[9,128,512]{2,1,0:T(8,128)(2,1)S(1)}, u32[]{:S(2)}) copy-start(bf16[9,128,512]{2,1,0:T(8,128)(2,1)S(1)} %collective-permute-done.refs_1_.refs_3_.refs_2_) | copy-start | bytes 3538948
  29.2 11.2 %collective-permute-start.1 = (bf16[9,128,512]{2,1,0:T(8,128)(2,1)S(1)}, bf16[9,128,512]{2,1,0:T(8,128)(2,1)S(1)}, u32[]{:S(2)}, u32[]{:S(2)}) collective-permute-start(bf16[9,128,512]{2,1,0:T(8,128)(2,1)S(1)} %collective-permute-done.refs_1_.refs_3_.refs_2_), channel_id=1, source_target_pairs={{0,1},{1,0},{2,3},{3,2},{4,5},{5,4},{6,7},{7,6},{8,9},{9,8},{10,11... | collective-permute-start | bytes 3538952 | tf_op jit(solution)/shard_map/ppermute | solution.py:297
  40.4 1.0 copy-start.6
  52.5 6.2 %copy-start.1 = (bf16[3,256,512]{2,1,0:T(8,128)(2,1)S(1)}, bf16[3,256,512]{2,1,0:T(8,128)(2,1)}, u32[]{:S(2)}) copy-start(bf16[3,256,512]{2,1,0:T(8,128)(2,1)} %refs_0_.5) | copy-start | bytes 2359300
  52.5 60.4 %collective-permute-start.2 = (bf16[32,64,512]{2,1,0:T(8,128)(2,1)}, bf16[32,64,512]{2,1,0:T(8,128)(2,1)S(1)}, u32[]{:S(2)}, u32[]{:S(2)}) collective-permute-start(bf16[32,64,512]{2,1,0:T(8,128)(2,1)} %shard_map.56.own), channel_id=1, source_target_pairs={{0,1},{1,0},{2,3},{3,2},{4,5},{5,4},{6,7},{7,6},{8,9},{9,8},{10,11... | collective-permute-start | bytes 6291464 | tf_op jit(solution)/shard_map/ppermute | solution.py:306
  55.1 39.5 %collective-permute-start.6 = (bf16[17,64,512]{2,1,0:T(8,128)(2,1)}, bf16[17,64,512]{2,1,0:T(8,128)(2,1)}, u32[]{:S(2)}, u32[]{:S(2)}) collective-permute-start(bf16[17,64,512]{2,1,0:T(8,128)(2,1)} %slice_bitcast_fusion), channel_id=1, source_target_pairs={{1,2},{2,1},{3,4},{4,3},{5,6},{6,5},{7,8},{8,7},{9,10},{10,9},{11,... | collective-permute-start | bytes 3342344 | tf_op jit(solution)/shard_map/ppermute | solution.py:291
  58.7 9.8 %collective-permute-start.4 = (bf16[3,128,512]{2,1,0:T(8,128)(2,1)S(1)}, bf16[3,128,512]{2,1,0:T(8,128)(2,1)S(1)}, u32[]{:S(2)}, u32[]{:S(2)}) collective-permute-start(bf16[3,128,512]{2,1,0:T(8,128)(2,1)S(1)} %constant_dynamic-slice_fusion), channel_id=1, source_target_pairs={{0,16},{16,0},{1,17},{17,1},{2,18},{18,2},{3,19},{19,3},{4,20},{20... | collective-permute-start | bytes 1179656 | tf_op jit(solution)/shard_map/ppermute | solution.py:295
  61.1 44.1 %collective-permute-start.7 = (bf16[8,64,512]{2,1,0:T(8,128)(2,1)S(1)}, bf16[8,64,512]{2,1,0:T(8,128)(2,1)}, u32[]{:S(2)}, u32[]{:S(2)}) collective-permute-start(bf16[8,64,512]{2,1,0:T(8,128)(2,1)S(1)} %slice_bitcast_fusion.1), channel_id=1, source_target_pairs={{1,2},{2,1},{3,4},{4,3},{5,6},{6,5},{7,8},{8,7},{9,10},{10,9},{11,... | collective-permute-start | bytes 1572872 | tf_op jit(solution)/shard_map/ppermute | solution.py:296
  68.5 36.7 %copy-start.2 = (bf16[3,128,512]{2,1,0:T(8,128)(2,1)}, bf16[3,128,512]{2,1,0:T(8,128)(2,1)S(1)}, u32[]{:S(2)}) copy-start(bf16[3,128,512]{2,1,0:T(8,128)(2,1)S(1)} %collective-permute-done.4.refs_1_) | copy-start | bytes 1179652
  68.5 44.4 %collective-permute-start.5 = (bf16[3,128,512]{2,1,0:T(8,128)(2,1)S(1)}, bf16[3,128,512]{2,1,0:T(8,128)(2,1)S(1)}, u32[]{:S(2)}, u32[]{:S(2)}) collective-permute-start(bf16[3,128,512]{2,1,0:T(8,128)(2,1)S(1)} %collective-permute-done.4.refs_1_), channel_id=1, source_target_pairs={{0,1},{1,0},{2,3},{3,2},{4,5},{5,4},{6,7},{7,6},{8,9},{9,8},{10,11... | collective-permute-start | bytes 1179656 | tf_op jit(solution)/shard_map/ppermute | solution.py:298
  70.5 55.4 %collective-permute-start.3 = (bf16[8,64,512]{2,1,0:T(8,128)(2,1)}, bf16[8,64,512]{2,1,0:T(8,128)(2,1)S(1)}, u32[]{:S(2)}, u32[]{:S(2)}) collective-permute-start(bf16[8,64,512]{2,1,0:T(8,128)(2,1)} %slice.20), channel_id=1, source_target_pairs={{1,2},{2,1},{3,4},{4,3},{5,6},{6,5},{7,8},{8,7},{9,10},{10,9},{11,... | collective-permute-start | bytes 1572872 | tf_op jit(solution)/shard_map/ppermute | solution.py:307
  112.9 0.8 copy-start.3
  112.9 1.4 %copy-start = (bf16[32,64,512]{2,1,0:T(8,128)(2,1)}, bf16[32,64,512]{2,1,0:T(8,128)(2,1)S(1)}, u32[]{:S(2)}) copy-start(bf16[32,64,512]{2,1,0:T(8,128)(2,1)S(1)} %collective-permute-done.2.mate) | copy-start | bytes 6291460
  125.9 0.8 copy-start.4

commit v2 on v0

--- a/solution.py
+++ b/solution.py
@@ -1,7 +1,387 @@
+import functools
+
 import jax
 import jax.numpy as jnp
 from jax import lax
+from jax.experimental import pallas as pl
+from jax.experimental.pallas import tpu as pltpu
 from jax.sharding import PartitionSpec as P
+
+ANY = pl.BlockSpec(memory_space=pltpu.HBM)
+
+
+def dot(a, b):
+    return jnp.dot(a, b, preferred_element_type=jnp.float32)
+
+
+def silu(v):
+    return v / (1 + jnp.exp(-v))
+
+
+def halves(width):
+    cut = width // 2
+    return [slice(0, cut), slice(cut, width)]
+
+
+def seat():
+    tile = lax.axis_index("tile")
+    return lax.axis_index("dp"), lax.rem(tile // 4, 2), lax.rem(tile, 2)
+
+
+def piece_rows(depth):
+    return 3 * depth // 16, depth // 8
+
+
+def piece_starts(depth):
+    _, pair, core = seat()
+    small, large = piece_rows(depth)
+    near = [(pair, core), (1 - pair, core), (pair, 1 - core), (1 - pair, 1 - core)]
+    return [(2 * p + c) * small for p, c in near] + [4 * small + c * large for c in (core, 1 - core)]
+
+
+def aligned(start):
+    return pl.multiple_of(start, 16)
+
+
+def rows_conv(padded, weights, first, rows, breadth, columns):
+    count = rows * breadth
+    place = lax.rem(lax.broadcasted_iota(jnp.int32, (count, 1), 0), breadth)
+    depth = padded.shape[2]
+    lines = jnp.concatenate(
+        [padded[pl.ds(first + dy, rows)].reshape(count, depth) for dy in range(3)], axis=1
+    )
+
+    def side(dx):
+        matrix = jnp.concatenate([weights[3 * dy + dx, :, columns] for dy in range(3)], axis=0)
+        return dot(lines, matrix)
+
+    total = side(1)
+    total += jnp.where(place == 0, 0.0, pltpu.roll(side(0), 1, 0))
+    total += jnp.where(place == breadth - 1, 0.0, pltpu.roll(side(2), count - 1, 0))
+    return total
+
+
+def base_kernel(rows, video, part, out, padded, weights, video_sem, part_sem):
+    height, breadth = video.shape[:2]
+    depth = part.shape[1]
+    steps = height // rows
+    i = pl.program_id(0)
+    group = lax.axis_index("dp")
+
+    def video_copy(j):
+        channels = pl.ds(pl.multiple_of(group * depth, 128), depth)
+        return pltpu.make_async_copy(
+            video.at[pl.ds(j * rows, rows), :, channels],
+            padded.at[pl.ds(j * rows + 1, rows)],
+            video_sem.at[j],
+        )
+
+    part_copy = pltpu.make_async_copy(part, weights, part_sem)
+
+    @pl.when(i == 0)
+    def _():
+        video_copy(0).start()
+        part_copy.start()
+        for j in range(1, steps):
+            video_copy(j).start()
+        padded[0] = jnp.zeros(padded.shape[1:], padded.dtype)
+        padded[height + 1] = jnp.zeros(padded.shape[1:], padded.dtype)
+        video_copy(0).wait()
+        part_copy.wait()
+
+    @pl.when(i + 1 < steps)
+    def _():
+        video_copy(i + 1).wait()
+
+    for columns in halves(out.shape[2]):
+        total = rows_conv(padded, weights, i * rows, rows, breadth, columns)
+        out[:, :, columns] = total.reshape(rows, breadth, -1)
+
+
+def base_call(video, part, rows, cost):
+    height, breadth, _ = video.shape
+    depth, width = part.shape[1:]
+    steps = height // rows
+    return pl.pallas_call(
+        functools.partial(base_kernel, rows),
+        grid=(steps,),
+        in_specs=[ANY, ANY],
+        out_specs=pl.BlockSpec((rows, breadth, width), lambda i: (i, 0, 0)),
+        scratch_shapes=[
+            pltpu.VMEM((height + 2, breadth, depth), video.dtype),
+            pltpu.VMEM((9, depth, width), video.dtype),
+            pltpu.SemaphoreType.DMA((steps,)),
+            pltpu.SemaphoreType.DMA,
+        ],
+        out_shape=jax.ShapeDtypeStruct((height, breadth, width), jnp.float32),
+        cost_estimate=cost,
+        compiler_params=pltpu.CompilerParams(vmem_limit_bytes=24 * 2**20),
+    )(video, part)
+
+
+def own_kernel(rows, pieces, video, base, bias, *refs):
+    parts = refs[:pieces]
+    height, breadth = video.shape[:2]
+    steps = height // rows
+    outs = refs[pieces : pieces + steps]
+    padded, weights, hidden, video_sem, part_sem, out_sem = refs[pieces + steps :]
+    depth = weights.shape[1]
+    i = pl.program_id(0)
+    group = lax.axis_index("dp")
+    starts = piece_starts(depth)
+
+    def video_copy(j):
+        channels = pl.ds(pl.multiple_of((1 - group) * depth, 128), depth)
+        return pltpu.make_async_copy(
+            video.at[pl.ds(j * rows, rows), :, channels],
+            padded.at[pl.ds(j * rows + 1, rows)],
+            video_sem.at[j],
+        )
+
+    def part_copy(p):
+        there = weights.at[:, pl.ds(aligned(starts[p]), parts[p].shape[1])]
+        return pltpu.make_async_copy(parts[p], there, part_sem.at[p])
+
+    def out_copy(j):
+        return pltpu.make_async_copy(hidden.at[j], outs[j], out_sem.at[j])
+
+    @pl.when(i == 0)
+    def _():
+        video_copy(0).start()
+        for p in range(pieces):
+            part_copy(p).start()
+        for j in range(1, steps):
+            video_copy(j).start()
+        padded[0] = jnp.zeros(padded.shape[1:], padded.dtype)
+        padded[height + 1] = jnp.zeros(padded.shape[1:], padded.dtype)
+        video_copy(0).wait()
+        for p in range(pieces):
+            part_copy(p).wait()
+
+    @pl.when(i + 1 < steps)
+    def _():
+        video_copy(i + 1).wait()
+
+    for columns in halves(weights.shape[2]):
+        total = rows_conv(padded, weights, i * rows, rows, breadth, columns)
+        total = silu(total + base[:, :, columns].reshape(total.shape) + bias[:, columns])
+        hidden[i, :, :, columns] = total.astype(hidden.dtype).reshape(rows, breadth, -1)
+
+    for j in range(steps):
+
+        @pl.when(i == j)
+        def _():
+            out_copy(j).start()
+
+    @pl.when(i == steps - 1)
+    def _():
+        for j in range(steps):
+            out_copy(j).wait()
+
+
+def own_call(video, base, bias, parts, depth, rows, cost):
+    height, breadth, _ = video.shape
+    width = base.shape[2]
+    steps = height // rows
+    return pl.pallas_call(
+        functools.partial(own_kernel, rows, len(parts)),
+        grid=(steps,),
+        in_specs=[
+            ANY,
+            pl.BlockSpec((rows, breadth, width), lambda i: (i, 0, 0)),
+            pl.BlockSpec((1, width), lambda i: (0, 0)),
+        ]
+        + [ANY] * len(parts),
+        out_specs=[ANY] * steps,
+        scratch_shapes=[
+            pltpu.VMEM((height + 2, breadth, depth), video.dtype),
+            pltpu.VMEM((9, depth, width), video.dtype),
+            pltpu.VMEM((steps, rows, breadth, width), video.dtype),
+            pltpu.SemaphoreType.DMA((steps,)),
+            pltpu.SemaphoreType.DMA((len(parts),)),
+            pltpu.SemaphoreType.DMA((steps,)),
+        ],
+        out_shape=[jax.ShapeDtypeStruct((rows, breadth, width), video.dtype)] * steps,
+        cost_estimate=cost,
+        compiler_params=pltpu.CompilerParams(vmem_limit_bytes=24 * 2**20),
+    )(video, base, bias, *parts)
+
+
+def mix_kernel(rows, begin, blocks, given, pieces, aliased, tiles, *refs):
+    refs = list(refs)
+
+    def take(count):
+        taken = refs[:count]
+        del refs[:count]
+        return taken
+
+    steps = pl.num_programs(0)
+    owns, mates = take(blocks), take(blocks)
+    fars = take(blocks if given else 1)
+    temporal_parts = take(1 + pieces[1])
+    spatial_parts = [] if given else take(1 + pieces[0])
+    spatial_bias, temporal_bias = take(2)
+    take(aliased)
+    (out,) = take(1)
+    own, mate, far, temporal, spatial, row_sem, mate_sem, far_sem, temporal_sem, spatial_sem = refs
+    breadth, width = out.shape[1:]
+    depth = temporal.shape[1]
+    group, _, core = seat()
+    tile = lax.axis_index("tile")
+    present = jnp.where(core == 0, tile > 0, tile < tiles - 1)
+    i = pl.program_id(0)
+
+    def part_copies(parts, weights, sem):
+        held = parts[0].shape[1]
+        there = (1 - group) * held
+        if len(parts) == 3:
+            starts = [group * held, there + core * (held // 2), there + (1 - core) * (held // 2)]
+        else:
+            starts = [group * held] + [there + start for start in piece_starts(held)]
+        return [
+            pltpu.make_async_copy(
+                part, weights.at[:, pl.ds(aligned(start), part.shape[1])], sem.at[p]
+            )
+            for p, (part, start) in enumerate(zip(parts, starts, strict=True))
+        ]
+
+    def block_copies(sources, target, sem):
+        return [
+            pltpu.make_async_copy(source, target.at[pl.ds(p * source.shape[0], source.shape[0])], sem.at[p])
+            for p, source in enumerate(sources)
+        ]
+
+    def far_copies():
+        if given:
+            return block_copies(fars, far, far_sem)
+        low = begin - 1
+        start, end = max(low, 0), min(low + far.shape[0], fars[0].shape[0])
+        return [
+            pltpu.make_async_copy(
+                fars[0].at[pl.ds(start, end - start)], far.at[pl.ds(start - low, end - start)], far_sem.at[0]
+            )
+        ]
+
+    first = part_copies(temporal_parts, temporal, temporal_sem)
+    first += block_copies(owns, own, row_sem) + block_copies(mates, mate, mate_sem)
+    second = far_copies() + ([] if given else part_copies(spatial_parts, spatial, spatial_sem))
+
+    @pl.when(i == 0)
+    def _():
+        for copy in first + second:
+            copy.start()
+        if not given and begin == 0:
+            far[0] = jnp.zeros(far.shape[1:], far.dtype)
+        for copy in first:
+            copy.wait()
+
+    count = rows * breadth
+    here = pl.ds(i * rows, rows)
+    own_lines = own[here].reshape(count, depth)
+    mate_lines = mate[here].reshape(count, depth)
+    mate_tap, far_tap = 2 - 2 * core, 2 * core
+    totals = [
+        dot(own_lines, temporal[1, :, columns]) + dot(mate_lines, temporal[mate_tap, :, columns])
+        for columns in halves(width)
+    ]
+
+    @pl.when(i == 0)
+    def _():
+        for copy in second:
+            copy.wait()
+
+    if given:
+        far_lines = far[here].reshape(count, depth)
+    else:
+        far_lines = jnp.concatenate(
+            [
+                silu(rows_conv(far, spatial, i * rows, rows, breadth, columns) + spatial_bias[:, columns]).astype(
+                    far.dtype
+                )
+                for columns in halves(depth)
+            ],
+            axis=1,
+        )
+    far_lines = jnp.where(present, far_lines, jnp.zeros_like(far_lines))
+    for total, columns in zip(totals, halves(width), strict=True):
+        total += dot(far_lines, temporal[far_tap, :, columns]) + temporal_bias[:, columns]
+        out[:, :, columns] = total.astype(out.dtype).reshape(rows, breadth, -1)
+
+
+def mix_call(shape, owns, mates, fars, given, temporal_parts, spatial_parts, biases, before, begin, rows, tiles, cost):
+    height, breadth, width = shape
+    dtype = owns[0].dtype
+    count = sum(own.shape[0] for own in owns)
+    depth = owns[0].shape[2]
+    aliased = 0 if before is None else 1
+    operands = [*owns, *mates, *fars, *temporal_parts, *spatial_parts]
+    whole = pl.BlockSpec((1, width), lambda i: (0, 0))
+    pieces = (len(spatial_parts) - 1, len(temporal_parts) - 1)
+    return pl.pallas_call(
+        functools.partial(mix_kernel, rows, begin, len(owns), given, pieces, aliased, tiles),
+        grid=(count // rows,),
+        in_specs=[ANY] * len(operands) + [whole, whole] + [ANY] * aliased,
+        out_specs=pl.BlockSpec((rows, breadth, width), lambda i: (i + begin // rows, 0, 0)),
+        scratch_shapes=[
+            pltpu.VMEM((count, breadth, depth), dtype),
+            pltpu.VMEM((count, breadth, depth), dtype),
+            pltpu.VMEM((count if given else count + 2, breadth, depth), dtype),
+            pltpu.VMEM((3, depth, width), dtype),
+            pltpu.VMEM((8, 128) if given else (9, depth, depth), dtype),
+            pltpu.SemaphoreType.DMA((len(owns),)),
+            pltpu.SemaphoreType.DMA((len(owns),)),
+            pltpu.SemaphoreType.DMA((len(fars),)),
+            pltpu.SemaphoreType.DMA((len(temporal_parts),)),
+            pltpu.SemaphoreType.DMA((max(len(spatial_parts), 1),)),
+        ],
+        out_shape=jax.ShapeDtypeStruct(shape, dtype),
+        input_output_aliases={len(operands) + 2: 0} if aliased else {},
+        cost_estimate=cost,
+        compiler_params=pltpu.CompilerParams(vmem_limit_bytes=30 * 2**20),
+    )(*operands, *biases, *([before] if aliased else []))
+
+
+def near_device(videos, spatial_filter, temporal_filter, spatial_bias, temporal_bias):
+    shape = videos.shape[2:]
+    height = shape[0]
+    video = videos.reshape(shape)
+    biases = [spatial_bias.reshape(1, -1), temporal_bias.reshape(1, -1)]
+    tiles = lax.axis_size("tile")
+    _, _, core = seat()
+    depth = spatial_filter.shape[1]
+    small, large = piece_rows(depth)
+    starts = piece_starts(depth)
+    swap = [(0, 1), (1, 0)]
+    mates = [(i, i ^ 1) for i in range(tiles)]
+    pairs = [(i, i ^ 4) for i in range(tiles)]
+    across = [pair for i in range(1, tiles - 1, 2) for pair in ((i, i + 1), (i + 1, i))]
+    light = pl.CostEstimate(flops=1000, bytes_accessed=1000, transcendentals=0)
+
+    rows = 8
+    sent = height - rows + 1
+    a_y = lax.ppermute(lax.dynamic_slice_in_dim(spatial_filter, starts[0], small, axis=1), "dp", swap)
+    b_y = lax.ppermute(lax.dynamic_slice_in_dim(spatial_filter, starts[4], large, axis=1), "dp", swap)
+    far = lax.ppermute(video[:sent], "tile", across)
+    a_z = lax.ppermute(a_y, "tile", pairs)
+    base = base_call(video, spatial_filter, rows, light)
+    a_y, a_z, b_y, base = lax.optimization_barrier((a_y, a_z, b_y, base))
+    pieces = [a_y, a_z, *(lax.ppermute(part, "tile", mates) for part in (a_y, a_z)), b_y]
+    pieces.append(lax.ppermute(b_y, "tile", mates))
+    part = temporal_filter.shape[1] // 2
+    c_y = lax.ppermute(lax.dynamic_slice_in_dim(temporal_filter, core * part, part, axis=1), "dp", swap)
+    temporal_parts = [temporal_filter, c_y, lax.ppermute(c_y, "tile", mates)]
+    spatial_parts = [spatial_filter, *pieces]
+
+    own = own_call(video, base, biases[0], pieces, depth, rows, light)
+    mate = [lax.ppermute(block, "tile", mates) for block in own]
+    last = lax.ppermute(own[-1], "tile", across)
+    out = mix_call(
+        shape, own[:-1], mate[:-1], [far], False, temporal_parts, spatial_parts, biases, None, 0, rows, tiles, light
+    )
+    out = mix_call(
+        shape, own[-1:], mate[-1:], [last], True, temporal_parts, [], biases, out, height - rows, rows, tiles, light
+    )
+    return out.reshape(videos.shape)
 
 
 def padded_2(block, sides, width):
@@ -41,16 +421,26 @@
     return jnp.dot(columns.reshape(-1, 3 * width), matrix, preferred_element_type=jnp.float32)
 
 
-def per_device(videos, spatial_filter, temporal_filter, spatial_bias, temporal_bias):
+def any_device(videos, spatial_filter, temporal_filter, spatial_bias, temporal_bias):
     samples, frames, height, breadth, channels = videos.shape
-    count_frames = videos.shape[1]
     padded = jnp.pad(videos, ((0, 0), (0, 0), (1, 1), (1, 1), (0, 0)))
     summed = spatial_term(padded, lax.all_gather(spatial_filter, "dp", axis=1, tiled=True))
     activated = jax.nn.silu(summed + spatial_bias).astype(jnp.bfloat16)
-    hidden = activated.reshape(samples, count_frames, height, breadth, channels)
+    hidden = activated.reshape(samples, frames, height, breadth, channels)
     framed = padded_2(hidden, (("tile", 1),), 1)
     result = temporal_term(framed, lax.all_gather(temporal_filter, "dp", axis=1, tiled=True))
     return (result + temporal_bias).astype(jnp.bfloat16).reshape(videos.shape)
+
+
+def per_device(videos, *rest):
+    near = (
+        videos.shape[0] == 1
+        and videos.shape[1] == 1
+        and videos.shape[2] % 32 == 0
+        and lax.axis_size("dp") == 2
+        and lax.axis_size("tile") % 8 == 0
+    )
+    return (near_device if near else any_device)(videos, *rest)
 
 
 def solution(mesh):

time: 154 us -> 73.1 us (0.47)
  waiting for transfers between devices: 89 us -> 18.3 us
  Pallas kernels: 0 us -> 29.8 us
  matrix products: 23.2 us -> 0 us
  between operations: 13.4 us -> 0.17 us
  local copies, waits for them, and re-layouts: 21.3 us -> 8.24 us
  starting transfers between devices: 5.86 us -> 16.2 us
    all_gather x2 -> x0, waiting for transfers between devices: 72.3 us -> none  [the longest x1 45 us: per_device(): lax.all_gather(spatial_filter, 'dp', axis=1, tiled=True)]
    pallas_call x0 -> x4, Pallas kernels: none -> 29.8 us  [the longest x2 16.1 us: mix_call(): pl.pallas_call(functools.partial(mix_kernel, rows, begin, len(owns), give...]
    dot_general x2 -> x0, matrix products: 23.2 us -> none  [the longest x1 15.8 us: spatial_term(): jnp.dot(columns.reshape(-1, 9 * width), matrix, preferred_element_type=jn...]
    unnamed x14 -> x12, local copies, waits for them, and re-layouts: 18.7 us -> 1.69 us
    ppermute x2 -> x14, starting transfers between devices: 5.82 us -> 16.2 us  [the longest x1 4.5 us: near_device(): far = lax.ppermute(video[:sent], 'tile', across)]
    dynamic_slice x0 -> x3, local copies, waits for them, and re-layouts: none -> 3.64 us  [the longest x1 1.86 us: near_device(): lax.dynamic_slice_in_dim(spatial_filter, starts[0], small, axis=1)]
    slice x0 -> x1, local copies, waits for them, and re-layouts: none -> 2.91 us  [near_device(): far = lax.ppermute(video[:sent], 'tile', across)]
    concatenate x1 -> x0, local copies, waits for them, and re-layouts: 2.58 us -> none  [spatial_term(): jnp.concatenate([padded[:, :, row_off:row_off + height, col_off:col_off +...]
  transfers between devices with their start and end apart: 4 -> 14, of which waited for: 3 -> 3; matrix products, arithmetic and copies ran while one was open for 14% -> 5% of each run, Pallas kernels for 0% -> 37%
where the time goes in v2:
time: 73.1 us; the launch traced here: 72.7 us
  Pallas kernels  29.8 us (41%)
  waiting for transfers between devices  18.3 us (25%)
  starting transfers between devices  16.2 us (22%)
  local copies, waits for them, and re-layouts  8.24 us (11%)
    pallas_call x2, Pallas kernels, mix_call(): pl.pallas_call(functools.partial(mix_kernel, rows, begin, len(owns), give...  16.1 us
    ppermute x1, waiting for transfers between devices, near_device(): lax.ppermute(lax.dynamic_slice_in_dim(spatial_filter, starts[0], small, a...  9.61 us
    pallas_call x1, Pallas kernels, own_call(): pl.pallas_call(functools.partial(own_kernel, rows, len(parts)), grid=(ste...  7.82 us
    ppermute x1, waiting for transfers between devices, near_device(): lax.ppermute(lax.dynamic_slice_in_dim(spatial_filter, starts[4], large, a...  6.32 us
    pallas_call x1, Pallas kernels, base_call(): pl.pallas_call(functools.partial(base_kernel, rows), grid=(steps,), in_sp...  5.9 us
    ppermute x1, starting transfers between devices, near_device(): far = lax.ppermute(video[:sent], 'tile', across)  4.5 us
    ppermute x1, starting transfers between devices, near_device(): last = lax.ppermute(own[-1], 'tile', across)  2.92 us
    slice x1, local copies, waits for them, and re-layouts, near_device(): far = lax.ppermute(video[:sent], 'tile', across)  2.91 us
  transfers between devices with their start and end apart: 14, of which 3 were waited for; matrix products, arithmetic and copies ran while one was open for 5% of the time, Pallas kernels for 37%

profile of v2, /device:TPU:1, one launch (start us, length us, event | category | flops | bytes accessed | tf_op | source)
XLA Modules:
  0.0 72.7 jit_solution(3779506491711852139)
XLA Ops:
  0.0 0.0 copy-start
  0.0 0.0 copy-start.3
  0.0 2.9 %slice_bitcast_fusion = bf16[25,64,512]{2,1,0:T(8,128)(2,1)} fusion(bf16[1,1,32,64,512]{4,3,2,1,0:T(8,128)(2,1)} %param.5), kind=kLoop, calls=%fused_computation | loop fusion | bytes 3276800 | tf_op jit(solution)/shard_map/slice | solution.py:364
  2.9 4.5 %collective-permute-start.13 = (bf16[25,64,512]{2,1,0:T(8,128)(2,1)}, bf16[25,64,512]{2,1,0:T(8,128)(2,1)}, u32[]{:S(2)}, u32[]{:S(2)}) collective-permute-start(bf16[25,64,512]{2,1,0:T(8,128)(2,1)} %slice_bitcast_fusion), channel_id=1, source_target_pairs={{1,2},{2,1},{3,4},{4,3},{5,6},{6,5},{7,8},{8,7},{9,10},{10,9},{11,... | collective-permute-start | bytes 4915208 | tf_op jit(solution)/shard_map/ppermute | solution.py:364
  7.5 1.9 %constant_dynamic-slice_fusion.2 = bf16[9,48,512]{2,1,0:T(8,128)(2,1)} fusion(bf16[9,256,512]{2,1,0:T(8,128)(2,1)} %refs_10_.1, s32[]{:T(128)S(6)} %select_n.15), kind=kLoop, calls=%fused_computation.3 | loop fusion | bytes 884740 | tf_op jit(solution)/shard_map/dynamic_slice | solution.py:362
  9.3 1.2 %collective-permute-start = (bf16[9,48,512]{2,1,0:T(8,128)(2,1)}, bf16[9,48,512]{2,1,0:T(8,128)(2,1)S(1)}, u32[]{:S(2)}, u32[]{:S(2)}) collective-permute-start(bf16[9,48,512]{2,1,0:T(8,128)(2,1)} %constant_dynamic-slice_fusion.2), channel_id=1, source_target_pairs={{0,16},{16,0},{1,17},{17,1},{2,18},{18,2},{3,19},{19,3},{4,20},{20... | collective-permute-start | bytes 1327112 | tf_op jit(solution)/shard_map/ppermute | solution.py:362
  10.5 9.6 %collective-permute-done.refs_0_.refs_11_ = bf16[9,48,512]{2,1,0:T(8,128)(2,1)S(1)} collective-permute-done((bf16[9,48,512]{2,1,0:T(8,128)(2,1)}, bf16[9,48,512]{2,1,0:T(8,128)(2,1)S(1)}, u32[]{:S(2)}, u32[]{:S(2)}) %collective-permute-start) | collective-permute-done | bytes 442400 | tf_op jit(solution)/shard_map/ppermute | solution.py:362
  20.2 2.8 %collective-permute-start.1 = (bf16[9,48,512]{2,1,0:T(8,128)(2,1)S(1)}, bf16[9,48,512]{2,1,0:T(8,128)(2,1)}, u32[]{:S(2)}, u32[]{:S(2)}) collective-permute-start(bf16[9,48,512]{2,1,0:T(8,128)(2,1)S(1)} %collective-permute-done.refs_0_.refs_11_), channel_id=1, source_target_pairs={{0,4},{1,5},{2,6},{3,7},{4,0},{5,1},{6,2},{7,3},{8,12},{9,13},{10,... | collective-permute-start | bytes 1327112 | tf_op jit(solution)/shard_map/ppermute | solution.py:365
  22.9 0.0 copy-done.3
  22.9 0.8 %constant_dynamic-slice_fusion = bf16[3,128,512]{2,1,0:T(8,128)(2,1)} fusion(bf16[3,256,512]{2,1,0:T(8,128)(2,1)S(1)} %copy-done.3, s32[]{:T(128)S(6)} %select_n.17), kind=kLoop, calls=%fused_computation.1 | loop fusion | bytes 786436 | tf_op jit(solution)/shard_map/dynamic_slice | solution.py:371
  23.7 1.2 %collective-permute-start.8 = (bf16[3,128,512]{2,1,0:T(8,128)(2,1)}, bf16[3,128,512]{2,1,0:T(8,128)(2,1)}, u32[]{:S(2)}, u32[]{:S(2)}) collective-permute-start(bf16[3,128,512]{2,1,0:T(8,128)(2,1)} %constant_dynamic-slice_fusion), channel_id=1, source_target_pairs={{0,16},{16,0},{1,17},{17,1},{2,18},{18,2},{3,19},{19,3},{4,20},{20... | collective-permute-start | bytes 1179656 | tf_op jit(solution)/shard_map/ppermute | solution.py:371
  25.0 1.0 %constant_dynamic-slice_fusion.1 = bf16[9,32,512]{2,1,0:T(8,128)(2,1)S(1)} fusion(bf16[9,256,512]{2,1,0:T(8,128)(2,1)} %refs_10_.1, s32[]{:T(128)S(6)} %select_n.16), kind=kLoop, calls=%fused_computation.2 | loop fusion | bytes 589828 | tf_op jit(solution)/shard_map/dynamic_slice | solution.py:363
  26.0 0.3 collective-permute-start.2
  26.3 0.0 copy-done
  26.3 0.0 copy-start.1
  26.3 1.7 %copy-done.1 = bf16[9,256,512]{2,1,0:T(8,128)(2,1)S(1)} copy-done((bf16[9,256,512]{2,1,0:T(8,128)(2,1)S(1)}, bf16[9,256,512]{2,1,0:T(8,128)(2,1)}, u32[]{:S(2)}) %copy-start.1) | copy-done | bytes 2359320
  27.9 0.0 copy-start.4
  27.9 5.9 %shard_map.55.base = f32[32,64,512]{2,1,0:T(8,128)S(1)} custom-call(bf16[32,64,512]{2,1,0:T(8,128)(2,1)S(1)} %bitcast.6, bf16[9,256,512]{2,1,0:T(8,128)(2,1)S(1)} %copy-done.1), custom_call_target="tpu_custom_call" | custom-call | flops 1000 | bytes 1000 | tf_op jit(solution)/shard_map/pallas_call | solution.py:105
  33.8 6.3 %collective-permute-done.2.refs_4_.refs_15_ = bf16[9,32,512]{2,1,0:T(8,128)(2,1)S(1)} collective-permute-done((bf16[9,32,512]{2,1,0:T(8,128)(2,1)S(1)}, bf16[9,32,512]{2,1,0:T(8,128)(2,1)S(1)}, u32[]{:S(2)}, u32[]{:S(2)}) %collective-permute-start.2) | collective-permute-done | bytes 294944 | tf_op jit(solution)/shard_map/ppermute | solution.py:363
  40.2 0.0 collective-permute-done.1.refs_1_.refs_12_
  40.2 1.6 %collective-permute-start.3 = (bf16[9,48,512]{2,1,0:T(8,128)(2,1)S(1)}, bf16[9,48,512]{2,1,0:T(8,128)(2,1)S(1)}, u32[]{:S(2)}, u32[]{:S(2)}) collective-permute-start(bf16[9,48,512]{2,1,0:T(8,128)(2,1)S(1)} %collective-permute-done.refs_0_.refs_11_), channel_id=1, source_target_pairs={{0,1},{1,0},{2,3},{3,2},{4,5},{5,4},{6,7},{7,6},{8,9},{9,8},{10,11... | collective-permute-start | bytes 1327112 | tf_op jit(solution)/shard_map/ppermute | solution.py:368
  41.8 0.0 collective-permute-start.4
  41.8 0.0 collective-permute-done.8.refs_8_.refs_4_
  41.8 0.5 collective-permute-start.9
  42.3 0.0 collective-permute-start.5
  42.3 2.3 %collective-permute-done.5.refs_5_.refs_16_ = bf16[9,32,512]{2,1,0:T(8,128)(2,1)S(1)} collective-permute-done((bf16[9,32,512]{2,1,0:T(8,128)(2,1)S(1)}, bf16[9,32,512]{2,1,0:T(8,128)(2,1)S(1)}, u32[]{:S(2)}, u32[]{:S(2)}) %collective-permute-start.5) | collective-permute-done | bytes 294944 | tf_op jit(solution)/shard_map/ppermute | solution.py:369
  44.7 0.0 collective-permute-done.3.refs_2_.refs_13_
  44.7 0.0 collective-permute-done.4.refs_3_.refs_14_
  44.7 0.0 copy-done.4
  44.7 0.0 copy-start.2
  44.7 0.0 copy-start.5
  44.7 7.8 %shard_map.56 = (bf16[8,64,512]{2,1,0:T(8,128)(2,1)S(1)}, bf16[8,64,512]{2,1,0:T(8,128)(2,1)S(1)}, bf16[8,64,512]{2,1,0:T(8,128)(2,1)S(1)}, bf16[8,64,512]{2,1,0:T(8,128)(2,1)S(1)}) custom-call(bf16[32,64,512]{2,1,0:T(8,128)(2,1)S(1)} %bitcast.7, f32[32,64,512]{2,1,0:T(8,128)S(1)} %shard_map.55.base, f32[1,512]{1,0:T(1,128)S(1)} %bitcast.8, ...), custom_call_target="tpu_custom_call" | custom-call | flops 1000 | bytes 1000 | tf_op jit(solution)/shard_map/pallas_call | solution.py:186
  52.5 0.4 collective-permute-start.10
  53.0 0.1 collective-permute-start.11
  53.1 0.4 collective-permute-start.12
  53.5 0.0 collective-permute-done.9.refs_9_.refs_5_
  53.5 0.1 collective-permute-start.6
  53.6 0.0 collective-permute-done.13.refs_6_
  53.6 2.9 %collective-permute-start.7 = (bf16[8,64,512]{2,1,0:T(8,128)(2,1)S(1)}, bf16[8,64,512]{2,1,0:T(8,128)(2,1)S(1)}, u32[]{:S(2)}, u32[]{:S(2)}) collective-permute-start(bf16[8,64,512]{2,1,0:T(8,128)(2,1)S(1)} %get-tuple-element.17.refs_0_), channel_id=1, source_target_pairs={{1,2},{2,1},{3,4},{4,3},{5,6},{6,5},{7,8},{8,7},{9,10},{10,9},{11,... | collective-permute-start | bytes 1572872 | tf_op jit(solution)/shard_map/ppermute | solution.py:377
  56.5 0.0 collective-permute-done.10.refs_3_
  56.6 0.0 collective-permute-done.11.refs_4_
  56.6 0.0 collective-permute-done.12.refs_5_
  56.6 0.0 copy-done.2
  56.6 0.0 copy-done.5
  56.6 13.1 %shard_map.57.refs_8_ = bf16[32,64,512]{2,1,0:T(8,128)(2,1)} custom-call(bf16[8,64,512]{2,1,0:T(8,128)(2,1)S(1)} %get-tuple-element.18.refs_0_, bf16[8,64,512]{2,1,0:T(8,128)(2,1)S(1)} %get-tuple-element.19.refs_1_, bf16[8,64,512]{2,1,0:T(8,128)(2,1)S(1)} %get-tuple-element.20.refs_2_, bf16[8,64,512]{2,1,0:T(8,128)(2,1)S(1)} %collective-permute-done.10.refs_3_, ...), custom_call_target="tpu_custom_call" | custom-call | flops 1000 | bytes 1000 | tf_op jit(solution)/shard_map/pallas_call | solution.py:320
  69.7 0.0 collective-permute-done.6.refs_1_
  69.7 0.0 collective-permute-done.7.refs_2_
  69.7 3.0 %shard_map.58 = bf16[32,64,512]{2,1,0:T(8,128)(2,1)} custom-call(bf16[8,64,512]{2,1,0:T(8,128)(2,1)S(1)} %get-tuple-element.17.refs_0_, bf16[8,64,512]{2,1,0:T(8,128)(2,1)S(1)} %collective-permute-done.6.refs_1_, bf16[8,64,512]{2,1,0:T(8,128)(2,1)S(1)} %collective-permute-done.7.refs_2_, ...), custom_call_target="tpu_custom_call", output_to_operand_aliasing={{}: (8, {})} | custom-call | flops 1000 | bytes 1000 | tf_op jit(solution)/shard_map/pallas_call | solution.py:320
Async XLA Ops:
  0.0 26.3 %copy-start = (bf16[1,1,32,64,512]{4,3,2,1,0:T(8,128)(2,1)S(1)}, bf16[1,1,32,64,512]{4,3,2,1,0:T(8,128)(2,1)}, u32[]{:S(2)}) copy-start(bf16[1,1,32,64,512]{4,3,2,1,0:T(8,128)(2,1)} %param.5) | copy-start | bytes 6291460
  0.0 22.9 %copy-start.3 = (bf16[3,256,512]{2,1,0:T(8,128)(2,1)S(1)}, bf16[3,256,512]{2,1,0:T(8,128)(2,1)}, u32[]{:S(2)}) copy-start(bf16[3,256,512]{2,1,0:T(8,128)(2,1)} %refs_3_.1) | copy-start | bytes 2359300
  2.9 50.7 %collective-permute-start.13 = (bf16[25,64,512]{2,1,0:T(8,128)(2,1)}, bf16[25,64,512]{2,1,0:T(8,128)(2,1)}, u32[]{:S(2)}, u32[]{:S(2)}) collective-permute-start(bf16[25,64,512]{2,1,0:T(8,128)(2,1)} %slice_bitcast_fusion), channel_id=1, source_target_pairs={{1,2},{2,1},{3,4},{4,3},{5,6},{6,5},{7,8},{8,7},{9,10},{10,9},{11,... | collective-permute-start | bytes 4915208 | tf_op jit(solution)/shard_map/ppermute | solution.py:364
  9.3 10.9 %collective-permute-start = (bf16[9,48,512]{2,1,0:T(8,128)(2,1)}, bf16[9,48,512]{2,1,0:T(8,128)(2,1)S(1)}, u32[]{:S(2)}, u32[]{:S(2)}) collective-permute-start(bf16[9,48,512]{2,1,0:T(8,128)(2,1)} %constant_dynamic-slice_fusion.2), channel_id=1, source_target_pairs={{0,16},{16,0},{1,17},{17,1},{2,18},{18,2},{3,19},{19,3},{4,20},{20... | collective-permute-start | bytes 1327112 | tf_op jit(solution)/shard_map/ppermute | solution.py:362
  20.2 20.0 %collective-permute-start.1 = (bf16[9,48,512]{2,1,0:T(8,128)(2,1)S(1)}, bf16[9,48,512]{2,1,0:T(8,128)(2,1)}, u32[]{:S(2)}, u32[]{:S(2)}) collective-permute-start(bf16[9,48,512]{2,1,0:T(8,128)(2,1)S(1)} %collective-permute-done.refs_0_.refs_11_), channel_id=1, source_target_pairs={{0,4},{1,5},{2,6},{3,7},{4,0},{5,1},{6,2},{7,3},{8,12},{9,13},{10,... | collective-permute-start | bytes 1327112 | tf_op jit(solution)/shard_map/ppermute | solution.py:365
  23.7 18.1 %collective-permute-start.8 = (bf16[3,128,512]{2,1,0:T(8,128)(2,1)}, bf16[3,128,512]{2,1,0:T(8,128)(2,1)}, u32[]{:S(2)}, u32[]{:S(2)}) collective-permute-start(bf16[3,128,512]{2,1,0:T(8,128)(2,1)} %constant_dynamic-slice_fusion), channel_id=1, source_target_pairs={{0,16},{16,0},{1,17},{17,1},{2,18},{18,2},{3,19},{19,3},{4,20},{20... | collective-permute-start | bytes 1179656 | tf_op jit(solution)/shard_map/ppermute | solution.py:371
  26.0 14.2 %collective-permute-start.2 = (bf16[9,32,512]{2,1,0:T(8,128)(2,1)S(1)}, bf16[9,32,512]{2,1,0:T(8,128)(2,1)S(1)}, u32[]{:S(2)}, u32[]{:S(2)}) collective-permute-start(bf16[9,32,512]{2,1,0:T(8,128)(2,1)S(1)} %constant_dynamic-slice_fusion.1), channel_id=1, source_target_pairs={{0,16},{16,0},{1,17},{17,1},{2,18},{18,2},{3,19},{19,3},{4,20},{20... | collective-permute-start | bytes 884744 | tf_op jit(solution)/shard_map/ppermute | solution.py:363
  26.3 1.7 %copy-start.1 = (bf16[9,256,512]{2,1,0:T(8,128)(2,1)S(1)}, bf16[9,256,512]{2,1,0:T(8,128)(2,1)}, u32[]{:S(2)}) copy-start(bf16[9,256,512]{2,1,0:T(8,128)(2,1)} %refs_10_.1) | copy-start | bytes 7077892
  27.9 16.7 %copy-start.4 = (f32[512]{0:T(512)S(1)}, f32[512]{0:T(512)}, u32[]{:S(2)}) copy-start(f32[512]{0:T(512)} %param.8) | copy-start | bytes 6148
  40.2 4.5 %collective-permute-start.3 = (bf16[9,48,512]{2,1,0:T(8,128)(2,1)S(1)}, bf16[9,48,512]{2,1,0:T(8,128)(2,1)S(1)}, u32[]{:S(2)}, u32[]{:S(2)}) collective-permute-start(bf16[9,48,512]{2,1,0:T(8,128)(2,1)S(1)} %collective-permute-done.refs_0_.refs_11_), channel_id=1, source_target_pairs={{0,1},{1,0},{2,3},{3,2},{4,5},{5,4},{6,7},{7,6},{8,9},{9,8},{10,11... | collective-permute-start | bytes 1327112 | tf_op jit(solution)/shard_map/ppermute | solution.py:368
  41.8 2.9 %collective-permute-start.4 = (bf16[9,48,512]{2,1,0:T(8,128)(2,1)}, bf16[9,48,512]{2,1,0:T(8,128)(2,1)S(1)}, u32[]{:S(2)}, u32[]{:S(2)}) collective-permute-start(bf16[9,48,512]{2,1,0:T(8,128)(2,1)} %collective-permute-done.1.refs_1_.refs_12_), channel_id=1, source_target_pairs={{0,1},{1,0},{2,3},{3,2},{4,5},{5,4},{6,7},{7,6},{8,9},{9,8},{10,11... | collective-permute-start | bytes 1327112 | tf_op jit(solution)/shard_map/ppermute | solution.py:368
  41.8 11.7 %collective-permute-start.9 = (bf16[3,128,512]{2,1,0:T(8,128)(2,1)}, bf16[3,128,512]{2,1,0:T(8,128)(2,1)S(1)}, u32[]{:S(2)}, u32[]{:S(2)}) collective-permute-start(bf16[3,128,512]{2,1,0:T(8,128)(2,1)} %collective-permute-done.8.refs_8_.refs_4_), channel_id=1, source_target_pairs={{0,1},{1,0},{2,3},{3,2},{4,5},{5,4},{6,7},{7,6},{8,9},{9,8},{10,11... | collective-permute-start | bytes 1179656 | tf_op jit(solution)/shard_map/ppermute | solution.py:372
  42.3 2.3 %collective-permute-start.5 = (bf16[9,32,512]{2,1,0:T(8,128)(2,1)S(1)}, bf16[9,32,512]{2,1,0:T(8,128)(2,1)S(1)}, u32[]{:S(2)}, u32[]{:S(2)}) collective-permute-start(bf16[9,32,512]{2,1,0:T(8,128)(2,1)S(1)} %collective-permute-done.2.refs_4_.refs_15_), channel_id=1, source_target_pairs={{0,1},{1,0},{2,3},{3,2},{4,5},{5,4},{6,7},{7,6},{8,9},{9,8},{10,11... | collective-permute-start | bytes 884744 | tf_op jit(solution)/shard_map/ppermute | solution.py:369
  44.7 11.9 %copy-start.2 = (bf16[9,256,512]{2,1,0:T(8,128)(2,1)S(1)}, bf16[9,256,512]{2,1,0:T(8,128)(2,1)}, u32[]{:S(2)}) copy-start(bf16[9,256,512]{2,1,0:T(8,128)(2,1)} %refs_10_.1) | copy-start | bytes 7077892
  44.7 11.9 %copy-start.5 = (f32[512]{0:T(512)S(1)}, f32[512]{0:T(512)}, u32[]{:S(2)}) copy-start(f32[512]{0:T(512)} %param.9) | copy-start | bytes 6148
  52.5 4.0 %collective-permute-start.10 = (bf16[8,64,512]{2,1,0:T(8,128)(2,1)S(1)}, bf16[8,64,512]{2,1,0:T(8,128)(2,1)S(1)}, u32[]{:S(2)}, u32[]{:S(2)}) collective-permute-start(bf16[8,64,512]{2,1,0:T(8,128)(2,1)S(1)} %get-tuple-element.18.refs_0_), channel_id=1, source_target_pairs={{0,1},{1,0},{2,3},{3,2},{4,5},{5,4},{6,7},{7,6},{8,9},{9,8},{10,11... | collective-permute-start | bytes 1572872 | tf_op jit(solution)/shard_map/ppermute | solution.py:376
  53.0 3.6 %collective-permute-start.11 = (bf16[8,64,512]{2,1,0:T(8,128)(2,1)S(1)}, bf16[8,64,512]{2,1,0:T(8,128)(2,1)S(1)}, u32[]{:S(2)}, u32[]{:S(2)}) collective-permute-start(bf16[8,64,512]{2,1,0:T(8,128)(2,1)S(1)} %get-tuple-element.19.refs_1_), channel_id=1, source_target_pairs={{0,1},{1,0},{2,3},{3,2},{4,5},{5,4},{6,7},{7,6},{8,9},{9,8},{10,11... | collective-permute-start | bytes 1572872 | tf_op jit(solution)/shard_map/ppermute | solution.py:376
  53.1 3.5 %collective-permute-start.12 = (bf16[8,64,512]{2,1,0:T(8,128)(2,1)S(1)}, bf16[8,64,512]{2,1,0:T(8,128)(2,1)S(1)}, u32[]{:S(2)}, u32[]{:S(2)}) collective-permute-start(bf16[8,64,512]{2,1,0:T(8,128)(2,1)S(1)} %get-tuple-element.20.refs_2_), channel_id=1, source_target_pairs={{0,1},{1,0},{2,3},{3,2},{4,5},{5,4},{6,7},{7,6},{8,9},{9,8},{10,11... | collective-permute-start | bytes 1572872 | tf_op jit(solution)/shard_map/ppermute | solution.py:376
  53.5 16.2 %collective-permute-start.6 = (bf16[8,64,512]{2,1,0:T(8,128)(2,1)S(1)}, bf16[8,64,512]{2,1,0:T(8,128)(2,1)S(1)}, u32[]{:S(2)}, u32[]{:S(2)}) collective-permute-start(bf16[8,64,512]{2,1,0:T(8,128)(2,1)S(1)} %get-tuple-element.17.refs_0_), channel_id=1, source_target_pairs={{0,1},{1,0},{2,3},{3,2},{4,5},{5,4},{6,7},{7,6},{8,9},{9,8},{10,11... | collective-permute-start | bytes 1572872 | tf_op jit(solution)/shard_map/ppermute | solution.py:376
  53.6 16.1 %collective-permute-start.7 = (bf16[8,64,512]{2,1,0:T(8,128)(2,1)S(1)}, bf16[8,64,512]{2,1,0:T(8,128)(2,1)S(1)}, u32[]{:S(2)}, u32[]{:S(2)}) collective-permute-start(bf16[8,64,512]{2,1,0:T(8,128)(2,1)S(1)} %get-tuple-element.17.refs_0_), channel_id=1, source_target_pairs={{1,2},{2,1},{3,4},{4,3},{5,6},{6,5},{7,8},{8,7},{9,10},{10,9},{11,... | collective-permute-start | bytes 1572872 | tf_op jit(solution)/shard_map/ppermute | solution.py:377

commit v3 on v2

v3 whole, which is shorter than its diff:
```python
import functools

import jax
import jax.numpy as jnp
from jax import lax
from jax.experimental import pallas as pl
from jax.experimental.pallas import tpu as pltpu
from jax.sharding import PartitionSpec as P

ANY = pl.BlockSpec(memory_space=pltpu.HBM)


def dot(a, b):
    return jnp.dot(a, b, preferred_element_type=jnp.float32)


def silu(v):
    return v / (1 + jnp.exp(-v))


def halves(width):
    cut = width // 2
    return [slice(0, cut), slice(cut, width)]


def seat():
    return lax.axis_index("dp"), lax.rem(lax.axis_index("tile"), 2)


def half_starts(depth):
    _, core = seat()
    return [core * (depth // 2), (1 - core) * (depth // 2)]


def aligned(start):
    return pl.multiple_of(start, 16)


def rows_conv(padded, weights, taps, first, rows, breadth, columns):
    count = rows * breadth
    place = lax.rem(lax.broadcasted_iota(jnp.int32, (count, 1), 0), breadth)
    depth = padded.shape[2]
    lines = [padded[pl.ds(first + dy, rows)].reshape(count, depth) for dy in range(3)]

    def side(dx):
        mine = [(n, tap // 3) for n, tap in enumerate(taps) if tap % 3 == dx]
        matrix = jnp.concatenate([weights[n, :, columns] for n, _ in mine], axis=0)
        return dot(jnp.concatenate([lines[dy] for _, dy in mine], axis=1), matrix)

    total = side(1)
    total += jnp.where(place == 0, 0.0, pltpu.roll(side(0), 1, 0))
    total += jnp.where(place == breadth - 1, 0.0, pltpu.roll(side(2), count - 1, 0))
    return total


def cut_kernel(cuts, *refs):
    sources, targets, sem = refs[: len(cuts)], refs[len(cuts) : -1], refs[-1]
    copies = []
    for source, parts in zip(sources, cuts, strict=True):
        for where, _ in parts:
            n = len(copies)
            copies.append(pltpu.make_async_copy(source.at[where()], targets[n], sem.at[n]))
    for copy in copies:
        copy.start()
    for copy in copies:
        copy.wait()


def cut_call(sources, cuts, cost):
    shapes = [
        pltpu.VMEM(shape, source.dtype)
        for source, parts in zip(sources, cuts, strict=True)
        for _, shape in parts
    ]
    return pl.pallas_call(
        functools.partial(cut_kernel, cuts),
        in_specs=[ANY] * len(sources),
        out_specs=[pl.BlockSpec(memory_space=pltpu.VMEM)] * len(shapes),
        scratch_shapes=[pltpu.SemaphoreType.DMA((len(shapes),))],
        out_shape=shapes,
        cost_estimate=cost,
    )(*sources)


def conv_kernel(rows, block, taps, held, has_base, last, video, *refs):
    refs = list(refs)
    base = refs.pop(0) if has_base else None
    bias = refs.pop(0) if last else None
    pieces = 1 if held else 2
    height, breadth = video.shape[:2]
    steps = height // rows
    padded, weights, hidden, video_sem, part_sem, out_sem = refs[-6:]
    blocks = height // block
    outs = refs[-6 - (blocks if last else 1) : -6]
    parts = refs[: -6 - len(outs)]
    depth = weights.shape[1]
    i = pl.program_id(0)
    group, _ = seat()
    starts = [0] if held else half_starts(depth)

    def video_copy(j):
        channels = pl.ds(pl.multiple_of((group if held else 1 - group) * depth, 128), depth)
        return pltpu.make_async_copy(
            video.at[pl.ds(j * rows, rows), :, channels],
            padded.at[pl.ds(j * rows + 1, rows)],
            video_sem.at[j],
        )

    def part_copies():
        copies = []
        at = 0
        for n in range(0, len(parts), pieces):
            size = parts[n].shape[0]
            for p, start in enumerate(starts):
                there = weights.at[pl.ds(at, size), pl.ds(aligned(start), parts[n + p].shape[1])]
                copies.append(pltpu.make_async_copy(parts[n + p], there, part_sem.at[n + p]))
            at += size
        return copies

    def out_copy(j):
        return pltpu.make_async_copy(hidden.at[pl.ds(j * block, block)], outs[j], out_sem.at[j])

    @pl.when(i == 0)
    def _():
        video_copy(0).start()
        for copy in part_copies():
            copy.start()
        for j in range(1, steps):
            video_copy(j).start()
        padded[0] = jnp.zeros(padded.shape[1:], padded.dtype)
        padded[height + 1] = jnp.zeros(padded.shape[1:], padded.dtype)
        video_copy(0).wait()
        for copy in part_copies():
            copy.wait()

    @pl.when(i + 1 < steps)
    def _():
        video_copy(i + 1).wait()

    for columns in halves(weights.shape[2]):
        total = rows_conv(padded, weights, taps, i * rows, rows, breadth, columns)
        if has_base:
            total += base[:, :, columns].reshape(total.shape)
        if last:
            total = silu(total + bias[:, columns])
            hidden[pl.ds(i * rows, rows), :, columns] = total.astype(hidden.dtype).reshape(rows, breadth, -1)
        else:
            outs[0][:, :, columns] = total.reshape(rows, breadth, -1)

    if last:
        for j in range(blocks):

            @pl.when(i == ((j + 1) * block - 1) // rows)
            def _():
                out_copy(j).start()

        @pl.when(i == steps - 1)
        def _():
            for j in range(blocks):
                out_copy(j).wait()


def conv_call(video, base, bias, parts, depth, taps, held, rows, block, cost):
    height, breadth, _ = video.shape
    width = parts[0].shape[2]
    steps = height // rows
    last = bias is not None
    blocks = height // block
    lines = pl.BlockSpec((rows, breadth, width), lambda i: (i, 0, 0))
    specs, operands = [ANY], [video]
    if base is not None:
        specs, operands = specs + [lines], operands + [base]
    if last:
        specs, operands = specs + [pl.BlockSpec((1, width), lambda i: (0, 0))], operands + [bias]
    return pl.pallas_call(
        functools.partial(conv_kernel, rows, block, taps, held, base is not None, last),
        grid=(steps,),
        in_specs=specs + [ANY] * len(parts),
        out_specs=[ANY] * blocks if last else lines,
        scratch_shapes=[
            pltpu.VMEM((height + 2, breadth, depth), video.dtype),
            pltpu.VMEM((len(taps), depth, width), video.dtype),
            pltpu.VMEM((height, breadth, width) if last else (8, 128), video.dtype),
            pltpu.SemaphoreType.DMA((steps,)),
            pltpu.SemaphoreType.DMA((len(parts),)),
            pltpu.SemaphoreType.DMA((blocks,)),
        ],
        out_shape=[jax.ShapeDtypeStruct((block, breadth, width), video.dtype)] * blocks
        if last
        else jax.ShapeDtypeStruct((height, breadth, width), jnp.float32),
        cost_estimate=cost,
        compiler_params=pltpu.CompilerParams(vmem_limit_bytes=32 * 2**20),
    )(*operands, *parts)


def mix_kernel(rows, begin, blocks, given, pieces, aliased, tiles, *refs):
    refs = list(refs)

    def take(count):
        taken = refs[:count]
        del refs[:count]
        return taken

    steps = pl.num_programs(0)
    fars = take(blocks if given else 1)
    owns, mates = take(blocks), take(blocks)
    temporal_parts = take(1 + pieces[1])
    spatial_parts = [] if given else take(1 + pieces[0])
    spatial_bias, temporal_bias = take(2)
    take(aliased)
    (out,) = take(1)
    own, mate, far, temporal, spatial, row_sem, mate_sem, far_sem, temporal_sem, spatial_sem = refs
    breadth, width = out.shape[1:]
    depth = temporal.shape[1]
    group, core = seat()
    tile = lax.axis_index("tile")
    present = jnp.where(core == 0, tile > 0, tile < tiles - 1)
    i = pl.program_id(0)

    def part_copies(parts, weights, sem):
        held = parts[0].shape[1]
        copies = [
            pltpu.make_async_copy(parts[0], weights.at[:, pl.ds(aligned(group * held), held)], sem.at[0])
        ]
        at = 0
        for n in range(1, len(parts), 2):
            size = parts[n].shape[0]
            for p, start in enumerate(half_starts(held)):
                there = pl.ds(aligned((1 - group) * held + start), held // 2)
                copies.append(
                    pltpu.make_async_copy(parts[n + p], weights.at[pl.ds(at, size), there], sem.at[n + p])
                )
            at += size
        return copies

    def block_copies(sources, target, sem):
        return [
            pltpu.make_async_copy(source, target.at[pl.ds(p * source.shape[0], source.shape[0])], sem.at[p])
            for p, source in enumerate(sources)
        ]

    def far_copies():
        if given:
            return block_copies(fars, far, far_sem)
        low = begin - 1
        start, end = max(low, 0), min(low + far.shape[0], fars[0].shape[0])
        return [
            pltpu.make_async_copy(
                fars[0].at[pl.ds(start, end - start)], far.at[pl.ds(start - low, end - start)], far_sem.at[0]
            )
        ]

    first = part_copies(temporal_parts, temporal, temporal_sem)
    first += block_copies(owns, own, row_sem) + block_copies(mates, mate, mate_sem)
    second = far_copies() + ([] if given else part_copies(spatial_parts, spatial, spatial_sem))

    @pl.when(i == 0)
    def _():
        for copy in first + second:
            copy.start()
        if not given and begin == 0:
            far[0] = jnp.zeros(far.shape[1:], far.dtype)
        for copy in first:
            copy.wait()

    count = rows * breadth
    here = pl.ds(i * rows, rows)
    own_lines = own[here].reshape(count, depth)
    mate_lines = mate[here].reshape(count, depth)
    mate_tap, far_tap = 2 - 2 * core, 2 * core
    totals = [
        dot(own_lines, temporal[1, :, columns]) + dot(mate_lines, temporal[mate_tap, :, columns])
        for columns in halves(width)
    ]

    @pl.when(i == 0)
    def _():
        for copy in second:
            copy.wait()

    if given:
        far_lines = far[here].reshape(count, depth)
    else:
        far_lines = jnp.concatenate(
            [
                silu(
                    rows_conv(far, spatial, range(9), i * rows, rows, breadth, columns) + spatial_bias[:, columns]
                ).astype(far.dtype)
                for columns in halves(depth)
            ],
            axis=1,
        )
    far_lines = jnp.where(present, far_lines, jnp.zeros_like(far_lines))
    for total, columns in zip(totals, halves(width), strict=True):
        total += dot(far_lines, temporal[far_tap, :, columns]) + temporal_bias[:, columns]
        out[:, :, columns] = total.astype(out.dtype).reshape(rows, breadth, -1)


def mix_call(shape, owns, mates, fars, given, temporal_parts, spatial_parts, biases, before, begin, rows, tiles, cost):
    height, breadth, width = shape
    dtype = owns[0].dtype
    count = sum(own.shape[0] for own in owns)
    depth = owns[0].shape[2]
    aliased = 0 if before is None else 1
    operands = [*fars, *owns, *mates, *temporal_parts, *spatial_parts]
    whole = pl.BlockSpec((1, width), lambda i: (0, 0))
    pieces = (len(spatial_parts) - 1, len(temporal_parts) - 1)
    return pl.pallas_call(
        functools.partial(mix_kernel, rows, begin, len(owns), given, pieces, aliased, tiles),
        grid=(count // rows,),
        in_specs=[ANY] * len(operands) + [whole, whole] + [ANY] * aliased,
        out_specs=pl.BlockSpec((rows, breadth, width), lambda i: (i + begin // rows, 0, 0)),
        scratch_shapes=[
            pltpu.VMEM((count, breadth, depth), dtype),
            pltpu.VMEM((count, breadth, depth), dtype),
            pltpu.VMEM((count if given else count + 2, breadth, depth), dtype),
            pltpu.VMEM((3, depth, width), dtype),
            pltpu.VMEM((8, 128) if given else (9, depth, depth), dtype),
            pltpu.SemaphoreType.DMA((len(owns),)),
            pltpu.SemaphoreType.DMA((len(owns),)),
            pltpu.SemaphoreType.DMA((len(fars),)),
            pltpu.SemaphoreType.DMA((len(temporal_parts),)),
            pltpu.SemaphoreType.DMA((max(len(spatial_parts), 1),)),
        ],
        out_shape=jax.ShapeDtypeStruct(shape, dtype),
        input_output_aliases={len(operands) + 2: 0} if aliased else {},
        cost_estimate=cost,
        compiler_params=pltpu.CompilerParams(vmem_limit_bytes=40 * 2**20),
    )(*operands, *biases, *([before] if aliased else []))


def near_device(videos, spatial_filter, temporal_filter, spatial_bias, temporal_bias):
    shape = videos.shape[2:]
    height, breadth, channels = shape
    video = videos.reshape(shape)
    biases = [spatial_bias.reshape(1, -1), temporal_bias.reshape(1, -1)]
    tiles = lax.axis_size("tile")
    depth, width = spatial_filter.shape[1:]
    half = depth // 2
    swap = [(0, 1), (1, 0)]
    mates = [(i, i ^ 1) for i in range(tiles)]
    across = [pair for i in range(1, tiles - 1, 2) for pair in ((i, i + 1), (i + 1, i))]
    light = pl.CostEstimate(flops=1000, bytes_accessed=1000, transcendentals=0)
    heavy = pl.CostEstimate(flops=10**12, bytes_accessed=1000, transcendentals=0)

    def mine(first, count):
        return lambda: (pl.ds(first, count), pl.ds(aligned(half_starts(depth)[0]), half))

    rows = 8
    sent = height - rows + 1
    taps = [(0, 3), (3, 2), (5, 4)]
    middle = taps[2][0]
    cuts = [
        [(mine(first, count), (count, half, width)) for first, count in taps],
        [(mine(0, 3), (3, half, width))],
        [(lambda: (pl.ds(0, sent),), (sent, breadth, channels))],
    ]
    *cut, c_y, far = cut_call([spatial_filter, temporal_filter, video], cuts, light)
    far = lax.ppermute(far, "tile", across)
    fetched = [lax.ppermute(piece, "dp", swap) for piece in cut]

    def both(pieces):
        return [half for piece in pieces for half in (piece, lax.ppermute(piece, "tile", mates))]

    base = conv_call(video, None, None, [spatial_filter], depth, range(9), True, 16, rows, light)
    *early, base = lax.optimization_barrier((*fetched[:2], base))
    early = both(early)
    base = conv_call(video, base, None, early, depth, range(middle), False, 16, rows, light)
    *late, base = lax.optimization_barrier((*fetched[2:], base))
    late = both(late)
    own = conv_call(video, base, biases[0], late, depth, range(middle, 9), False, 16, rows, light)
    temporal_parts = [temporal_filter, *both([lax.ppermute(c_y, "dp", swap)])]
    spatial_parts = [spatial_filter, *early, *late]

    last = lax.ppermute(own[-1], "tile", across)
    mate = [lax.ppermute(block, "tile", mates) for block in own]
    out = mix_call(
        shape, own[:-1], mate[:-1], [far], False, temporal_parts, spatial_parts, biases, None, 0, 12, tiles, heavy
    )
    out = mix_call(
        shape, own[-1:], mate[-1:], [last], True, temporal_parts, [], biases, out, height - rows, rows, tiles, light
    )
    return out.reshape(videos.shape)


def padded_2(block, sides, width):
    for axis, dim in sides:
        count = lax.axis_size(axis)
        forward = [(i, i + 1) for i in range(count - 1)]
        backward = [(target, source) for source, target in forward]
        low = lax.ppermute(
            lax.slice_in_dim(block, block.shape[dim] - width, None, axis=dim), axis, forward
        )
        high = lax.ppermute(lax.slice_in_dim(block, 0, width, axis=dim), axis, backward)
        block = jnp.concatenate([low, block, high], axis=dim)
    return block


def spatial_term(padded, weight_piece):
    width = weight_piece.shape[1]
    height = padded.shape[2] - 2
    breadth = padded.shape[3] - 2
    columns = jnp.concatenate(
        [
            padded[:, :, row_off : row_off + height, col_off : col_off + breadth, :]
            for row_off in range(3)
            for col_off in range(3)
        ],
        axis=4,
    )
    matrix = weight_piece.reshape(9 * width, weight_piece.shape[2])
    return jnp.dot(columns.reshape(-1, 9 * width), matrix, preferred_element_type=jnp.float32)


def temporal_term(framed, weight_piece):
    width = weight_piece.shape[1]
    frames = framed.shape[1] - 2
    columns = jnp.concatenate([framed[:, lag : lag + frames] for lag in range(3)], axis=4)
    matrix = weight_piece.reshape(3 * width, weight_piece.shape[2])
    return jnp.dot(columns.reshape(-1, 3 * width), matrix, preferred_element_type=jnp.float32)


def any_device(videos, spatial_filter, temporal_filter, spatial_bias, temporal_bias):
    samples, frames, height, breadth, channels = videos.shape
    padded = jnp.pad(videos, ((0, 0), (0, 0), (1, 1), (1, 1), (0, 0)))
    summed = spatial_term(padded, lax.all_gather(spatial_filter, "dp", axis=1, tiled=True))
    activated = jax.nn.silu(summed + spatial_bias).astype(jnp.bfloat16)
    hidden = activated.reshape(samples, frames, height, breadth, channels)
    framed = padded_2(hidden, (("tile", 1),), 1)
    result = temporal_term(framed, lax.all_gather(temporal_filter, "dp", axis=1, tiled=True))
    return (result + temporal_bias).astype(jnp.bfloat16).reshape(videos.shape)


def per_device(videos, *rest):
    near = (
        videos.shape[0] == 1
        and videos.shape[1] == 1
        and videos.shape[2] % 32 == 0
        and lax.axis_size("dp") == 2
        and lax.axis_size("tile") % 2 == 0
    )
    return (near_device if near else any_device)(videos, *rest)


def solution(mesh):
    return jax.shard_map(
        per_device,
        mesh=mesh,
        in_specs=(
            P("dp", "tile", None, None, None),
            P(None, "dp", None),
            P(None, "dp", None),
            P(),
            P(),
        ),
        out_specs=P("dp", "tile", None, None, None),
        check_vma=False,
    )
```

time: 73.1 us -> 64.4 us (0.88)
  waiting for transfers between devices: 18.3 us -> 10.9 us
  local copies, waits for them, and re-layouts: 8.24 us -> 3.27 us
  Pallas kernels: 29.8 us -> 31.5 us
  starting transfers between devices: 16.2 us -> 17.9 us
    ppermute x9, waiting for transfers between devices: 18.3 us -> 10.9 us  [the longest x3 4.02 us: near_device(): fetched = [lax.ppermute(piece, 'dp', swap) for piece in cut]]
    dynamic_slice x3 -> x0, local copies, waits for them, and re-layouts: 3.64 us -> none  [the longest x1 1.86 us: near_device(): lax.dynamic_slice_in_dim(spatial_filter, starts[0], small, axis=1)]
    slice x1 -> x0, local copies, waits for them, and re-layouts: 2.91 us -> none  [near_device(): far = lax.ppermute(video[:sent], 'tile', across)]
    pallas_call x2 -> x4, Pallas kernels: 13.7 us -> 15.4 us  [the longest x3 13.5 us: conv_call(): pl.pallas_call(functools.partial(conv_kernel, rows, block, taps, held, ba...]
    unnamed x12, local copies, waits for them, and re-layouts: 1.69 us -> 3.27 us
    ppermute x9, starting transfers between devices: 12.2 us -> 13.3 us  [the longest x1 4.38 us: near_device(): far = lax.ppermute(far, 'tile', across)]
  transfers between devices with their start and end apart: 14 -> 14, of which waited for: 3 -> 5; matrix products, arithmetic and copies ran while one was open for 5% -> 0% of each run, Pallas kernels for 37% -> 41%
where the time goes in v3:
time: 64.4 us; the launch traced here: 63.7 us
  Pallas kernels  31.5 us (49%)
  starting transfers between devices  17.9 us (28%)
  waiting for transfers between devices  10.9 us (17%)
  local copies, waits for them, and re-layouts  3.27 us (5%)
    pallas_call x2, Pallas kernels, mix_call(): pl.pallas_call(functools.partial(mix_kernel, rows, begin, len(owns), give...  16 us
    pallas_call x3, Pallas kernels, conv_call(): pl.pallas_call(functools.partial(conv_kernel, rows, block, taps, held, ba...  13.5 us
    ppermute x1, starting transfers between devices, near_device(): far = lax.ppermute(far, 'tile', across)  4.38 us
    ppermute x3, waiting for transfers between devices, near_device(): fetched = [lax.ppermute(piece, 'dp', swap) for piece in cut]  4.02 us
    ppermute x4, starting transfers between devices, both(): lax.ppermute(piece, 'tile', mates)  3.93 us
    ppermute x1, waiting for transfers between devices, near_device(): temporal_parts = [temporal_filter, *both([lax.ppermute(c_y, 'dp', swap)])]  3.74 us
    ppermute x1, starting transfers between devices, near_device(): last = lax.ppermute(own[-1], 'tile', across)  3.59 us
    ppermute x3, starting transfers between devices, near_device(): fetched = [lax.ppermute(piece, 'dp', swap) for piece in cut]  3.52 us
  transfers between devices with their start and end apart: 14, of which 5 were waited for; matrix products, arithmetic and copies ran while one was open for 0% of the time, Pallas kernels for 41%

profile of v3, /device:TPU:1, one launch (start us, length us, event | category | flops | bytes accessed | tf_op | source)
XLA Modules:
  0.0 63.7 jit_solution(6719997494229277357)
XLA Ops:
  0.0 2.0 %shard_map.55 = (bf16[3,128,512]{2,1,0:T(8,128)(2,1)S(1)}, bf16[2,128,512]{2,1,0:T(8,128)(2,1)S(1)}, bf16[4,128,512]{2,1,0:T(8,128)(2,1)S(1)}, bf16[3,128,512]{2,1,0:T(8,128)(2,1)S(1)}, bf16[25,64,512]{2,1,0:T(8,128)(2,1)S(1)}) custom-call(bf16[9,256,512]{2,1,0:T(8,128)(2,1)} %refs_10_.1, bf16[3,256,512]{2,1,0:T(8,128)(2,1)} %refs_3_.1, ...), custom_call_target="tpu_custom_call" | custom-call | flops 1000 | bytes 1000 | tf_op jit(solution)/shard_map/pallas_call | solution.py:75
  2.0 2.1 %collective-permute-start.1 = (bf16[3,128,512]{2,1,0:T(8,128)(2,1)S(1)}, bf16[3,128,512]{2,1,0:T(8,128)(2,1)S(1)}, u32[]{:S(2)}, u32[]{:S(2)}) collective-permute-start(bf16[3,128,512]{2,1,0:T(8,128)(2,1)S(1)} %get-tuple-element.20), channel_id=1, source_target_pairs={{0,16},{16,0},{1,17},{17,1},{2,18},{18,2},{3,19},{19,3},{4,20},{20... | collective-permute-start | bytes 1179656 | tf_op jit(solution)/shard_map/ppermute | solution.py:360
  4.1 0.1 collective-permute-start.2
  4.2 4.4 %collective-permute-start.10 = (bf16[25,64,512]{2,1,0:T(8,128)(2,1)S(1)}, bf16[25,64,512]{2,1,0:T(8,128)(2,1)S(1)}, u32[]{:S(2)}, u32[]{:S(2)}) collective-permute-start(bf16[25,64,512]{2,1,0:T(8,128)(2,1)S(1)} %get-tuple-element.29), channel_id=1, source_target_pairs={{1,2},{2,1},{3,4},{4,3},{5,6},{6,5},{7,8},{8,7},{9,10},{10,9},{11,... | collective-permute-start | bytes 4915208 | tf_op jit(solution)/shard_map/ppermute | solution.py:359
  8.6 1.3 %collective-permute-start = (bf16[4,128,512]{2,1,0:T(8,128)(2,1)S(1)}, bf16[4,128,512]{2,1,0:T(8,128)(2,1)S(1)}, u32[]{:S(2)}, u32[]{:S(2)}) collective-permute-start(bf16[4,128,512]{2,1,0:T(8,128)(2,1)S(1)} %get-tuple-element.19), channel_id=1, source_target_pairs={{0,16},{16,0},{1,17},{17,1},{2,18},{18,2},{3,19},{19,3},{4,20},{20... | collective-permute-start | bytes 1572872 | tf_op jit(solution)/shard_map/ppermute | solution.py:360
  9.9 0.0 copy-start
  9.9 1.6 %copy-done = bf16[1,1,32,64,512]{4,3,2,1,0:T(8,128)(2,1)S(1)} copy-done((bf16[1,1,32,64,512]{4,3,2,1,0:T(8,128)(2,1)S(1)}, bf16[1,1,32,64,512]{4,3,2,1,0:T(8,128)(2,1)}, u32[]{:S(2)}) %copy-start) | copy-done | bytes 2097176
  11.5 0.0 copy-start.1
  11.5 1.7 %copy-done.1 = bf16[9,256,512]{2,1,0:T(8,128)(2,1)S(1)} copy-done((bf16[9,256,512]{2,1,0:T(8,128)(2,1)S(1)}, bf16[9,256,512]{2,1,0:T(8,128)(2,1)}, u32[]{:S(2)}) %copy-start.1) | copy-done | bytes 2359320
  13.1 5.5 %shard_map.56.refs_0_ = f32[32,64,512]{2,1,0:T(8,128)S(1)} custom-call(bf16[32,64,512]{2,1,0:T(8,128)(2,1)S(1)} %bitcast.5, bf16[9,256,512]{2,1,0:T(8,128)(2,1)S(1)} %copy-done.1), custom_call_target="tpu_custom_call" | custom-call | flops 1000 | bytes 1000 | tf_op jit(solution)/shard_map/pallas_call | solution.py:175
  18.7 0.0 copy-start.4
  18.7 0.0 collective-permute-done.2.refs_3_.refs_13_
  18.7 0.0 collective-permute-done.1.refs_1_.refs_11_
  18.7 1.9 %collective-permute-start.3 = (bf16[3,128,512]{2,1,0:T(8,128)(2,1)S(1)}, bf16[3,128,512]{2,1,0:T(8,128)(2,1)S(1)}, u32[]{:S(2)}, u32[]{:S(2)}) collective-permute-start(bf16[3,128,512]{2,1,0:T(8,128)(2,1)S(1)} %collective-permute-done.1.refs_1_.refs_11_), channel_id=1, source_target_pairs={{0,1},{1,0},{2,3},{3,2},{4,5},{5,4},{6,7},{7,6},{8,9},{9,8},{10,11... | collective-permute-start | bytes 1179656 | tf_op jit(solution)/shard_map/ppermute | solution.py:363
  20.6 0.0 collective-permute-start.4
  20.6 1.7 %collective-permute-done.4.refs_4_.refs_14_ = bf16[2,128,512]{2,1,0:T(8,128)(2,1)S(1)} collective-permute-done((bf16[2,128,512]{2,1,0:T(8,128)(2,1)S(1)}, bf16[2,128,512]{2,1,0:T(8,128)(2,1)S(1)}, u32[]{:S(2)}, u32[]{:S(2)}) %collective-permute-start.4) | collective-permute-done | bytes 262176 | tf_op jit(solution)/shard_map/ppermute | solution.py:363
  22.3 0.0 collective-permute-done.3.refs_2_.refs_12_
  22.4 3.4 %shard_map.57.refs_0_ = f32[32,64,512]{2,1,0:T(8,128)S(1)} custom-call(bf16[32,64,512]{2,1,0:T(8,128)(2,1)S(1)} %bitcast.6, f32[32,64,512]{2,1,0:T(8,128)S(1)} %shard_map.56.refs_0_, bf16[3,128,512]{2,1,0:T(8,128)(2,1)S(1)} %collective-permute-done.1.refs_1_.refs_11_, bf16[3,128,512]{2,1,0:T(8,128)(2,1)S(1)} %collective-permute-done.3.refs_2_.refs_12_, ...), custom_call_target="tpu_custom_call" | custom-call | flops 1000 | bytes 1000 | tf_op jit(solution)/shard_map/pallas_call | solution.py:175
  25.8 4.0 %collective-permute-done.refs_2_.refs_15_ = bf16[4,128,512]{2,1,0:T(8,128)(2,1)S(1)} collective-permute-done((bf16[4,128,512]{2,1,0:T(8,128)(2,1)S(1)}, bf16[4,128,512]{2,1,0:T(8,128)(2,1)S(1)}, u32[]{:S(2)}, u32[]{:S(2)}) %collective-permute-start) | collective-permute-done | bytes 524320 | tf_op jit(solution)/shard_map/ppermute | solution.py:360
  29.8 1.2 %collective-permute-start.5 = (bf16[4,128,512]{2,1,0:T(8,128)(2,1)S(1)}, bf16[4,128,512]{2,1,0:T(8,128)(2,1)S(1)}, u32[]{:S(2)}, u32[]{:S(2)}) collective-permute-start(bf16[4,128,512]{2,1,0:T(8,128)(2,1)S(1)} %collective-permute-done.refs_2_.refs_15_), channel_id=1, source_target_pairs={{0,1},{1,0},{2,3},{3,2},{4,5},{5,4},{6,7},{7,6},{8,9},{9,8},{10,11... | collective-permute-start | bytes 1572872 | tf_op jit(solution)/shard_map/ppermute | solution.py:363
  31.0 1.5 %collective-permute-start.8 = (bf16[3,128,512]{2,1,0:T(8,128)(2,1)S(1)}, bf16[3,128,512]{2,1,0:T(8,128)(2,1)S(1)}, u32[]{:S(2)}, u32[]{:S(2)}) collective-permute-start(bf16[3,128,512]{2,1,0:T(8,128)(2,1)S(1)} %get-tuple-element.28), channel_id=1, source_target_pairs={{0,16},{16,0},{1,17},{17,1},{2,18},{18,2},{3,19},{19,3},{4,20},{20... | collective-permute-start | bytes 1179656 | tf_op jit(solution)/shard_map/ppermute | solution.py:372
  32.5 0.1 collective-permute-done.5.refs_3_.refs_16_
  32.6 0.0 copy-done.4
  32.6 0.0 copy-start.2
  32.6 0.0 copy-start.3
  32.6 0.0 copy-start.5
  32.6 4.5 %shard_map.58 = (bf16[8,64,512]{2,1,0:T(8,128)(2,1)S(1)}, bf16[8,64,512]{2,1,0:T(8,128)(2,1)S(1)}, bf16[8,64,512]{2,1,0:T(8,128)(2,1)S(1)}, bf16[8,64,512]{2,1,0:T(8,128)(2,1)}) custom-call(bf16[32,64,512]{2,1,0:T(8,128)(2,1)S(1)} %bitcast.7, f32[32,64,512]{2,1,0:T(8,128)S(1)} %shard_map.57.refs_0_, f32[1,512]{1,0:T(1,128)S(1)} %bitcast.8, ...), custom_call_target="tpu_custom_call" | custom-call | flops 1000 | bytes 1000 | tf_op jit(solution)/shard_map/pallas_call | solution.py:175
  37.1 0.4 collective-permute-start.11
  37.5 0.1 collective-permute-start.12
  37.7 0.4 collective-permute-start.13
  38.0 3.7 %collective-permute-done.8.refs_8_.refs_4_ = bf16[3,128,512]{2,1,0:T(8,128)(2,1)S(1)} collective-permute-done((bf16[3,128,512]{2,1,0:T(8,128)(2,1)S(1)}, bf16[3,128,512]{2,1,0:T(8,128)(2,1)S(1)}, u32[]{:S(2)}, u32[]{:S(2)}) %collective-permute-start.8) | collective-permute-done | bytes 393248 | tf_op jit(solution)/shard_map/ppermute | solution.py:372
  41.8 0.8 %collective-permute-start.9 = (bf16[3,128,512]{2,1,0:T(8,128)(2,1)S(1)}, bf16[3,128,512]{2,1,0:T(8,128)(2,1)S(1)}, u32[]{:S(2)}, u32[]{:S(2)}) collective-permute-start(bf16[3,128,512]{2,1,0:T(8,128)(2,1)S(1)} %collective-permute-done.8.refs_8_.refs_4_), channel_id=1, source_target_pairs={{0,1},{1,0},{2,3},{3,2},{4,5},{5,4},{6,7},{7,6},{8,9},{9,8},{10,11... | collective-permute-start | bytes 1179656 | tf_op jit(solution)/shard_map/ppermute | solution.py:363
  42.6 1.3 %collective-permute-done.9.refs_9_.refs_5_ = bf16[3,128,512]{2,1,0:T(8,128)(2,1)S(1)} collective-permute-done((bf16[3,128,512]{2,1,0:T(8,128)(2,1)S(1)}, bf16[3,128,512]{2,1,0:T(8,128)(2,1)S(1)}, u32[]{:S(2)}, u32[]{:S(2)}) %collective-permute-start.9) | collective-permute-done | bytes 393248 | tf_op jit(solution)/shard_map/ppermute | solution.py:363
  43.9 3.6 %collective-permute-start.6 = (bf16[8,64,512]{2,1,0:T(8,128)(2,1)}, bf16[8,64,512]{2,1,0:T(8,128)(2,1)}, u32[]{:S(2)}, u32[]{:S(2)}) collective-permute-start(bf16[8,64,512]{2,1,0:T(8,128)(2,1)} %get-tuple-element.27.refs_1_), channel_id=1, source_target_pairs={{1,2},{2,1},{3,4},{4,3},{5,6},{6,5},{7,8},{8,7},{9,10},{10,9},{11,... | collective-permute-start | bytes 1572872 | tf_op jit(solution)/shard_map/ppermute | solution.py:375
  47.5 0.0 collective-permute-done.10.refs_0_
  47.5 0.1 collective-permute-start.7
  47.6 0.0 collective-permute-done.11.refs_4_
  47.6 0.0 collective-permute-done.12.refs_5_
  47.6 0.0 collective-permute-done.13.refs_6_
  47.6 0.0 copy-done.2
  47.6 0.0 copy-done.3
  47.6 0.0 copy-done.5
  47.7 12.7 %shard_map.59.refs_8_ = bf16[32,64,512]{2,1,0:T(8,128)(2,1)} custom-call(bf16[25,64,512]{2,1,0:T(8,128)(2,1)S(1)} %collective-permute-done.10.refs_0_, bf16[8,64,512]{2,1,0:T(8,128)(2,1)S(1)} %get-tuple-element.30.refs_1_, bf16[8,64,512]{2,1,0:T(8,128)(2,1)S(1)} %get-tuple-element.31.refs_2_, bf16[8,64,512]{2,1,0:T(8,128)(2,1)S(1)} %get-tuple-element.32.refs_3_, ...), custom_call_target="tpu_custom_call" | custom-call | flops 999999995904 | bytes 1000 | tf_op jit(solution)/shard_map/pallas_call | solution.py:308
  60.3 0.0 collective-permute-done.6.refs_0_
  60.4 0.0 collective-permute-done.7.refs_2_
  60.4 3.4 %shard_map.60 = bf16[32,64,512]{2,1,0:T(8,128)(2,1)} custom-call(bf16[8,64,512]{2,1,0:T(8,128)(2,1)} %collective-permute-done.6.refs_0_, bf16[8,64,512]{2,1,0:T(8,128)(2,1)} %get-tuple-element.27.refs_1_, bf16[8,64,512]{2,1,0:T(8,128)(2,1)} %collective-permute-done.7.refs_2_, bf16[3,256,512]{2,1,0:T(8,128)(2,1)S(1)} %copy-done.3, ...), custom_call_target="tpu_custom_call", output_to_operand_aliasing={{}: (8, {})} | custom-call | flops 1000 | bytes 1000 | tf_op jit(solution)/shard_map/pallas_call | solution.py:308
Async XLA Ops:
  2.0 16.7 %collective-permute-start.1 = (bf16[3,128,512]{2,1,0:T(8,128)(2,1)S(1)}, bf16[3,128,512]{2,1,0:T(8,128)(2,1)S(1)}, u32[]{:S(2)}, u32[]{:S(2)}) collective-permute-start(bf16[3,128,512]{2,1,0:T(8,128)(2,1)S(1)} %get-tuple-element.20), channel_id=1, source_target_pairs={{0,16},{16,0},{1,17},{17,1},{2,18},{18,2},{3,19},{19,3},{4,20},{20... | collective-permute-start | bytes 1179656 | tf_op jit(solution)/shard_map/ppermute | solution.py:360
  4.1 14.6 %collective-permute-start.2 = (bf16[2,128,512]{2,1,0:T(8,128)(2,1)S(1)}, bf16[2,128,512]{2,1,0:T(8,128)(2,1)S(1)}, u32[]{:S(2)}, u32[]{:S(2)}) collective-permute-start(bf16[2,128,512]{2,1,0:T(8,128)(2,1)S(1)} %get-tuple-element.21), channel_id=1, source_target_pairs={{0,16},{16,0},{1,17},{17,1},{2,18},{18,2},{3,19},{19,3},{4,20},{20... | collective-permute-start | bytes 786440 | tf_op jit(solution)/shard_map/ppermute | solution.py:360
  4.2 43.3 %collective-permute-start.10 = (bf16[25,64,512]{2,1,0:T(8,128)(2,1)S(1)}, bf16[25,64,512]{2,1,0:T(8,128)(2,1)S(1)}, u32[]{:S(2)}, u32[]{:S(2)}) collective-permute-start(bf16[25,64,512]{2,1,0:T(8,128)(2,1)S(1)} %get-tuple-element.29), channel_id=1, source_target_pairs={{1,2},{2,1},{3,4},{4,3},{5,6},{6,5},{7,8},{8,7},{9,10},{10,9},{11,... | collective-permute-start | bytes 4915208 | tf_op jit(solution)/shard_map/ppermute | solution.py:359
  8.6 21.2 %collective-permute-start = (bf16[4,128,512]{2,1,0:T(8,128)(2,1)S(1)}, bf16[4,128,512]{2,1,0:T(8,128)(2,1)S(1)}, u32[]{:S(2)}, u32[]{:S(2)}) collective-permute-start(bf16[4,128,512]{2,1,0:T(8,128)(2,1)S(1)} %get-tuple-element.19), channel_id=1, source_target_pairs={{0,16},{16,0},{1,17},{17,1},{2,18},{18,2},{3,19},{19,3},{4,20},{20... | collective-permute-start | bytes 1572872 | tf_op jit(solution)/shard_map/ppermute | solution.py:360
  9.9 1.6 %copy-start = (bf16[1,1,32,64,512]{4,3,2,1,0:T(8,128)(2,1)S(1)}, bf16[1,1,32,64,512]{4,3,2,1,0:T(8,128)(2,1)}, u32[]{:S(2)}) copy-start(bf16[1,1,32,64,512]{4,3,2,1,0:T(8,128)(2,1)} %param.5) | copy-start | bytes 6291460
  11.5 1.7 %copy-start.1 = (bf16[9,256,512]{2,1,0:T(8,128)(2,1)S(1)}, bf16[9,256,512]{2,1,0:T(8,128)(2,1)}, u32[]{:S(2)}) copy-start(bf16[9,256,512]{2,1,0:T(8,128)(2,1)} %refs_10_.1) | copy-start | bytes 7077892
  18.7 13.9 %copy-start.4 = (f32[512]{0:T(512)S(1)}, f32[512]{0:T(512)}, u32[]{:S(2)}) copy-start(f32[512]{0:T(512)} %param.8) | copy-start | bytes 6148
  18.7 3.6 %collective-permute-start.3 = (bf16[3,128,512]{2,1,0:T(8,128)(2,1)S(1)}, bf16[3,128,512]{2,1,0:T(8,128)(2,1)S(1)}, u32[]{:S(2)}, u32[]{:S(2)}) collective-permute-start(bf16[3,128,512]{2,1,0:T(8,128)(2,1)S(1)} %collective-permute-done.1.refs_1_.refs_11_), channel_id=1, source_target_pairs={{0,1},{1,0},{2,3},{3,2},{4,5},{5,4},{6,7},{7,6},{8,9},{9,8},{10,11... | collective-permute-start | bytes 1179656 | tf_op jit(solution)/shard_map/ppermute | solution.py:363
  20.6 1.7 %collective-permute-start.4 = (bf16[2,128,512]{2,1,0:T(8,128)(2,1)S(1)}, bf16[2,128,512]{2,1,0:T(8,128)(2,1)S(1)}, u32[]{:S(2)}, u32[]{:S(2)}) collective-permute-start(bf16[2,128,512]{2,1,0:T(8,128)(2,1)S(1)} %collective-permute-done.2.refs_3_.refs_13_), channel_id=1, source_target_pairs={{0,1},{1,0},{2,3},{3,2},{4,5},{5,4},{6,7},{7,6},{8,9},{9,8},{10,11... | collective-permute-start | bytes 786440 | tf_op jit(solution)/shard_map/ppermute | solution.py:363
  29.8 2.8 %collective-permute-start.5 = (bf16[4,128,512]{2,1,0:T(8,128)(2,1)S(1)}, bf16[4,128,512]{2,1,0:T(8,128)(2,1)S(1)}, u32[]{:S(2)}, u32[]{:S(2)}) collective-permute-start(bf16[4,128,512]{2,1,0:T(8,128)(2,1)S(1)} %collective-permute-done.refs_2_.refs_15_), channel_id=1, source_target_pairs={{0,1},{1,0},{2,3},{3,2},{4,5},{5,4},{6,7},{7,6},{8,9},{9,8},{10,11... | collective-permute-start | bytes 1572872 | tf_op jit(solution)/shard_map/ppermute | solution.py:363
  31.0 10.7 %collective-permute-start.8 = (bf16[3,128,512]{2,1,0:T(8,128)(2,1)S(1)}, bf16[3,128,512]{2,1,0:T(8,128)(2,1)S(1)}, u32[]{:S(2)}, u32[]{:S(2)}) collective-permute-start(bf16[3,128,512]{2,1,0:T(8,128)(2,1)S(1)} %get-tuple-element.28), channel_id=1, source_target_pairs={{0,16},{16,0},{1,17},{17,1},{2,18},{18,2},{3,19},{19,3},{4,20},{20... | collective-permute-start | bytes 1179656 | tf_op jit(solution)/shard_map/ppermute | solution.py:372
  32.6 15.1 %copy-start.2 = (bf16[9,256,512]{2,1,0:T(8,128)(2,1)S(1)}, bf16[9,256,512]{2,1,0:T(8,128)(2,1)}, u32[]{:S(2)}) copy-start(bf16[9,256,512]{2,1,0:T(8,128)(2,1)} %refs_10_.1) | copy-start | bytes 7077892
  32.6 15.1 %copy-start.3 = (bf16[3,256,512]{2,1,0:T(8,128)(2,1)S(1)}, bf16[3,256,512]{2,1,0:T(8,128)(2,1)}, u32[]{:S(2)}) copy-start(bf16[3,256,512]{2,1,0:T(8,128)(2,1)} %refs_3_.1) | copy-start | bytes 2359300
  32.6 15.1 %copy-start.5 = (f32[512]{0:T(512)S(1)}, f32[512]{0:T(512)}, u32[]{:S(2)}) copy-start(f32[512]{0:T(512)} %param.9) | copy-start | bytes 6148
  37.1 10.5 %collective-permute-start.11 = (bf16[8,64,512]{2,1,0:T(8,128)(2,1)S(1)}, bf16[8,64,512]{2,1,0:T(8,128)(2,1)S(1)}, u32[]{:S(2)}, u32[]{:S(2)}) collective-permute-start(bf16[8,64,512]{2,1,0:T(8,128)(2,1)S(1)} %get-tuple-element.30.refs_1_), channel_id=1, source_target_pairs={{0,1},{1,0},{2,3},{3,2},{4,5},{5,4},{6,7},{7,6},{8,9},{9,8},{10,11... | collective-permute-start | bytes 1572872 | tf_op jit(solution)/shard_map/ppermute | solution.py:376
  37.5 10.1 %collective-permute-start.12 = (bf16[8,64,512]{2,1,0:T(8,128)(2,1)S(1)}, bf16[8,64,512]{2,1,0:T(8,128)(2,1)S(1)}, u32[]{:S(2)}, u32[]{:S(2)}) collective-permute-start(bf16[8,64,512]{2,1,0:T(8,128)(2,1)S(1)} %get-tuple-element.31.refs_2_), channel_id=1, source_target_pairs={{0,1},{1,0},{2,3},{3,2},{4,5},{5,4},{6,7},{7,6},{8,9},{9,8},{10,11... | collective-permute-start | bytes 1572872 | tf_op jit(solution)/shard_map/ppermute | solution.py:376
  37.7 10.0 %collective-permute-start.13 = (bf16[8,64,512]{2,1,0:T(8,128)(2,1)S(1)}, bf16[8,64,512]{2,1,0:T(8,128)(2,1)S(1)}, u32[]{:S(2)}, u32[]{:S(2)}) collective-permute-start(bf16[8,64,512]{2,1,0:T(8,128)(2,1)S(1)} %get-tuple-element.32.refs_3_), channel_id=1, source_target_pairs={{0,1},{1,0},{2,3},{3,2},{4,5},{5,4},{6,7},{7,6},{8,9},{9,8},{10,11... | collective-permute-start | bytes 1572872 | tf_op jit(solution)/shard_map/ppermute | solution.py:376
  41.8 2.1 %collective-permute-start.9 = (bf16[3,128,512]{2,1,0:T(8,128)(2,1)S(1)}, bf16[3,128,512]{2,1,0:T(8,128)(2,1)S(1)}, u32[]{:S(2)}, u32[]{:S(2)}) collective-permute-start(bf16[3,128,512]{2,1,0:T(8,128)(2,1)S(1)} %collective-permute-done.8.refs_8_.refs_4_), channel_id=1, source_target_pairs={{0,1},{1,0},{2,3},{3,2},{4,5},{5,4},{6,7},{7,6},{8,9},{9,8},{10,11... | collective-permute-start | bytes 1179656 | tf_op jit(solution)/shard_map/ppermute | solution.py:363
  43.9 16.4 %collective-permute-start.6 = (bf16[8,64,512]{2,1,0:T(8,128)(2,1)}, bf16[8,64,512]{2,1,0:T(8,128)(2,1)}, u32[]{:S(2)}, u32[]{:S(2)}) collective-permute-start(bf16[8,64,512]{2,1,0:T(8,128)(2,1)} %get-tuple-element.27.refs_1_), channel_id=1, source_target_pairs={{1,2},{2,1},{3,4},{4,3},{5,6},{6,5},{7,8},{8,7},{9,10},{10,9},{11,... | collective-permute-start | bytes 1572872 | tf_op jit(solution)/shard_map/ppermute | solution.py:375
  47.5 12.8 %collective-permute-start.7 = (bf16[8,64,512]{2,1,0:T(8,128)(2,1)}, bf16[8,64,512]{2,1,0:T(8,128)(2,1)}, u32[]{:S(2)}, u32[]{:S(2)}) collective-permute-start(bf16[8,64,512]{2,1,0:T(8,128)(2,1)} %get-tuple-element.27.refs_1_), channel_id=1, source_target_pairs={{0,1},{1,0},{2,3},{3,2},{4,5},{5,4},{6,7},{7,6},{8,9},{9,8},{10,11... | collective-permute-start | bytes 1572872 | tf_op jit(solution)/shard_map/ppermute | solution.py:376

commit v4 on v3

--- a/solution.py
+++ b/solution.py
@@ -30,6 +30,11 @@
 def half_starts(depth):
     _, core = seat()
     return [core * (depth // 2), (1 - core) * (depth // 2)]
+
+
+def relay_starts(size):
+    pair = lax.rem(lax.axis_index("tile") // 4, 2)
+    return [pair * size, (1 - pair) * size]
 
 
 def aligned(start):
@@ -82,16 +87,16 @@
     )(*sources)
 
 
-def conv_kernel(rows, block, taps, held, has_base, last, video, *refs):
+def conv_kernel(rows, blocks, taps, held, has_base, last, video, *refs):
     refs = list(refs)
     base = refs.pop(0) if has_base else None
     bias = refs.pop(0) if last else None
+    tail = refs.pop(0) if last else None
     pieces = 1 if held else 2
     height, breadth = video.shape[:2]
     steps = height // rows
     padded, weights, hidden, video_sem, part_sem, out_sem = refs[-6:]
-    blocks = height // block
-    outs = refs[-6 - (blocks if last else 1) : -6]
+    outs = refs[-6 - len(blocks) : -6] if last else refs[-7:-6]
     parts = refs[: -6 - len(outs)]
     depth = weights.shape[1]
     i = pl.program_id(0)
@@ -108,21 +113,30 @@
 
     def part_copies():
         copies = []
-        at = 0
-        for n in range(0, len(parts), pieces):
-            size = parts[n].shape[0]
+        sizes = [part.shape[0] for part in parts[::pieces]]
+        begins = relay_starts(sizes[0]) if last else [sum(sizes[:n]) for n in range(len(sizes))]
+        for n, (size, begin) in enumerate(zip(sizes, begins, strict=True)):
             for p, start in enumerate(starts):
-                there = weights.at[pl.ds(at, size), pl.ds(aligned(start), parts[n + p].shape[1])]
-                copies.append(pltpu.make_async_copy(parts[n + p], there, part_sem.at[n + p]))
-            at += size
+                part = parts[n * pieces + p]
+                there = weights.at[pl.ds(begin, size), pl.ds(aligned(start), part.shape[1])]
+                copies.append(pltpu.make_async_copy(part, there, part_sem.at[n * pieces + p]))
         return copies
 
     def out_copy(j):
-        return pltpu.make_async_copy(hidden.at[pl.ds(j * block, block)], outs[j], out_sem.at[j])
+        there = outs[j].at[pl.ds(0, blocks[j])]
+        return pltpu.make_async_copy(hidden.at[pl.ds(sum(blocks[:j]), blocks[j])], there, out_sem.at[j])
+
+    if last:
+        lines = tail.shape[0]
+        tail_in = pltpu.make_async_copy(tail, hidden.at[pl.ds(height, lines)], out_sem.at[len(blocks)])
+        there = outs[-2].at[pl.ds(blocks[-2], lines)]
+        tail_out = pltpu.make_async_copy(hidden.at[pl.ds(height, lines)], there, out_sem.at[len(blocks)])
 
     @pl.when(i == 0)
     def _():
         video_copy(0).start()
+        if last:
+            tail_in.start()
         for copy in part_copies():
             copy.start()
         for j in range(1, steps):
@@ -148,44 +162,53 @@
             outs[0][:, :, columns] = total.reshape(rows, breadth, -1)
 
     if last:
-        for j in range(blocks):
-
-            @pl.when(i == ((j + 1) * block - 1) // rows)
+        for j in range(len(blocks)):
+
+            @pl.when(i == (sum(blocks[: j + 1]) - 1) // rows)
             def _():
                 out_copy(j).start()
 
+        @pl.when(i == 0)
+        def _():
+            tail_in.wait()
+            tail_out.start()
+
         @pl.when(i == steps - 1)
         def _():
-            for j in range(blocks):
+            tail_out.wait()
+            for j in range(len(blocks)):
                 out_copy(j).wait()
 
 
-def conv_call(video, base, bias, parts, depth, taps, held, rows, block, cost):
+def conv_call(video, base, bias, tail, parts, depth, taps, held, rows, blocks, cost):
     height, breadth, _ = video.shape
     width = parts[0].shape[2]
     steps = height // rows
     last = bias is not None
-    blocks = height // block
     lines = pl.BlockSpec((rows, breadth, width), lambda i: (i, 0, 0))
     specs, operands = [ANY], [video]
     if base is not None:
         specs, operands = specs + [lines], operands + [base]
     if last:
-        specs, operands = specs + [pl.BlockSpec((1, width), lambda i: (0, 0))], operands + [bias]
+        specs, operands = specs + [pl.BlockSpec((1, width), lambda i: (0, 0)), ANY], operands + [bias, tail]
+        extra = [0] * (len(blocks) - 2) + [tail.shape[0], 0]
     return pl.pallas_call(
-        functools.partial(conv_kernel, rows, block, taps, held, base is not None, last),
+        functools.partial(conv_kernel, rows, blocks, taps, held, base is not None, last),
         grid=(steps,),
         in_specs=specs + [ANY] * len(parts),
-        out_specs=[ANY] * blocks if last else lines,
+        out_specs=[ANY] * len(blocks) if last else lines,
         scratch_shapes=[
             pltpu.VMEM((height + 2, breadth, depth), video.dtype),
             pltpu.VMEM((len(taps), depth, width), video.dtype),
-            pltpu.VMEM((height, breadth, width) if last else (8, 128), video.dtype),
+            pltpu.VMEM((height + tail.shape[0], breadth, width) if last else (16, 128), video.dtype),
             pltpu.SemaphoreType.DMA((steps,)),
             pltpu.SemaphoreType.DMA((len(parts),)),
-            pltpu.SemaphoreType.DMA((blocks,)),
+            pltpu.SemaphoreType.DMA((len(blocks) + 1,)),
         ],
-        out_shape=[jax.ShapeDtypeStruct((block, breadth, width), video.dtype)] * blocks
+        out_shape=[
+            jax.ShapeDtypeStruct((block + more, breadth, width), video.dtype)
+            for block, more in zip(blocks, extra, strict=True)
+        ]
         if last
         else jax.ShapeDtypeStruct((height, breadth, width), jnp.float32),
         cost_estimate=cost,
@@ -193,7 +216,7 @@
     )(*operands, *parts)
 
 
-def mix_kernel(rows, begin, blocks, given, pieces, aliased, tiles, *refs):
+def mix_kernel(rows, begin, sizes, given, parts, tiles, *refs):
     refs = list(refs)
 
     def take(count):
@@ -201,15 +224,16 @@
         del refs[:count]
         return taken
 
-    steps = pl.num_programs(0)
-    fars = take(blocks if given else 1)
+    blocks = len(sizes)
     owns, mates = take(blocks), take(blocks)
-    temporal_parts = take(1 + pieces[1])
-    spatial_parts = [] if given else take(1 + pieces[0])
+    (far_part,) = take(1)
+    temporal_parts = take(1 if given else 2)
+    spatial_parts = take(parts)
     spatial_bias, temporal_bias = take(2)
-    take(aliased)
+    take(1 if given else 0)
     (out,) = take(1)
-    own, mate, far, temporal, spatial, row_sem, mate_sem, far_sem, temporal_sem, spatial_sem = refs
+    (temporal,) = temporal_parts if given else take(1)
+    own, mate, far, spatial, row_sem, mate_sem, far_sem, spatial_sem = refs
     breadth, width = out.shape[1:]
     depth = temporal.shape[1]
     group, core = seat()
@@ -217,60 +241,76 @@
     present = jnp.where(core == 0, tile > 0, tile < tiles - 1)
     i = pl.program_id(0)
 
-    def part_copies(parts, weights, sem):
-        held = parts[0].shape[1]
-        copies = [
-            pltpu.make_async_copy(parts[0], weights.at[:, pl.ds(aligned(group * held), held)], sem.at[0])
-        ]
-        at = 0
-        for n in range(1, len(parts), 2):
-            size = parts[n].shape[0]
+    def spatial_copies():
+        held = spatial_parts[0].shape[1]
+        there = spatial.at[:, pl.ds(aligned(group * held), held)]
+        copies = [pltpu.make_async_copy(spatial_parts[0], there, spatial_sem.at[0])]
+        counts = [part.shape[0] for part in spatial_parts[1::2]]
+        begins = [sum(counts[:n]) for n in range(len(counts))]
+        begins[-2:] = [begins[-2] + start for start in relay_starts(counts[-1])]
+        for n, (count, first) in enumerate(zip(counts, begins, strict=True)):
             for p, start in enumerate(half_starts(held)):
-                there = pl.ds(aligned((1 - group) * held + start), held // 2)
-                copies.append(
-                    pltpu.make_async_copy(parts[n + p], weights.at[pl.ds(at, size), there], sem.at[n + p])
-                )
-            at += size
+                at = 2 * n + p + 1
+                there = spatial.at[pl.ds(first, count), pl.ds(aligned((1 - group) * held + start), held // 2)]
+                copies.append(pltpu.make_async_copy(spatial_parts[at], there, spatial_sem.at[at]))
         return copies
 
     def block_copies(sources, target, sem):
         return [
-            pltpu.make_async_copy(source, target.at[pl.ds(p * source.shape[0], source.shape[0])], sem.at[p])
-            for p, source in enumerate(sources)
+            pltpu.make_async_copy(
+                source.at[pl.ds(0, size)], target.at[pl.ds(sum(sizes[:p]), size)], sem.at[p]
+            )
+            for p, (source, size) in enumerate(zip(sources, sizes, strict=True))
         ]
 
-    def far_copies():
-        if given:
-            return block_copies(fars, far, far_sem)
-        low = begin - 1
-        start, end = max(low, 0), min(low + far.shape[0], fars[0].shape[0])
-        return [
-            pltpu.make_async_copy(
-                fars[0].at[pl.ds(start, end - start)], far.at[pl.ds(start - low, end - start)], far_sem.at[0]
-            )
-        ]
-
-    first = part_copies(temporal_parts, temporal, temporal_sem)
-    first += block_copies(owns, own, row_sem) + block_copies(mates, mate, mate_sem)
-    second = far_copies() + ([] if given else part_copies(spatial_parts, spatial, spatial_sem))
+    first = []
+    if given:
+        first = block_copies(owns, own, row_sem) + block_copies(mates, mate, mate_sem)
+        second = [pltpu.make_async_copy(far_part, far, far_sem)]
+    else:
+        second = [pltpu.make_async_copy(far_part, far.at[pl.ds(1, far_part.shape[0])], far_sem)]
+        second += spatial_copies()
 
     @pl.when(i == 0)
     def _():
         for copy in first + second:
             copy.start()
-        if not given and begin == 0:
+        if not given:
             far[0] = jnp.zeros(far.shape[1:], far.dtype)
         for copy in first:
             copy.wait()
 
     count = rows * breadth
     here = pl.ds(i * rows, rows)
-    own_lines = own[here].reshape(count, depth)
-    mate_lines = mate[here].reshape(count, depth)
+    if not given:
+
+        @pl.when(i == 0)
+        def _():
+            local, mine = temporal_parts
+            held, part = depth // 2, depth // 4
+            there = (1 - group) * held
+            temporal[:, pl.ds(aligned(group * held), held)] = local[...]
+            temporal[:, pl.ds(aligned(there + core * part), part)] = mine[...]
+            tail = mates[-1][sizes[-1] :].reshape(3, part, width)
+            temporal[:, pl.ds(aligned(there + (1 - core) * part), part)] = tail
+
+        for j in range(blocks):
+
+            @pl.when(i == j)
+            def _():
+                own[...] = owns[j][:rows]
+                mate[...] = mates[j][:rows]
+
+        own_lines, mate_lines = (ref[...].reshape(count, depth) for ref in (own, mate))
+    else:
+        own_lines, mate_lines = (ref[here].reshape(count, depth) for ref in (own, mate))
     mate_tap, far_tap = 2 - 2 * core, 2 * core
+
+    def matrix(tap, columns):
+        return temporal[tap, :, columns]
+
     totals = [
-        dot(own_lines, temporal[1, :, columns]) + dot(mate_lines, temporal[mate_tap, :, columns])
-        for columns in halves(width)
+        dot(own_lines, matrix(1, columns)) + dot(mate_lines, matrix(mate_tap, columns)) for columns in halves(width)
     ]
 
     @pl.when(i == 0)
@@ -292,41 +332,50 @@
         )
     far_lines = jnp.where(present, far_lines, jnp.zeros_like(far_lines))
     for total, columns in zip(totals, halves(width), strict=True):
-        total += dot(far_lines, temporal[far_tap, :, columns]) + temporal_bias[:, columns]
+        total += dot(far_lines, matrix(far_tap, columns)) + temporal_bias[:, columns]
         out[:, :, columns] = total.astype(out.dtype).reshape(rows, breadth, -1)
 
 
-def mix_call(shape, owns, mates, fars, given, temporal_parts, spatial_parts, biases, before, begin, rows, tiles, cost):
+def mix_call(shape, far, owns, mates, sizes, temporal_parts, spatial_parts, biases, before, begin, rows, tiles, cost):
     height, breadth, width = shape
-    dtype = owns[0].dtype
-    count = sum(own.shape[0] for own in owns)
-    depth = owns[0].shape[2]
-    aliased = 0 if before is None else 1
-    operands = [*fars, *owns, *mates, *temporal_parts, *spatial_parts]
+    dtype = far.dtype
+    count, depth = sum(sizes), far.shape[2]
+    given = before is not None
+    operands = [*owns, *mates, far, *temporal_parts, *spatial_parts]
+    specs = [ANY] * len(operands)
+    in_vmem = pl.BlockSpec(memory_space=pltpu.VMEM)
+    if given:
+        specs[-1] = in_vmem
+    else:
+        for n in (*range(2 * len(owns)), 2 * len(owns) + 1, 2 * len(owns) + 2):
+            specs[n] = in_vmem
+            operands[n] = pltpu.with_memory_space_constraint(operands[n], pltpu.VMEM)
     whole = pl.BlockSpec((1, width), lambda i: (0, 0))
-    pieces = (len(spatial_parts) - 1, len(temporal_parts) - 1)
+    out_shape = [jax.ShapeDtypeStruct(shape, dtype)]
+    out_specs = [pl.BlockSpec((rows, breadth, width), lambda i: (i + begin // rows, 0, 0))]
+    if not given:
+        out_shape.append(pltpu.VMEM((3, depth, width), dtype))
+        out_specs.append(in_vmem)
     return pl.pallas_call(
-        functools.partial(mix_kernel, rows, begin, len(owns), given, pieces, aliased, tiles),
+        functools.partial(mix_kernel, rows, begin, sizes, given, len(spatial_parts), tiles),
         grid=(count // rows,),
-        in_specs=[ANY] * len(operands) + [whole, whole] + [ANY] * aliased,
-        out_specs=pl.BlockSpec((rows, breadth, width), lambda i: (i + begin // rows, 0, 0)),
+        in_specs=specs + [whole, whole] + [ANY] * given,
+        out_specs=out_specs,
         scratch_shapes=[
-            pltpu.VMEM((count, breadth, depth), dtype),
-            pltpu.VMEM((count, breadth, depth), dtype),
+            pltpu.VMEM((rows, breadth, depth), dtype),
+            pltpu.VMEM((rows, breadth, depth), dtype),
             pltpu.VMEM((count if given else count + 2, breadth, depth), dtype),
-            pltpu.VMEM((3, depth, width), dtype),
-            pltpu.VMEM((8, 128) if given else (9, depth, depth), dtype),
+            pltpu.VMEM((16, 128) if given else (9, depth, depth), dtype),
             pltpu.SemaphoreType.DMA((len(owns),)),
             pltpu.SemaphoreType.DMA((len(owns),)),
-            pltpu.SemaphoreType.DMA((len(fars),)),
-            pltpu.SemaphoreType.DMA((len(temporal_parts),)),
+            pltpu.SemaphoreType.DMA,
             pltpu.SemaphoreType.DMA((max(len(spatial_parts), 1),)),
         ],
-        out_shape=jax.ShapeDtypeStruct(shape, dtype),
-        input_output_aliases={len(operands) + 2: 0} if aliased else {},
+        out_shape=out_shape,
+        input_output_aliases={len(operands) + 2: 0} if given else {},
         cost_estimate=cost,
         compiler_params=pltpu.CompilerParams(vmem_limit_bytes=40 * 2**20),
-    )(*operands, *biases, *([before] if aliased else []))
+    )(*operands, *biases, *([before] if given else []))
 
 
 def near_device(videos, spatial_filter, temporal_filter, spatial_bias, temporal_bias):
@@ -339,6 +388,7 @@
     half = depth // 2
     swap = [(0, 1), (1, 0)]
     mates = [(i, i ^ 1) for i in range(tiles)]
+    pairs = [(i, i ^ 4) for i in range(tiles)]
     across = [pair for i in range(1, tiles - 1, 2) for pair in ((i, i + 1), (i + 1, i))]
     light = pl.CostEstimate(flops=1000, bytes_accessed=1000, transcendentals=0)
     heavy = pl.CostEstimate(flops=10**12, bytes_accessed=1000, transcendentals=0)
@@ -346,12 +396,16 @@
     def mine(first, count):
         return lambda: (pl.ds(first, count), pl.ds(aligned(half_starts(depth)[0]), half))
 
-    rows = 8
-    sent = height - rows + 1
-    taps = [(0, 3), (3, 2), (5, 4)]
-    middle = taps[2][0]
+    def relayed():
+        return mine(middle + relay_starts(relay)[0], relay)()
+
+    unit = height // 32
+    blocks = tuple(unit * block for block in (8, 8, 8, 8))
+    sent = height - blocks[-1] + 1
+    taps = [(0, 3), (3, 2)]
+    middle, relay = 5, 2
     cuts = [
-        [(mine(first, count), (count, half, width)) for first, count in taps],
+        [(mine(first, count), (count, half, width)) for first, count in taps] + [(relayed, (relay, half, width))],
         [(mine(0, 3), (3, half, width))],
         [(lambda: (pl.ds(0, sent),), (sent, breadth, channels))],
     ]
@@ -362,23 +416,26 @@
     def both(pieces):
         return [half for piece in pieces for half in (piece, lax.ppermute(piece, "tile", mates))]
 
-    base = conv_call(video, None, None, [spatial_filter], depth, range(9), True, 16, rows, light)
+    base = conv_call(video, None, None, None, [spatial_filter], depth, range(9), True, 16, blocks, light)
     *early, base = lax.optimization_barrier((*fetched[:2], base))
     early = both(early)
-    base = conv_call(video, base, None, early, depth, range(middle), False, 16, rows, light)
-    *late, base = lax.optimization_barrier((*fetched[2:], base))
+    base = conv_call(video, base, None, None, early, depth, range(middle), False, 16, blocks, light)
+    other = lax.ppermute(fetched[-1], "tile", pairs)
+    *late, base = lax.optimization_barrier((fetched[-1], other, base))
     late = both(late)
-    own = conv_call(video, base, biases[0], late, depth, range(middle, 9), False, 16, rows, light)
-    temporal_parts = [temporal_filter, *both([lax.ppermute(c_y, "dp", swap)])]
+    c_y = lax.ppermute(c_y, "dp", swap)
+    tail = c_y.reshape(-1, breadth, width)
+    own = conv_call(video, base, biases[0], tail, late, depth, range(middle, 9), False, 16, blocks, light)
+    temporal_parts = [temporal_filter, c_y]
     spatial_parts = [spatial_filter, *early, *late]
 
     last = lax.ppermute(own[-1], "tile", across)
     mate = [lax.ppermute(block, "tile", mates) for block in own]
-    out = mix_call(
-        shape, own[:-1], mate[:-1], [far], False, temporal_parts, spatial_parts, biases, None, 0, 12, tiles, heavy
+    out, temporal = mix_call(
+        shape, far, own[:-1], mate[:-1], blocks[:-1], temporal_parts, spatial_parts, biases, None, 0, 8, tiles, heavy
     )
-    out = mix_call(
-        shape, own[-1:], mate[-1:], [last], True, temporal_parts, [], biases, out, height - rows, rows, tiles, light
+    (out,) = mix_call(
+        shape, last, own[-1:], mate[-1:], blocks[-1:], [temporal], [], biases, out, sent - 1, blocks[-1], tiles, light
     )
     return out.reshape(videos.shape)
 
@@ -431,15 +488,16 @@
     return (result + temporal_bias).astype(jnp.bfloat16).reshape(videos.shape)
 
 
-def per_device(videos, *rest):
+def per_device(videos, spatial_filter, *rest):
     near = (
         videos.shape[0] == 1
         and videos.shape[1] == 1
         and videos.shape[2] % 32 == 0
+        and spatial_filter.shape[1] % (2 * videos.shape[3]) == 0
         and lax.axis_size("dp") == 2
-        and lax.axis_size("tile") % 2 == 0
+        and lax.axis_size("tile") % 8 == 0
     )
-    return (near_device if near else any_device)(videos, *rest)
+    return (near_device if near else any_device)(videos, spatial_filter, *rest)
 
 
 def solution(mesh):

time: 64.4 us -> 62.1 us (0.964)
  waiting for transfers between devices: 10.9 us -> 7.8 us
  starting transfers between devices: 17.9 us -> 18.8 us
    ppermute x4, waiting for transfers between devices: 3.15 us -> 1.53 us  [both(): lax.ppermute(piece, 'tile', mates)]
    ppermute x1 -> x2, waiting for transfers between devices: 3.74 us -> 2.5 us  [the longest x1 2.5 us: near_device(): other = lax.ppermute(fetched[-1], 'tile', pairs)]
    ppermute x1 -> x2, starting transfers between devices: 1.46 us -> 2.44 us  [the longest x1 1.24 us: near_device(): c_y = lax.ppermute(c_y, 'dp', swap)]
    ppermute x1, starting transfers between devices: 3.59 us -> 2.8 us  [near_device(): last = lax.ppermute(own[-1], 'tile', across)]
  transfers between devices with their start and end apart: 14 -> 15, of which waited for: 5 -> 5; matrix products, arithmetic and copies ran while one was open for 0% -> 0% of each run, Pallas kernels for 41% -> 43%
where the time goes in v4:
time: 62.1 us; the launch traced here: 61.5 us
  Pallas kernels  31.5 us (51%)
  starting transfers between devices  18.8 us (30%)
  waiting for transfers between devices  7.8 us (13%)
  local copies, waits for them, and re-layouts  3.27 us (5%)
    pallas_call x2, Pallas kernels, mix_call(): pl.pallas_call(functools.partial(mix_kernel, rows, begin, sizes, given, l...  15.7 us
    pallas_call x3, Pallas kernels, conv_call(): pl.pallas_call(functools.partial(conv_kernel, rows, blocks, taps, held, b...  13.9 us
    ppermute x1, starting transfers between devices, near_device(): far = lax.ppermute(far, 'tile', across)  4.51 us
    ppermute x4, starting transfers between devices, both(): lax.ppermute(piece, 'tile', mates)  4.45 us
    ppermute x3, starting transfers between devices, near_device(): fetched = [lax.ppermute(piece, 'dp', swap) for piece in cut]  3.6 us
    ppermute x3, waiting for transfers between devices, near_device(): fetched = [lax.ppermute(piece, 'dp', swap) for piece in cut]  3.56 us
    unnamed x12, local copies, waits for them, and re-layouts  3.27 us
    ppermute x1, starting transfers between devices, near_device(): last = lax.ppermute(own[-1], 'tile', across)  2.8 us
  transfers between devices with their start and end apart: 15, of which 5 were waited for; matrix products, arithmetic and copies ran while one was open for 0% of the time, Pallas kernels for 43%

profile of v4, /device:TPU:1, one launch (start us, length us, event | category | flops | bytes accessed | tf_op | source)
XLA Modules:
  0.0 61.5 jit_solution(16219657425724765343)
XLA Ops:
  0.0 1.9 %shard_map.55 = (bf16[3,128,512]{2,1,0:T(8,128)(2,1)S(1)}, bf16[2,128,512]{2,1,0:T(8,128)(2,1)S(1)}, bf16[2,128,512]{2,1,0:T(8,128)(2,1)S(1)}, bf16[3,128,512]{2,1,0:T(8,128)(2,1)S(1)}, bf16[25,64,512]{2,1,0:T(8,128)(2,1)S(1)}) custom-call(bf16[9,256,512]{2,1,0:T(8,128)(2,1)} %refs_9_.1, bf16[3,256,512]{2,1,0:T(8,128)(2,1)} %refs_7_.1, ...), custom_call_target="tpu_custom_call" | custom-call | flops 1000 | bytes 1000 | tf_op jit(solution)/shard_map/pallas_call | solution.py:80
  1.9 2.1 %collective-permute-start.2 = (bf16[3,128,512]{2,1,0:T(8,128)(2,1)S(1)}, bf16[3,128,512]{2,1,0:T(8,128)(2,1)S(1)}, u32[]{:S(2)}, u32[]{:S(2)}) collective-permute-start(bf16[3,128,512]{2,1,0:T(8,128)(2,1)S(1)} %get-tuple-element.23), channel_id=1, source_target_pairs={{0,16},{16,0},{1,17},{17,1},{2,18},{18,2},{3,19},{19,3},{4,20},{20... | collective-permute-start | bytes 1179656 | tf_op jit(solution)/shard_map/ppermute | solution.py:414
  4.0 0.1 collective-permute-start.3
  4.1 1.4 %collective-permute-start = (bf16[2,128,512]{2,1,0:T(8,128)(2,1)S(1)}, bf16[2,128,512]{2,1,0:T(8,128)(2,1)S(1)}, u32[]{:S(2)}, u32[]{:S(2)}) collective-permute-start(bf16[2,128,512]{2,1,0:T(8,128)(2,1)S(1)} %get-tuple-element.22), channel_id=1, source_target_pairs={{0,16},{16,0},{1,17},{17,1},{2,18},{18,2},{3,19},{19,3},{4,20},{20... | collective-permute-start | bytes 786440 | tf_op jit(solution)/shard_map/ppermute | solution.py:414
  5.5 4.5 %collective-permute-start.14 = (bf16[25,64,512]{2,1,0:T(8,128)(2,1)S(1)}, bf16[25,64,512]{2,1,0:T(8,128)(2,1)S(1)}, u32[]{:S(2)}, u32[]{:S(2)}) collective-permute-start(bf16[25,64,512]{2,1,0:T(8,128)(2,1)S(1)} %get-tuple-element.36), channel_id=1, source_target_pairs={{1,2},{2,1},{3,4},{4,3},{5,6},{6,5},{7,8},{8,7},{9,10},{10,9},{11,... | collective-permute-start | bytes 4915208 | tf_op jit(solution)/shard_map/ppermute | solution.py:413
  10.0 0.0 copy-start
  10.0 1.6 %copy-done = bf16[1,1,32,64,512]{4,3,2,1,0:T(8,128)(2,1)S(1)} copy-done((bf16[1,1,32,64,512]{4,3,2,1,0:T(8,128)(2,1)S(1)}, bf16[1,1,32,64,512]{4,3,2,1,0:T(8,128)(2,1)}, u32[]{:S(2)}) %copy-start) | copy-done | bytes 2097176
  11.6 0.0 copy-start.1
  11.6 1.7 %copy-done.1 = bf16[9,256,512]{2,1,0:T(8,128)(2,1)S(1)} copy-done((bf16[9,256,512]{2,1,0:T(8,128)(2,1)S(1)}, bf16[9,256,512]{2,1,0:T(8,128)(2,1)}, u32[]{:S(2)}) %copy-start.1) | copy-done | bytes 2359320
  13.3 5.5 %shard_map.56.refs_0_ = f32[32,64,512]{2,1,0:T(8,128)S(1)} custom-call(bf16[32,64,512]{2,1,0:T(8,128)(2,1)S(1)} %bitcast.6, bf16[9,256,512]{2,1,0:T(8,128)(2,1)S(1)} %copy-done.1), custom_call_target="tpu_custom_call" | custom-call | flops 1000 | bytes 1000 | tf_op jit(solution)/shard_map/pallas_call | solution.py:195
  18.8 0.0 collective-permute-done.3.refs_3_.refs_12_
  18.8 0.0 collective-permute-done.2.refs_1_.refs_10_
  18.8 1.7 %collective-permute-start.4 = (bf16[3,128,512]{2,1,0:T(8,128)(2,1)S(1)}, bf16[3,128,512]{2,1,0:T(8,128)(2,1)S(1)}, u32[]{:S(2)}, u32[]{:S(2)}) collective-permute-start(bf16[3,128,512]{2,1,0:T(8,128)(2,1)S(1)} %collective-permute-done.2.refs_1_.refs_10_), channel_id=1, source_target_pairs={{0,1},{1,0},{2,3},{3,2},{4,5},{5,4},{6,7},{7,6},{8,9},{9,8},{10,11... | collective-permute-start | bytes 1179656 | tf_op jit(solution)/shard_map/ppermute | solution.py:417
  20.5 0.0 collective-permute-start.5
  20.5 3.6 %collective-permute-done.refs_3_.refs_14_ = bf16[2,128,512]{2,1,0:T(8,128)(2,1)S(1)} collective-permute-done((bf16[2,128,512]{2,1,0:T(8,128)(2,1)S(1)}, bf16[2,128,512]{2,1,0:T(8,128)(2,1)S(1)}, u32[]{:S(2)}, u32[]{:S(2)}) %collective-permute-start) | collective-permute-done | bytes 262176 | tf_op jit(solution)/shard_map/ppermute | solution.py:414
  24.1 1.2 %collective-permute-start.1 = (bf16[2,128,512]{2,1,0:T(8,128)(2,1)S(1)}, bf16[2,128,512]{2,1,0:T(8,128)(2,1)S(1)}, u32[]{:S(2)}, u32[]{:S(2)}) collective-permute-start(bf16[2,128,512]{2,1,0:T(8,128)(2,1)S(1)} %collective-permute-done.refs_3_.refs_14_), channel_id=1, source_target_pairs={{0,4},{1,5},{2,6},{3,7},{4,0},{5,1},{6,2},{7,3},{8,12},{9,13},{10,... | collective-permute-start | bytes 786440 | tf_op jit(solution)/shard_map/ppermute | solution.py:423
  25.3 0.0 copy-start.4
  25.3 1.2 %collective-permute-start.6 = (bf16[3,128,512]{2,1,0:T(8,128)(2,1)S(1)}, bf16[3,128,512]{2,1,0:T(8,128)(2,1)S(1)}, u32[]{:S(2)}, u32[]{:S(2)}) collective-permute-start(bf16[3,128,512]{2,1,0:T(8,128)(2,1)S(1)} %get-tuple-element.29), channel_id=1, source_target_pairs={{0,16},{16,0},{1,17},{17,1},{2,18},{18,2},{3,19},{19,3},{4,20},{20... | collective-permute-start | bytes 1179656 | tf_op jit(solution)/shard_map/ppermute | solution.py:426
  26.5 0.0 collective-permute-done.5.refs_4_.refs_13_
  26.5 0.0 collective-permute-done.4.refs_2_.refs_11_
  26.5 3.4 %shard_map.57.refs_0_ = f32[32,64,512]{2,1,0:T(8,128)S(1)} custom-call(bf16[32,64,512]{2,1,0:T(8,128)(2,1)S(1)} %bitcast.7, f32[32,64,512]{2,1,0:T(8,128)S(1)} %shard_map.56.refs_0_, bf16[3,128,512]{2,1,0:T(8,128)(2,1)S(1)} %collective-permute-done.2.refs_1_.refs_10_, bf16[3,128,512]{2,1,0:T(8,128)(2,1)S(1)} %collective-permute-done.4.refs_2_.refs_11_, ...), custom_call_target="tpu_custom_call" | custom-call | flops 1000 | bytes 1000 | tf_op jit(solution)/shard_map/pallas_call | solution.py:195
  30.0 2.5 %collective-permute-done.1.refs_5_.refs_16_ = bf16[2,128,512]{2,1,0:T(8,128)(2,1)S(1)} collective-permute-done((bf16[2,128,512]{2,1,0:T(8,128)(2,1)S(1)}, bf16[2,128,512]{2,1,0:T(8,128)(2,1)S(1)}, u32[]{:S(2)}, u32[]{:S(2)}) %collective-permute-start.1) | collective-permute-done | bytes 262176 | tf_op jit(solution)/shard_map/ppermute | solution.py:423
  32.5 2.7 %collective-permute-start.7 = (bf16[2,128,512]{2,1,0:T(8,128)(2,1)S(1)}, bf16[2,128,512]{2,1,0:T(8,128)(2,1)S(1)}, u32[]{:S(2)}, u32[]{:S(2)}) collective-permute-start(bf16[2,128,512]{2,1,0:T(8,128)(2,1)S(1)} %collective-permute-done.refs_3_.refs_14_), channel_id=1, source_target_pairs={{0,1},{1,0},{2,3},{3,2},{4,5},{5,4},{6,7},{7,6},{8,9},{9,8},{10,11... | collective-permute-start | bytes 786440 | tf_op jit(solution)/shard_map/ppermute | solution.py:417
  35.2 0.0 collective-permute-start.8
  35.2 0.0 collective-permute-done.6.refs_8_
  35.2 1.2 %collective-permute-done.7.refs_4_.refs_15_ = bf16[2,128,512]{2,1,0:T(8,128)(2,1)S(1)} collective-permute-done((bf16[2,128,512]{2,1,0:T(8,128)(2,1)S(1)}, bf16[2,128,512]{2,1,0:T(8,128)(2,1)S(1)}, u32[]{:S(2)}, u32[]{:S(2)}) %collective-permute-start.7) | collective-permute-done | bytes 262176 | tf_op jit(solution)/shard_map/ppermute | solution.py:417
  36.4 0.4 collective-permute-done.8.refs_6_.refs_17_
  36.8 0.0 copy-done.4
  36.8 0.0 copy-start.2
  36.8 0.0 copy-start.3
  36.8 0.0 copy-start.5
  36.8 5.0 %shard_map.58 = (bf16[8,64,512]{2,1,0:T(8,128)(2,1)S(1)}, bf16[8,64,512]{2,1,0:T(8,128)(2,1)S(1)}, bf16[14,64,512]{2,1,0:T(8,128)(2,1)S(1)}, bf16[8,64,512]{2,1,0:T(8,128)(2,1)}) custom-call(bf16[32,64,512]{2,1,0:T(8,128)(2,1)S(1)} %bitcast.8, f32[32,64,512]{2,1,0:T(8,128)S(1)} %shard_map.57.refs_0_, f32[1,512]{1,0:T(1,128)S(1)} %bitcast.10, ...), custom_call_target="tpu_custom_call" | custom-call | flops 1000 | bytes 1000 | tf_op jit(solution)/shard_map/pallas_call | solution.py:195
  41.8 0.4 collective-permute-start.13
  42.2 0.1 collective-permute-start.11
  42.3 0.4 collective-permute-start.12
  42.7 2.8 %collective-permute-start.10 = (bf16[8,64,512]{2,1,0:T(8,128)(2,1)}, bf16[8,64,512]{2,1,0:T(8,128)(2,1)}, u32[]{:S(2)}, u32[]{:S(2)}) collective-permute-start(bf16[8,64,512]{2,1,0:T(8,128)(2,1)} %get-tuple-element.32.refs_0_), channel_id=1, source_target_pairs={{1,2},{2,1},{3,4},{4,3},{5,6},{6,5},{7,8},{8,7},{9,10},{10,9},{11,... | collective-permute-start | bytes 1572872 | tf_op jit(solution)/shard_map/ppermute | solution.py:432
  45.5 0.0 collective-permute-done.11.refs_3_
  45.5 0.1 collective-permute-start.9
  45.6 0.2 collective-permute-done.12.refs_4_
  45.8 0.0 collective-permute-done.14.refs_6_
  45.8 0.0 collective-permute-done.13.refs_5_
  45.8 0.0 copy-done.2
  45.8 0.0 copy-done.3
  45.8 0.0 copy-done.5
  45.8 12.6 %shard_map.59 = (bf16[32,64,512]{2,1,0:T(8,128)(2,1)}, bf16[3,512,512]{2,1,0:T(8,128)(2,1)S(1)}) custom-call(bf16[8,64,512]{2,1,0:T(8,128)(2,1)S(1)} %get-tuple-element.33.refs_0_, bf16[8,64,512]{2,1,0:T(8,128)(2,1)S(1)} %get-tuple-element.34.refs_1_, bf16[14,64,512]{2,1,0:T(8,128)(2,1)S(1)} %get-tuple-element.35.refs_2_, ...), custom_call_target="tpu_custom_call" | custom-call | flops 999999995904 | bytes 1000 | tf_op jit(solution)/shard_map/pallas_call | solution.py:359
  58.5 0.0 collective-permute-done.10.refs_2_
  58.5 0.0 collective-permute-done.9.refs_1_
  58.5 3.1 %shard_map.60 = bf16[32,64,512]{2,1,0:T(8,128)(2,1)} custom-call(bf16[8,64,512]{2,1,0:T(8,128)(2,1)} %get-tuple-element.32.refs_0_, bf16[8,64,512]{2,1,0:T(8,128)(2,1)} %collective-permute-done.9.refs_1_, bf16[8,64,512]{2,1,0:T(8,128)(2,1)} %collective-permute-done.10.refs_2_, ...), custom_call_target="tpu_custom_call", output_to_operand_aliasing={{}: (6, {})} | custom-call | flops 1000 | bytes 1000 | tf_op jit(solution)/shard_map/pallas_call | solution.py:359
Async XLA Ops:
  1.9 16.9 %collective-permute-start.2 = (bf16[3,128,512]{2,1,0:T(8,128)(2,1)S(1)}, bf16[3,128,512]{2,1,0:T(8,128)(2,1)S(1)}, u32[]{:S(2)}, u32[]{:S(2)}) collective-permute-start(bf16[3,128,512]{2,1,0:T(8,128)(2,1)S(1)} %get-tuple-element.23), channel_id=1, source_target_pairs={{0,16},{16,0},{1,17},{17,1},{2,18},{18,2},{3,19},{19,3},{4,20},{20... | collective-permute-start | bytes 1179656 | tf_op jit(solution)/shard_map/ppermute | solution.py:414
  4.0 14.8 %collective-permute-start.3 = (bf16[2,128,512]{2,1,0:T(8,128)(2,1)S(1)}, bf16[2,128,512]{2,1,0:T(8,128)(2,1)S(1)}, u32[]{:S(2)}, u32[]{:S(2)}) collective-permute-start(bf16[2,128,512]{2,1,0:T(8,128)(2,1)S(1)} %get-tuple-element.24), channel_id=1, source_target_pairs={{0,16},{16,0},{1,17},{17,1},{2,18},{18,2},{3,19},{19,3},{4,20},{20... | collective-permute-start | bytes 786440 | tf_op jit(solution)/shard_map/ppermute | solution.py:414
  4.1 20.0 %collective-permute-start = (bf16[2,128,512]{2,1,0:T(8,128)(2,1)S(1)}, bf16[2,128,512]{2,1,0:T(8,128)(2,1)S(1)}, u32[]{:S(2)}, u32[]{:S(2)}) collective-permute-start(bf16[2,128,512]{2,1,0:T(8,128)(2,1)S(1)} %get-tuple-element.22), channel_id=1, source_target_pairs={{0,16},{16,0},{1,17},{17,1},{2,18},{18,2},{3,19},{19,3},{4,20},{20... | collective-permute-start | bytes 786440 | tf_op jit(solution)/shard_map/ppermute | solution.py:414
  5.5 40.3 %collective-permute-start.14 = (bf16[25,64,512]{2,1,0:T(8,128)(2,1)S(1)}, bf16[25,64,512]{2,1,0:T(8,128)(2,1)S(1)}, u32[]{:S(2)}, u32[]{:S(2)}) collective-permute-start(bf16[25,64,512]{2,1,0:T(8,128)(2,1)S(1)} %get-tuple-element.36), channel_id=1, source_target_pairs={{1,2},{2,1},{3,4},{4,3},{5,6},{6,5},{7,8},{8,7},{9,10},{10,9},{11,... | collective-permute-start | bytes 4915208 | tf_op jit(solution)/shard_map/ppermute | solution.py:413
  10.0 1.6 %copy-start = (bf16[1,1,32,64,512]{4,3,2,1,0:T(8,128)(2,1)S(1)}, bf16[1,1,32,64,512]{4,3,2,1,0:T(8,128)(2,1)}, u32[]{:S(2)}) copy-start(bf16[1,1,32,64,512]{4,3,2,1,0:T(8,128)(2,1)} %param.5) | copy-start | bytes 6291460
  11.6 1.7 %copy-start.1 = (bf16[9,256,512]{2,1,0:T(8,128)(2,1)S(1)}, bf16[9,256,512]{2,1,0:T(8,128)(2,1)}, u32[]{:S(2)}) copy-start(bf16[9,256,512]{2,1,0:T(8,128)(2,1)} %refs_9_.1) | copy-start | bytes 7077892
  18.8 7.7 %collective-permute-start.4 = (bf16[3,128,512]{2,1,0:T(8,128)(2,1)S(1)}, bf16[3,128,512]{2,1,0:T(8,128)(2,1)S(1)}, u32[]{:S(2)}, u32[]{:S(2)}) collective-permute-start(bf16[3,128,512]{2,1,0:T(8,128)(2,1)S(1)} %collective-permute-done.2.refs_1_.refs_10_), channel_id=1, source_target_pairs={{0,1},{1,0},{2,3},{3,2},{4,5},{5,4},{6,7},{7,6},{8,9},{9,8},{10,11... | collective-permute-start | bytes 1179656 | tf_op jit(solution)/shard_map/ppermute | solution.py:417
  20.5 6.0 %collective-permute-start.5 = (bf16[2,128,512]{2,1,0:T(8,128)(2,1)S(1)}, bf16[2,128,512]{2,1,0:T(8,128)(2,1)S(1)}, u32[]{:S(2)}, u32[]{:S(2)}) collective-permute-start(bf16[2,128,512]{2,1,0:T(8,128)(2,1)S(1)} %collective-permute-done.3.refs_3_.refs_12_), channel_id=1, source_target_pairs={{0,1},{1,0},{2,3},{3,2},{4,5},{5,4},{6,7},{7,6},{8,9},{9,8},{10,11... | collective-permute-start | bytes 786440 | tf_op jit(solution)/shard_map/ppermute | solution.py:417
  24.1 8.4 %collective-permute-start.1 = (bf16[2,128,512]{2,1,0:T(8,128)(2,1)S(1)}, bf16[2,128,512]{2,1,0:T(8,128)(2,1)S(1)}, u32[]{:S(2)}, u32[]{:S(2)}) collective-permute-start(bf16[2,128,512]{2,1,0:T(8,128)(2,1)S(1)} %collective-permute-done.refs_3_.refs_14_), channel_id=1, source_target_pairs={{0,4},{1,5},{2,6},{3,7},{4,0},{5,1},{6,2},{7,3},{8,12},{9,13},{10,... | collective-permute-start | bytes 786440 | tf_op jit(solution)/shard_map/ppermute | solution.py:423
  25.3 11.5 %copy-start.4 = (f32[512]{0:T(512)S(1)}, f32[512]{0:T(512)}, u32[]{:S(2)}) copy-start(f32[512]{0:T(512)} %param.8) | copy-start | bytes 6148
  25.3 9.9 %collective-permute-start.6 = (bf16[3,128,512]{2,1,0:T(8,128)(2,1)S(1)}, bf16[3,128,512]{2,1,0:T(8,128)(2,1)S(1)}, u32[]{:S(2)}, u32[]{:S(2)}) collective-permute-start(bf16[3,128,512]{2,1,0:T(8,128)(2,1)S(1)} %get-tuple-element.29), channel_id=1, source_target_pairs={{0,16},{16,0},{1,17},{17,1},{2,18},{18,2},{3,19},{19,3},{4,20},{20... | collective-permute-start | bytes 1179656 | tf_op jit(solution)/shard_map/ppermute | solution.py:426
  32.5 3.9 %collective-permute-start.7 = (bf16[2,128,512]{2,1,0:T(8,128)(2,1)S(1)}, bf16[2,128,512]{2,1,0:T(8,128)(2,1)S(1)}, u32[]{:S(2)}, u32[]{:S(2)}) collective-permute-start(bf16[2,128,512]{2,1,0:T(8,128)(2,1)S(1)} %collective-permute-done.refs_3_.refs_14_), channel_id=1, source_target_pairs={{0,1},{1,0},{2,3},{3,2},{4,5},{5,4},{6,7},{7,6},{8,9},{9,8},{10,11... | collective-permute-start | bytes 786440 | tf_op jit(solution)/shard_map/ppermute | solution.py:417
  35.2 1.5 %collective-permute-start.8 = (bf16[2,128,512]{2,1,0:T(8,128)(2,1)S(1)}, bf16[2,128,512]{2,1,0:T(8,128)(2,1)S(1)}, u32[]{:S(2)}, u32[]{:S(2)}) collective-permute-start(bf16[2,128,512]{2,1,0:T(8,128)(2,1)S(1)} %collective-permute-done.1.refs_5_.refs_16_), channel_id=1, source_target_pairs={{0,1},{1,0},{2,3},{3,2},{4,5},{5,4},{6,7},{7,6},{8,9},{9,8},{10,11... | collective-permute-start | bytes 786440 | tf_op jit(solution)/shard_map/ppermute | solution.py:417
  36.8 9.0 %copy-start.2 = (bf16[9,256,512]{2,1,0:T(8,128)(2,1)S(1)}, bf16[9,256,512]{2,1,0:T(8,128)(2,1)}, u32[]{:S(2)}) copy-start(bf16[9,256,512]{2,1,0:T(8,128)(2,1)} %refs_9_.1) | copy-start | bytes 7077892
  36.8 9.0 %copy-start.3 = (bf16[3,256,512]{2,1,0:T(8,128)(2,1)S(1)}, bf16[3,256,512]{2,1,0:T(8,128)(2,1)}, u32[]{:S(2)}) copy-start(bf16[3,256,512]{2,1,0:T(8,128)(2,1)} %refs_7_.1) | copy-start | bytes 2359300
  36.8 9.0 %copy-start.5 = (f32[512]{0:T(512)S(1)}, f32[512]{0:T(512)}, u32[]{:S(2)}) copy-start(f32[512]{0:T(512)} %param.9) | copy-start | bytes 6148
  41.8 4.0 %collective-permute-start.13 = (bf16[14,64,512]{2,1,0:T(8,128)(2,1)S(1)}, bf16[14,64,512]{2,1,0:T(8,128)(2,1)S(1)}, u32[]{:S(2)}, u32[]{:S(2)}) collective-permute-start(bf16[14,64,512]{2,1,0:T(8,128)(2,1)S(1)} %get-tuple-element.35.refs_2_), channel_id=1, source_target_pairs={{0,1},{1,0},{2,3},{3,2},{4,5},{5,4},{6,7},{7,6},{8,9},{9,8},{10,11... | collective-permute-start | bytes 2752520 | tf_op jit(solution)/shard_map/ppermute | solution.py:433
  42.2 3.3 %collective-permute-start.11 = (bf16[8,64,512]{2,1,0:T(8,128)(2,1)S(1)}, bf16[8,64,512]{2,1,0:T(8,128)(2,1)S(1)}, u32[]{:S(2)}, u32[]{:S(2)}) collective-permute-start(bf16[8,64,512]{2,1,0:T(8,128)(2,1)S(1)} %get-tuple-element.33.refs_0_), channel_id=1, source_target_pairs={{0,1},{1,0},{2,3},{3,2},{4,5},{5,4},{6,7},{7,6},{8,9},{9,8},{10,11... | collective-permute-start | bytes 1572872 | tf_op jit(solution)/shard_map/ppermute | solution.py:433
  42.3 3.5 %collective-permute-start.12 = (bf16[8,64,512]{2,1,0:T(8,128)(2,1)S(1)}, bf16[8,64,512]{2,1,0:T(8,128)(2,1)S(1)}, u32[]{:S(2)}, u32[]{:S(2)}) collective-permute-start(bf16[8,64,512]{2,1,0:T(8,128)(2,1)S(1)} %get-tuple-element.34.refs_1_), channel_id=1, source_target_pairs={{0,1},{1,0},{2,3},{3,2},{4,5},{5,4},{6,7},{7,6},{8,9},{9,8},{10,11... | collective-permute-start | bytes 1572872 | tf_op jit(solution)/shard_map/ppermute | solution.py:433
  42.7 15.8 %collective-permute-start.10 = (bf16[8,64,512]{2,1,0:T(8,128)(2,1)}, bf16[8,64,512]{2,1,0:T(8,128)(2,1)}, u32[]{:S(2)}, u32[]{:S(2)}) collective-permute-start(bf16[8,64,512]{2,1,0:T(8,128)(2,1)} %get-tuple-element.32.refs_0_), channel_id=1, source_target_pairs={{1,2},{2,1},{3,4},{4,3},{5,6},{6,5},{7,8},{8,7},{9,10},{10,9},{11,... | collective-permute-start | bytes 1572872 | tf_op jit(solution)/shard_map/ppermute | solution.py:432
  45.5 13.0 %collective-permute-start.9 = (bf16[8,64,512]{2,1,0:T(8,128)(2,1)}, bf16[8,64,512]{2,1,0:T(8,128)(2,1)}, u32[]{:S(2)}, u32[]{:S(2)}) collective-permute-start(bf16[8,64,512]{2,1,0:T(8,128)(2,1)} %get-tuple-element.32.refs_0_), channel_id=1, source_target_pairs={{0,1},{1,0},{2,3},{3,2},{4,5},{5,4},{6,7},{7,6},{8,9},{9,8},{10,11... | collective-permute-start | bytes 1572872 | tf_op jit(solution)/shard_map/ppermute | solution.py:433

commit v5 on v4

v5 whole, which is shorter than its diff:
```python
import functools

import jax
import jax.numpy as jnp
from jax import lax
from jax.experimental import pallas as pl
from jax.experimental.pallas import tpu as pltpu
from jax.sharding import PartitionSpec as P

ANY = pl.BlockSpec(memory_space=pltpu.HBM)


def dot(a, b):
    return jnp.dot(a, b, preferred_element_type=jnp.float32)


def silu(v):
    return v / (1 + jnp.exp(-v))


def halves(width):
    cut = width // 2
    return [slice(0, cut), slice(cut, width)]


def seat():
    return lax.axis_index("dp"), lax.rem(lax.axis_index("tile"), 2)


def half_starts(depth):
    _, core = seat()
    return [core * (depth // 2), (1 - core) * (depth // 2)]


def relay_starts(size):
    pair = lax.rem(lax.axis_index("tile") // 4, 2)
    return [pair * size, (1 - pair) * size]


def aligned(start):
    return pl.multiple_of(start, 16)


def rows_conv(padded, weights, taps, first, rows, breadth, columns):
    count = rows * breadth
    place = lax.rem(lax.broadcasted_iota(jnp.int32, (count, 1), 0), breadth)
    depth = padded.shape[2]
    lines = [padded[pl.ds(first + dy, rows)].reshape(count, depth) for dy in range(3)]

    def side(dx):
        mine = [(n, tap // 3) for n, tap in enumerate(taps) if tap % 3 == dx]
        matrix = jnp.concatenate([weights(n, columns) for n, _ in mine], axis=0)
        return dot(jnp.concatenate([lines[dy] for _, dy in mine], axis=1), matrix)

    total = side(1)
    total += jnp.where(place == 0, 0.0, pltpu.roll(side(0), 1, 0))
    total += jnp.where(place == breadth - 1, 0.0, pltpu.roll(side(2), count - 1, 0))
    return total


def cut_kernel(cuts, *refs):
    sources, targets, sem = refs[: len(cuts)], refs[len(cuts) : -1], refs[-1]
    copies = []
    for source, parts in zip(sources, cuts, strict=True):
        for where, _ in parts:
            n = len(copies)
            copies.append(pltpu.make_async_copy(source.at[where()], targets[n], sem.at[n]))
    for copy in copies:
        copy.start()
    for copy in copies:
        copy.wait()


def cut_call(sources, cuts, cost):
    shapes = [
        pltpu.VMEM(shape, source.dtype)
        for source, parts in zip(sources, cuts, strict=True)
        for _, shape in parts
    ]
    return pl.pallas_call(
        functools.partial(cut_kernel, cuts),
        in_specs=[ANY] * len(sources),
        out_specs=[pl.BlockSpec(memory_space=pltpu.VMEM)] * len(shapes),
        scratch_shapes=[pltpu.SemaphoreType.DMA((len(shapes),))],
        out_shape=shapes,
        cost_estimate=cost,
    )(*sources)


def block_spans(blocks, step, rows):
    spans = []
    for j, size in enumerate(blocks):
        at = sum(blocks[:j])
        low, high = max(at, step * rows), min(at + size, (step + 1) * rows)
        if high > low:
            spans.append((j, slice(low - at, high - at), slice(low - step * rows, high - step * rows)))
    return spans


def conv_kernel(rows, taps, held, video, *refs):
    refs = list(refs)
    base = None if held else refs.pop(0)
    weights, video_sem, part_sem = refs[-3:]
    out, padded = refs[-5:-3]
    parts = refs[:-5]
    height, breadth = video.shape[:2]
    steps = height // rows
    depth = padded.shape[2]
    pieces = 1 if held else 2
    i = pl.program_id(0)
    group, _ = seat()
    starts = [0] if held else half_starts(depth)

    def video_copy(j):
        channels = pl.ds(pl.multiple_of((group if held else 1 - group) * depth, 128), depth)
        return pltpu.make_async_copy(
            video.at[pl.ds(j * rows, rows), :, channels],
            padded.at[pl.ds(j * rows + 1, rows)],
            video_sem.at[j],
        )

    def part_copies():
        copies, begin = [], 0
        for n in range(0, len(parts), pieces):
            size = parts[n].shape[0]
            for p, start in enumerate(starts):
                there = weights.at[pl.ds(begin, size), pl.ds(aligned(start), parts[n + p].shape[1])]
                copies.append(pltpu.make_async_copy(parts[n + p], there, part_sem.at[n + p]))
            begin += size
        return copies

    @pl.when(i == 0)
    def _():
        video_copy(0).start()
        for copy in part_copies():
            copy.start()
        for j in range(1, steps):
            video_copy(j).start()
        padded[0] = jnp.zeros(padded.shape[1:], padded.dtype)
        padded[height + 1] = jnp.zeros(padded.shape[1:], padded.dtype)
        video_copy(0).wait()
        for copy in part_copies():
            copy.wait()

    @pl.when(i + 1 < steps)
    def _():
        video_copy(i + 1).wait()

    for columns in halves(out.shape[2]):
        total = rows_conv(padded, lambda n, c: weights[n, :, c], taps, i * rows, rows, breadth, columns)
        here = pl.ds(i * rows, rows)
        if not held:
            total += base[here, :, columns].reshape(total.shape)
        out[here, :, columns] = total.reshape(rows, breadth, -1)


IN_VMEM = pl.BlockSpec(memory_space=pltpu.VMEM)


def in_vmem(array):
    return pltpu.with_memory_space_constraint(array, pltpu.VMEM)


def conv_call(video, base, parts, depth, taps, rows, cost):
    height, breadth, _ = video.shape
    width = parts[0].shape[2]
    steps = height // rows
    held = base is None
    padded = (height + 2, breadth, depth)
    return pl.pallas_call(
        functools.partial(conv_kernel, rows, taps, held),
        grid=(steps,),
        in_specs=[ANY] + [IN_VMEM] * (not held) + [ANY] * len(parts),
        out_specs=[IN_VMEM] * (1 if held else 2),
        scratch_shapes=[pltpu.VMEM(padded, video.dtype)] * held
        + [
            pltpu.VMEM((len(taps), depth, width), video.dtype),
            pltpu.SemaphoreType.DMA((steps,)),
            pltpu.SemaphoreType.DMA((len(parts),)),
        ],
        out_shape=[pltpu.VMEM((height, breadth, width), jnp.float32)]
        + [pltpu.VMEM(padded, video.dtype)] * (not held),
        cost_estimate=cost,
        compiler_params=pltpu.CompilerParams(vmem_limit_bytes=24 * 2**20),
    )(video, *([] if held else [in_vmem(base)]), *parts)


def own_kernel(rows, blocks, taps, padded, base, bias, tail, *refs):
    parts = refs[: -len(blocks) - 2]
    outs, whole, part_sem = refs[-len(blocks) - 2 : -2], refs[-2], refs[-1]
    local, early, late = parts[0], parts[1:-4], parts[-4:]
    breadth, depth = padded.shape[1:]
    steps = (padded.shape[0] - 2) // rows
    group, _ = seat()
    other = (1 - group) * depth

    def early_copies():
        there = whole.at[:, pl.ds(aligned(group * depth), depth)]
        copies, begin = [pltpu.make_async_copy(local, there, part_sem.at[0])], 0
        for n in range(0, len(early), 2):
            size = early[n].shape[0]
            for p, start in enumerate(half_starts(depth)):
                there = whole.at[pl.ds(begin, size), pl.ds(aligned(other + start), early[n + p].shape[1])]
                copies.append(pltpu.make_async_copy(early[n + p], there, part_sem.at[1 + n + p]))
            begin += size
        return copies

    for copy in early_copies():
        copy.start()
    for n, first in enumerate(relay_starts(late[0].shape[0])):
        for p, start in enumerate(half_starts(depth)):
            part = late[2 * n + p]
            for tap in range(part.shape[0]):
                whole[taps[0] + first + tap, pl.ds(aligned(other + start), part.shape[1])] = part[tap]
    outs[-2][blocks[-2] :] = tail[...]

    def matrix(n, columns):
        return whole[taps[n], pl.ds(aligned(other), depth), columns]

    for step in range(steps):
        for columns in halves(whole.shape[2]):
            total = rows_conv(padded, matrix, taps, step * rows, rows, breadth, columns)
            total += base[step * rows : (step + 1) * rows, :, columns].reshape(total.shape)
            hidden = silu(total + bias[:, columns]).astype(padded.dtype).reshape(rows, breadth, -1)
            for j, there, here in block_spans(blocks, step, rows):
                outs[j][there, :, columns] = hidden[here]

    for copy in early_copies():
        copy.wait()


def own_call(padded, base, bias, tail, parts, taps, rows, blocks, cost):
    height, breadth, depth = padded.shape[0] - 2, *padded.shape[1:]
    width = base.shape[2]
    sizes = [*blocks[:-2], blocks[-2] + tail.shape[0], blocks[-1]]
    operands = [padded, base, bias, tail, *parts]
    near_too = [n for n in range(len(operands)) if n < 4 or n >= len(operands) - 4]
    for n in near_too:
        operands[n] = in_vmem(operands[n])
    return pl.pallas_call(
        functools.partial(own_kernel, rows, blocks, taps),
        in_specs=[IN_VMEM if n in near_too else ANY for n in range(len(operands))],
        out_specs=[IN_VMEM] * (len(blocks) + 1),
        scratch_shapes=[pltpu.SemaphoreType.DMA((len(parts) - 4,))],
        out_shape=[pltpu.VMEM((size, breadth, width), padded.dtype) for size in sizes]
        + [pltpu.VMEM((9, 2 * depth, width), padded.dtype)],
        cost_estimate=cost,
        compiler_params=pltpu.CompilerParams(vmem_limit_bytes=24 * 2**20),
    )(*operands)


def mix_kernel(rows, begin, sizes, given, tiles, *refs):
    refs = list(refs)

    def take(count):
        taken = refs[:count]
        del refs[:count]
        return taken

    blocks = len(sizes)
    owns, mates = take(blocks), take(blocks)
    (far_part,) = take(1)
    temporal_parts = take(1 if given else 2)
    spatial = take(0 if given else 1)
    spatial_bias, temporal_bias = take(2)
    take(1 if given else 0)
    (out,) = take(1)
    (temporal,) = temporal_parts if given else take(1)
    own, mate, far, far_sem = refs
    breadth, width = out.shape[1:]
    depth = temporal.shape[1]
    group, core = seat()
    tile = lax.axis_index("tile")
    present = jnp.where(core == 0, tile > 0, tile < tiles - 1)
    i = pl.program_id(0)

    if given:
        second = []
        (own,), (mate,), far = owns, mates, far_part
    else:
        second = [pltpu.make_async_copy(far_part, far.at[pl.ds(1, far_part.shape[0])], far_sem)]

    @pl.when(i == 0)
    def _():
        for copy in second:
            copy.start()
        if not given:
            far[0] = jnp.zeros(far.shape[1:], far.dtype)

    count = rows * breadth
    here = pl.ds(i * rows, rows)
    if not given:

        @pl.when(i == 0)
        def _():
            local, mine = temporal_parts
            held, part = depth // 2, depth // 4
            there = (1 - group) * held
            temporal[:, pl.ds(aligned(group * held), held)] = local[...]
            temporal[:, pl.ds(aligned(there + core * part), part)] = mine[...]
            tail = mates[-1][sizes[-1] :].reshape(3, part, width)
            temporal[:, pl.ds(aligned(there + (1 - core) * part), part)] = tail

        for step in range(sum(sizes) // rows):

            @pl.when(i == step)
            def _():
                for j, there, here in block_spans(sizes, step, rows):
                    own[here], mate[here] = owns[j][there], mates[j][there]

        own_lines, mate_lines = (ref[...].reshape(count, depth) for ref in (own, mate))
    else:
        own_lines, mate_lines = (ref[here].reshape(count, depth) for ref in (own, mate))
    mate_tap, far_tap = 2 - 2 * core, 2 * core

    def matrix(tap, columns):
        return temporal[tap, :, columns]

    def spatial_rows(tap, columns):
        return spatial[0][tap, :, columns]

    def product(lines, taps, columns):
        return dot(jnp.concatenate(lines, axis=1), jnp.concatenate([matrix(tap, columns) for tap in taps], axis=0))

    def masked(lines):
        return jnp.where(present, lines, jnp.zeros_like(lines))

    def put(total, columns):
        total += temporal_bias[:, columns]
        out[:, :, columns] = total.astype(out.dtype).reshape(rows, breadth, -1)

    if given:
        lines = [own_lines, mate_lines, masked(far[here].reshape(count, depth))]
        for columns in halves(width):
            put(product(lines, (1, mate_tap, far_tap), columns), columns)
        return

    totals = [product([own_lines, mate_lines], (1, mate_tap), columns) for columns in halves(width)]

    @pl.when(i == 0)
    def _():
        for copy in second:
            copy.wait()

    far_lines = jnp.concatenate(
        [
            silu(
                rows_conv(far, spatial_rows, range(9), i * rows, rows, breadth, columns) + spatial_bias[:, columns]
            ).astype(far.dtype)
            for columns in halves(depth)
        ],
        axis=1,
    )
    far_lines = masked(far_lines)
    for total, columns in zip(totals, halves(width), strict=True):
        put(total + dot(far_lines, matrix(far_tap, columns)), columns)


def mix_call(shape, far, owns, mates, sizes, temporal_parts, spatial, biases, before, begin, rows, tiles, cost):
    height, breadth, width = shape
    dtype = far.dtype
    count, depth = sum(sizes), far.shape[2]
    given = before is not None
    operands = [*owns, *mates, far, *temporal_parts, *spatial]
    specs = [ANY] * len(operands)
    for n in range(len(operands)):
        if given or n != 2 * len(owns):
            specs[n] = IN_VMEM
            operands[n] = in_vmem(operands[n])
    out_shape = [jax.ShapeDtypeStruct(shape, dtype)]
    out_specs = [pl.BlockSpec((rows, breadth, width), lambda i: (i + begin // rows, 0, 0))]
    if not given:
        out_shape.append(pltpu.VMEM((3, depth, width), dtype))
        out_specs.append(IN_VMEM)
    return pl.pallas_call(
        functools.partial(mix_kernel, rows, begin, sizes, given, tiles),
        grid=(count // rows,),
        in_specs=specs + [IN_VMEM, IN_VMEM] + [ANY] * given,
        out_specs=out_specs,
        scratch_shapes=[
            pltpu.VMEM((16, 128) if given else (rows, breadth, depth), dtype),
            pltpu.VMEM((16, 128) if given else (rows, breadth, depth), dtype),
            pltpu.VMEM((16, 128) if given else (count + 2, breadth, depth), dtype),
            pltpu.SemaphoreType.DMA,
        ],
        out_shape=out_shape,
        input_output_aliases={len(operands) + 2: 0} if given else {},
        cost_estimate=cost,
        compiler_params=pltpu.CompilerParams(vmem_limit_bytes=40 * 2**20),
    )(*operands, *map(in_vmem, biases), *([before] if given else []))


def near_device(videos, spatial_filter, temporal_filter, spatial_bias, temporal_bias):
    shape = videos.shape[2:]
    height, breadth, channels = shape
    video = videos.reshape(shape)
    biases = [spatial_bias.reshape(1, -1), temporal_bias.reshape(1, -1)]
    tiles = lax.axis_size("tile")
    depth, width = spatial_filter.shape[1:]
    half = depth // 2
    swap = [(0, 1), (1, 0)]
    mates = [(i, i ^ 1) for i in range(tiles)]
    pairs = [(i, i ^ 4) for i in range(tiles)]
    across = [pair for i in range(1, tiles - 1, 2) for pair in ((i, i + 1), (i + 1, i))]
    light = pl.CostEstimate(flops=1000, bytes_accessed=1000, transcendentals=0)
    heavy = pl.CostEstimate(flops=10**12, bytes_accessed=1000, transcendentals=0)

    def mine(first, count):
        return lambda: (pl.ds(first, count), pl.ds(aligned(half_starts(depth)[0]), half))

    def relayed():
        return mine(middle + relay_starts(relay)[0], relay)()

    unit = height // 32
    blocks = tuple(unit * block for block in (8, 8, 8, 8))
    sent = height - blocks[-1] + 1
    taps = [(0, 3), (3, 2)]
    middle, relay = 5, 2
    cuts = [
        [(mine(first, count), (count, half, width)) for first, count in taps] + [(relayed, (relay, half, width))],
        [(mine(0, 3), (3, half, width))],
        [(lambda: (pl.ds(0, sent),), (sent, breadth, channels))],
    ]
    *cut, c_y, far = cut_call([spatial_filter, temporal_filter, video], cuts, light)
    far = lax.ppermute(far, "tile", across)
    fetched = [lax.ppermute(piece, "dp", swap) for piece in cut]

    def both(pieces):
        return [half for piece in pieces for half in (piece, lax.ppermute(piece, "tile", mates))]

    (base,) = conv_call(video, None, [spatial_filter], depth, range(9), 16, light)
    *early, base = lax.optimization_barrier((*fetched[:-1], base))
    early = both(early)
    base, padded = conv_call(video, base, early, depth, range(middle), 16, light)
    other = lax.ppermute(fetched[-1], "tile", pairs)
    *late, base = lax.optimization_barrier((fetched[-1], other, base))
    late = both(late)
    c_y = lax.ppermute(c_y, "dp", swap)
    tail = c_y.reshape(-1, breadth, width)
    parts = [spatial_filter, *early, *late]
    *own, spatial = own_call(padded, base, biases[0], tail, parts, range(middle, 9), 16, blocks, light)
    temporal_parts = [temporal_filter, c_y]

    last = lax.ppermute(own[-1], "tile", across)
    mate = [lax.ppermute(block, "tile", mates) for block in own]
    out, temporal = mix_call(
        shape, far, own[:-1], mate[:-1], blocks[:-1], temporal_parts, [spatial], biases, None, 0, 12, tiles, heavy
    )
    (out,) = mix_call(
        shape, last, own[-1:], mate[-1:], blocks[-1:], [temporal], [], biases, out, sent - 1, blocks[-1], tiles, light
    )
    return out.reshape(videos.shape)


def padded_2(block, sides, width):
    for axis, dim in sides:
        count = lax.axis_size(axis)
        forward = [(i, i + 1) for i in range(count - 1)]
        backward = [(target, source) for source, target in forward]
        low = lax.ppermute(
            lax.slice_in_dim(block, block.shape[dim] - width, None, axis=dim), axis, forward
        )
        high = lax.ppermute(lax.slice_in_dim(block, 0, width, axis=dim), axis, backward)
        block = jnp.concatenate([low, block, high], axis=dim)
    return block


def spatial_term(padded, weight_piece):
    width = weight_piece.shape[1]
    height = padded.shape[2] - 2
    breadth = padded.shape[3] - 2
    columns = jnp.concatenate(
        [
            padded[:, :, row_off : row_off + height, col_off : col_off + breadth, :]
            for row_off in range(3)
            for col_off in range(3)
        ],
        axis=4,
    )
    matrix = weight_piece.reshape(9 * width, weight_piece.shape[2])
    return jnp.dot(columns.reshape(-1, 9 * width), matrix, preferred_element_type=jnp.float32)


def temporal_term(framed, weight_piece):
    width = weight_piece.shape[1]
    frames = framed.shape[1] - 2
    columns = jnp.concatenate([framed[:, lag : lag + frames] for lag in range(3)], axis=4)
    matrix = weight_piece.reshape(3 * width, weight_piece.shape[2])
    return jnp.dot(columns.reshape(-1, 3 * width), matrix, preferred_element_type=jnp.float32)


def any_device(videos, spatial_filter, temporal_filter, spatial_bias, temporal_bias):
    samples, frames, height, breadth, channels = videos.shape
    padded = jnp.pad(videos, ((0, 0), (0, 0), (1, 1), (1, 1), (0, 0)))
    summed = spatial_term(padded, lax.all_gather(spatial_filter, "dp", axis=1, tiled=True))
    activated = jax.nn.silu(summed + spatial_bias).astype(jnp.bfloat16)
    hidden = activated.reshape(samples, frames, height, breadth, channels)
    framed = padded_2(hidden, (("tile", 1),), 1)
    result = temporal_term(framed, lax.all_gather(temporal_filter, "dp", axis=1, tiled=True))
    return (result + temporal_bias).astype(jnp.bfloat16).reshape(videos.shape)


def per_device(videos, spatial_filter, *rest):
    near = (
        videos.shape[0] == 1
        and videos.shape[1] == 1
        and videos.shape[2] % 32 == 0
        and spatial_filter.shape[1] % (2 * videos.shape[3]) == 0
        and lax.axis_size("dp") == 2
        and lax.axis_size("tile") % 8 == 0
    )
    return (near_device if near else any_device)(videos, spatial_filter, *rest)


def solution(mesh):
    return jax.shard_map(
        per_device,
        mesh=mesh,
        in_specs=(
            P("dp", "tile", None, None, None),
            P(None, "dp", None),
            P(None, "dp", None),
            P(),
            P(),
        ),
        out_specs=P("dp", "tile", None, None, None),
        check_vma=False,
    )
```

time: 62.1 us -> 61.6 us (level)
  Pallas kernels: 31.5 us -> 30.6 us
    pallas_call x5, Pallas kernels: 29.6 us -> 28.7 us  [the longest x2 15.2 us: mix_call(): pl.pallas_call(functools.partial(mix_kernel, rows, begin, sizes, given, t...]
  transfers between devices with their start and end apart: 15 -> 15, of which waited for: 5 -> 5; matrix products, arithmetic and copies ran while one was open for 0% -> 0% of each run, Pallas kernels for 43% -> 42%
where the time goes in v5:
time: 61.6 us; the launch traced here: 61 us
  Pallas kernels  30.6 us (50%)
  starting transfers between devices  19 us (31%)
  waiting for transfers between devices  7.76 us (13%)
  local copies, waits for them, and re-layouts  3.27 us (5%)
    pallas_call x2, Pallas kernels, mix_call(): pl.pallas_call(functools.partial(mix_kernel, rows, begin, sizes, given, t...  15.2 us
    pallas_call x2, Pallas kernels, conv_call(): pl.pallas_call(functools.partial(conv_kernel, rows, taps, held), grid=(st...  8.89 us
    pallas_call x1, Pallas kernels, own_call(): pl.pallas_call(functools.partial(own_kernel, rows, blocks, taps), in_spec...  4.67 us
    ppermute x1, starting transfers between devices, near_device(): far = lax.ppermute(far, 'tile', across)  4.51 us
    ppermute x4, starting transfers between devices, both(): lax.ppermute(piece, 'tile', mates)  4.5 us
    ppermute x3, starting transfers between devices, near_device(): fetched = [lax.ppermute(piece, 'dp', swap) for piece in cut]  3.6 us
    ppermute x3, waiting for transfers between devices, near_device(): fetched = [lax.ppermute(piece, 'dp', swap) for piece in cut]  3.56 us
    unnamed x12, local copies, waits for them, and re-layouts  3.27 us
  transfers between devices with their start and end apart: 15, of which 5 were waited for; matrix products, arithmetic and copies ran while one was open for 0% of the time, Pallas kernels for 42%

profile of v5, /device:TPU:1, one launch (start us, length us, event | category | flops | bytes accessed | tf_op | source)
XLA Modules:
  0.0 61.0 jit_solution(907407107286474467)
XLA Ops:
  0.0 1.9 %shard_map.55 = (bf16[3,128,512]{2,1,0:T(8,128)(2,1)S(1)}, bf16[2,128,512]{2,1,0:T(8,128)(2,1)S(1)}, bf16[2,128,512]{2,1,0:T(8,128)(2,1)S(1)}, bf16[3,128,512]{2,1,0:T(8,128)(2,1)S(1)}, bf16[25,64,512]{2,1,0:T(8,128)(2,1)S(1)}) custom-call(bf16[9,256,512]{2,1,0:T(8,128)(2,1)} %refs_0_.5, bf16[3,256,512]{2,1,0:T(8,128)(2,1)} %refs_7_.1, ...), custom_call_target="tpu_custom_call" | custom-call | flops 1000 | bytes 1000 | tf_op jit(solution)/shard_map/pallas_call | solution.py:80
  1.9 2.1 %collective-permute-start = (bf16[3,128,512]{2,1,0:T(8,128)(2,1)S(1)}, bf16[3,128,512]{2,1,0:T(8,128)(2,1)S(1)}, u32[]{:S(2)}, u32[]{:S(2)}) collective-permute-start(bf16[3,128,512]{2,1,0:T(8,128)(2,1)S(1)} %get-tuple-element.25), channel_id=1, source_target_pairs={{0,16},{16,0},{1,17},{17,1},{2,18},{18,2},{3,19},{19,3},{4,20},{20... | collective-permute-start | bytes 1179656 | tf_op jit(solution)/shard_map/ppermute | solution.py:426
  4.0 0.1 collective-permute-start.1
  4.1 1.4 %collective-permute-start.4 = (bf16[2,128,512]{2,1,0:T(8,128)(2,1)S(1)}, bf16[2,128,512]{2,1,0:T(8,128)(2,1)S(1)}, u32[]{:S(2)}, u32[]{:S(2)}) collective-permute-start(bf16[2,128,512]{2,1,0:T(8,128)(2,1)S(1)} %get-tuple-element.31), channel_id=1, source_target_pairs={{0,16},{16,0},{1,17},{17,1},{2,18},{18,2},{3,19},{19,3},{4,20},{20... | collective-permute-start | bytes 786440 | tf_op jit(solution)/shard_map/ppermute | solution.py:426
  5.5 4.5 %collective-permute-start.14 = (bf16[25,64,512]{2,1,0:T(8,128)(2,1)S(1)}, bf16[25,64,512]{2,1,0:T(8,128)(2,1)S(1)}, u32[]{:S(2)}, u32[]{:S(2)}) collective-permute-start(bf16[25,64,512]{2,1,0:T(8,128)(2,1)S(1)} %get-tuple-element.41), channel_id=1, source_target_pairs={{1,2},{2,1},{3,4},{4,3},{5,6},{6,5},{7,8},{8,7},{9,10},{10,9},{11,... | collective-permute-start | bytes 4915208 | tf_op jit(solution)/shard_map/ppermute | solution.py:425
  10.0 0.0 copy-start
  10.0 1.7 %copy-done = bf16[9,256,512]{2,1,0:T(8,128)(2,1)S(1)} copy-done((bf16[9,256,512]{2,1,0:T(8,128)(2,1)S(1)}, bf16[9,256,512]{2,1,0:T(8,128)(2,1)}, u32[]{:S(2)}) %copy-start) | copy-done | bytes 2359320
  11.7 0.0 copy-start.2
  11.7 1.6 %copy-done.2 = bf16[1,1,32,64,512]{4,3,2,1,0:T(8,128)(2,1)S(1)} copy-done((bf16[1,1,32,64,512]{4,3,2,1,0:T(8,128)(2,1)S(1)}, bf16[1,1,32,64,512]{4,3,2,1,0:T(8,128)(2,1)}, u32[]{:S(2)}) %copy-start.2) | copy-done | bytes 2097176
  13.3 5.5 %shard_map.56.refs_0_ = f32[32,64,512]{2,1,0:T(8,128)S(1)} custom-call(bf16[32,64,512]{2,1,0:T(8,128)(2,1)S(1)} %bitcast.6, bf16[9,256,512]{2,1,0:T(8,128)(2,1)S(1)} %copy-done), custom_call_target="tpu_custom_call" | custom-call | flops 1000 | bytes 1000 | tf_op jit(solution)/shard_map/pallas_call | solution.py:170
  18.8 0.0 collective-permute-done.1.refs_3_
  18.8 0.0 collective-permute-done.refs_1_
  18.8 1.7 %collective-permute-start.2 = (bf16[3,128,512]{2,1,0:T(8,128)(2,1)S(1)}, bf16[3,128,512]{2,1,0:T(8,128)(2,1)S(1)}, u32[]{:S(2)}, u32[]{:S(2)}) collective-permute-start(bf16[3,128,512]{2,1,0:T(8,128)(2,1)S(1)} %collective-permute-done.refs_1_), channel_id=1, source_target_pairs={{0,1},{1,0},{2,3},{3,2},{4,5},{5,4},{6,7},{7,6},{8,9},{9,8},{10,11... | collective-permute-start | bytes 1179656 | tf_op jit(solution)/shard_map/ppermute | solution.py:429
  20.5 0.0 collective-permute-start.3
  20.5 3.6 %collective-permute-done.4.refs_5_ = bf16[2,128,512]{2,1,0:T(8,128)(2,1)S(1)} collective-permute-done((bf16[2,128,512]{2,1,0:T(8,128)(2,1)S(1)}, bf16[2,128,512]{2,1,0:T(8,128)(2,1)S(1)}, u32[]{:S(2)}, u32[]{:S(2)}) %collective-permute-start.4) | collective-permute-done | bytes 262176 | tf_op jit(solution)/shard_map/ppermute | solution.py:426
  24.1 1.2 %collective-permute-start.5 = (bf16[2,128,512]{2,1,0:T(8,128)(2,1)S(1)}, bf16[2,128,512]{2,1,0:T(8,128)(2,1)S(1)}, u32[]{:S(2)}, u32[]{:S(2)}) collective-permute-start(bf16[2,128,512]{2,1,0:T(8,128)(2,1)S(1)} %collective-permute-done.4.refs_5_), channel_id=1, source_target_pairs={{0,4},{1,5},{2,6},{3,7},{4,0},{5,1},{6,2},{7,3},{8,12},{9,13},{10,... | collective-permute-start | bytes 786440 | tf_op jit(solution)/shard_map/ppermute | solution.py:435
  25.3 0.0 copy-start.1
  25.3 0.0 copy-start.4
  25.3 1.2 %collective-permute-start.6 = (bf16[3,128,512]{2,1,0:T(8,128)(2,1)S(1)}, bf16[3,128,512]{2,1,0:T(8,128)(2,1)S(1)}, u32[]{:S(2)}, u32[]{:S(2)}) collective-permute-start(bf16[3,128,512]{2,1,0:T(8,128)(2,1)S(1)} %get-tuple-element.34), channel_id=1, source_target_pairs={{0,16},{16,0},{1,17},{17,1},{2,18},{18,2},{3,19},{19,3},{4,20},{20... | collective-permute-start | bytes 1179656 | tf_op jit(solution)/shard_map/ppermute | solution.py:438
  26.5 0.0 collective-permute-done.3.refs_4_
  26.5 0.0 collective-permute-done.2.refs_2_
  26.6 3.4 %shard_map.57 = (f32[32,64,512]{2,1,0:T(8,128)S(1)}, bf16[34,64,256]{2,1,0:T(8,128)(2,1)S(1)}) custom-call(bf16[32,64,512]{2,1,0:T(8,128)(2,1)S(1)} %bitcast.7, f32[32,64,512]{2,1,0:T(8,128)S(1)} %shard_map.56.refs_0_, bf16[3,128,512]{2,1,0:T(8,128)(2,1)S(1)} %collective-permute-done.refs_1_, bf16[3,128,512]{2,1,0:T(8,128)(2,1)S(1)} %collective-permute-done.2.refs_2_, ...), custom_call_target="tpu_custom_call" | custom-call | flops 1000 | bytes 1000 | tf_op jit(solution)/shard_map/pallas_call | solution.py:170
  29.9 2.5 %collective-permute-done.5.refs_7_ = bf16[2,128,512]{2,1,0:T(8,128)(2,1)S(1)} collective-permute-done((bf16[2,128,512]{2,1,0:T(8,128)(2,1)S(1)}, bf16[2,128,512]{2,1,0:T(8,128)(2,1)S(1)}, u32[]{:S(2)}, u32[]{:S(2)}) %collective-permute-start.5) | collective-permute-done | bytes 262176 | tf_op jit(solution)/shard_map/ppermute | solution.py:435
  32.5 2.7 %collective-permute-start.7 = (bf16[2,128,512]{2,1,0:T(8,128)(2,1)S(1)}, bf16[2,128,512]{2,1,0:T(8,128)(2,1)S(1)}, u32[]{:S(2)}, u32[]{:S(2)}) collective-permute-start(bf16[2,128,512]{2,1,0:T(8,128)(2,1)S(1)} %collective-permute-done.4.refs_5_), channel_id=1, source_target_pairs={{0,1},{1,0},{2,3},{3,2},{4,5},{5,4},{6,7},{7,6},{8,9},{9,8},{10,11... | collective-permute-start | bytes 786440 | tf_op jit(solution)/shard_map/ppermute | solution.py:429
  35.2 0.0 collective-permute-start.8
  35.2 0.0 collective-permute-done.6.refs_8_
  35.2 1.2 %collective-permute-done.7.refs_6_ = bf16[2,128,512]{2,1,0:T(8,128)(2,1)S(1)} collective-permute-done((bf16[2,128,512]{2,1,0:T(8,128)(2,1)S(1)}, bf16[2,128,512]{2,1,0:T(8,128)(2,1)S(1)}, u32[]{:S(2)}, u32[]{:S(2)}) %collective-permute-start.7) | collective-permute-done | bytes 262176 | tf_op jit(solution)/shard_map/ppermute | solution.py:429
  36.4 0.4 collective-permute-done.8.refs_8_
  36.8 0.0 copy-done.1
  36.8 0.0 copy-done.4
  36.8 0.0 copy-start.3
  36.8 0.0 copy-start.5
  36.8 4.7 %shard_map.58 = (bf16[8,64,512]{2,1,0:T(8,128)(2,1)S(1)}, bf16[8,64,512]{2,1,0:T(8,128)(2,1)S(1)}, bf16[14,64,512]{2,1,0:T(8,128)(2,1)S(1)}, bf16[8,64,512]{2,1,0:T(8,128)(2,1)}, bf16[9,512,512]{2,1,0:T(8,128)(2,1)S(1)}) custom-call(bf16[34,64,256]{2,1,0:T(8,128)(2,1)S(1)} %get-tuple-element.30.padded, f32[32,64,512]{2,1,0:T(8,128)S(1)} %get-tuple-element.33.base, ...), custom_call_target="tpu_custom_call" | custom-call | flops 1000 | bytes 1000 | tf_op jit(solution)/shard_map/pallas_call | solution.py:240
  41.5 0.4 collective-permute-start.13
  41.9 0.1 collective-permute-start.11
  42.0 0.4 collective-permute-start.12
  42.4 3.0 %collective-permute-start.10 = (bf16[8,64,512]{2,1,0:T(8,128)(2,1)}, bf16[8,64,512]{2,1,0:T(8,128)(2,1)}, u32[]{:S(2)}, u32[]{:S(2)}) collective-permute-start(bf16[8,64,512]{2,1,0:T(8,128)(2,1)} %get-tuple-element.37.refs_0_), channel_id=1, source_target_pairs={{1,2},{2,1},{3,4},{4,3},{5,6},{6,5},{7,8},{8,7},{9,10},{10,9},{11,... | collective-permute-start | bytes 1572872 | tf_op jit(solution)/shard_map/ppermute | solution.py:444
  45.4 0.0 collective-permute-done.11.refs_3_
  45.4 0.1 collective-permute-start.9
  45.5 0.0 collective-permute-done.12.refs_4_
  45.5 0.1 collective-permute-done.14.refs_6_
  45.6 0.0 collective-permute-done.13.refs_5_
  45.6 0.0 copy-done.3
  45.6 0.0 copy-done.5
  45.6 12.0 %shard_map.59 = (bf16[32,64,512]{2,1,0:T(8,128)(2,1)}, bf16[3,512,512]{2,1,0:T(8,128)(2,1)S(1)}) custom-call(bf16[8,64,512]{2,1,0:T(8,128)(2,1)S(1)} %get-tuple-element.38.refs_0_, bf16[8,64,512]{2,1,0:T(8,128)(2,1)S(1)} %get-tuple-element.39.refs_1_, bf16[14,64,512]{2,1,0:T(8,128)(2,1)S(1)} %get-tuple-element.40.refs_2_, ...), custom_call_target="tpu_custom_call" | custom-call | flops 999999995904 | bytes 1000 | tf_op jit(solution)/shard_map/pallas_call | solution.py:375
  57.6 0.0 collective-permute-done.10.refs_2_
  57.6 0.0 collective-permute-done.9.refs_1_
  57.7 3.1 %shard_map.60 = bf16[32,64,512]{2,1,0:T(8,128)(2,1)} custom-call(bf16[8,64,512]{2,1,0:T(8,128)(2,1)} %get-tuple-element.37.refs_0_, bf16[8,64,512]{2,1,0:T(8,128)(2,1)} %collective-permute-done.9.refs_1_, bf16[8,64,512]{2,1,0:T(8,128)(2,1)} %collective-permute-done.10.refs_2_, ...), custom_call_target="tpu_custom_call", output_to_operand_aliasing={{}: (6, {})} | custom-call | flops 1000 | bytes 1000 | tf_op jit(solution)/shard_map/pallas_call | solution.py:375
Async XLA Ops:
  1.9 16.9 %collective-permute-start = (bf16[3,128,512]{2,1,0:T(8,128)(2,1)S(1)}, bf16[3,128,512]{2,1,0:T(8,128)(2,1)S(1)}, u32[]{:S(2)}, u32[]{:S(2)}) collective-permute-start(bf16[3,128,512]{2,1,0:T(8,128)(2,1)S(1)} %get-tuple-element.25), channel_id=1, source_target_pairs={{0,16},{16,0},{1,17},{17,1},{2,18},{18,2},{3,19},{19,3},{4,20},{20... | collective-permute-start | bytes 1179656 | tf_op jit(solution)/shard_map/ppermute | solution.py:426
  4.0 14.8 %collective-permute-start.1 = (bf16[2,128,512]{2,1,0:T(8,128)(2,1)S(1)}, bf16[2,128,512]{2,1,0:T(8,128)(2,1)S(1)}, u32[]{:S(2)}, u32[]{:S(2)}) collective-permute-start(bf16[2,128,512]{2,1,0:T(8,128)(2,1)S(1)} %get-tuple-element.26), channel_id=1, source_target_pairs={{0,16},{16,0},{1,17},{17,1},{2,18},{18,2},{3,19},{19,3},{4,20},{20... | collective-permute-start | bytes 786440 | tf_op jit(solution)/shard_map/ppermute | solution.py:426
  4.1 20.0 %collective-permute-start.4 = (bf16[2,128,512]{2,1,0:T(8,128)(2,1)S(1)}, bf16[2,128,512]{2,1,0:T(8,128)(2,1)S(1)}, u32[]{:S(2)}, u32[]{:S(2)}) collective-permute-start(bf16[2,128,512]{2,1,0:T(8,128)(2,1)S(1)} %get-tuple-element.31), channel_id=1, source_target_pairs={{0,16},{16,0},{1,17},{17,1},{2,18},{18,2},{3,19},{19,3},{4,20},{20... | collective-permute-start | bytes 786440 | tf_op jit(solution)/shard_map/ppermute | solution.py:426
  5.5 40.1 %collective-permute-start.14 = (bf16[25,64,512]{2,1,0:T(8,128)(2,1)S(1)}, bf16[25,64,512]{2,1,0:T(8,128)(2,1)S(1)}, u32[]{:S(2)}, u32[]{:S(2)}) collective-permute-start(bf16[25,64,512]{2,1,0:T(8,128)(2,1)S(1)} %get-tuple-element.41), channel_id=1, source_target_pairs={{1,2},{2,1},{3,4},{4,3},{5,6},{6,5},{7,8},{8,7},{9,10},{10,9},{11,... | collective-permute-start | bytes 4915208 | tf_op jit(solution)/shard_map/ppermute | solution.py:425
  10.0 1.7 %copy-start = (bf16[9,256,512]{2,1,0:T(8,128)(2,1)S(1)}, bf16[9,256,512]{2,1,0:T(8,128)(2,1)}, u32[]{:S(2)}) copy-start(bf16[9,256,512]{2,1,0:T(8,128)(2,1)} %refs_0_.5) | copy-start | bytes 7077892
  11.7 1.6 %copy-start.2 = (bf16[1,1,32,64,512]{4,3,2,1,0:T(8,128)(2,1)S(1)}, bf16[1,1,32,64,512]{4,3,2,1,0:T(8,128)(2,1)}, u32[]{:S(2)}) copy-start(bf16[1,1,32,64,512]{4,3,2,1,0:T(8,128)(2,1)} %param.5) | copy-start | bytes 6291460
  18.8 7.8 %collective-permute-start.2 = (bf16[3,128,512]{2,1,0:T(8,128)(2,1)S(1)}, bf16[3,128,512]{2,1,0:T(8,128)(2,1)S(1)}, u32[]{:S(2)}, u32[]{:S(2)}) collective-permute-start(bf16[3,128,512]{2,1,0:T(8,128)(2,1)S(1)} %collective-permute-done.refs_1_), channel_id=1, source_target_pairs={{0,1},{1,0},{2,3},{3,2},{4,5},{5,4},{6,7},{7,6},{8,9},{9,8},{10,11... | collective-permute-start | bytes 1179656 | tf_op jit(solution)/shard_map/ppermute | solution.py:429
  20.5 6.0 %collective-permute-start.3 = (bf16[2,128,512]{2,1,0:T(8,128)(2,1)S(1)}, bf16[2,128,512]{2,1,0:T(8,128)(2,1)S(1)}, u32[]{:S(2)}, u32[]{:S(2)}) collective-permute-start(bf16[2,128,512]{2,1,0:T(8,128)(2,1)S(1)} %collective-permute-done.1.refs_3_), channel_id=1, source_target_pairs={{0,1},{1,0},{2,3},{3,2},{4,5},{5,4},{6,7},{7,6},{8,9},{9,8},{10,11... | collective-permute-start | bytes 786440 | tf_op jit(solution)/shard_map/ppermute | solution.py:429
  24.1 8.4 %collective-permute-start.5 = (bf16[2,128,512]{2,1,0:T(8,128)(2,1)S(1)}, bf16[2,128,512]{2,1,0:T(8,128)(2,1)S(1)}, u32[]{:S(2)}, u32[]{:S(2)}) collective-permute-start(bf16[2,128,512]{2,1,0:T(8,128)(2,1)S(1)} %collective-permute-done.4.refs_5_), channel_id=1, source_target_pairs={{0,4},{1,5},{2,6},{3,7},{4,0},{5,1},{6,2},{7,3},{8,12},{9,13},{10,... | collective-permute-start | bytes 786440 | tf_op jit(solution)/shard_map/ppermute | solution.py:435
  25.3 11.5 %copy-start.1 = (bf16[9,256,512]{2,1,0:T(8,128)(2,1)S(1)}, bf16[9,256,512]{2,1,0:T(8,128)(2,1)}, u32[]{:S(2)}) copy-start(bf16[9,256,512]{2,1,0:T(8,128)(2,1)} %refs_0_.5) | copy-start | bytes 7077892
  25.3 11.5 %copy-start.4 = (f32[512]{0:T(512)S(1)}, f32[512]{0:T(512)}, u32[]{:S(2)}) copy-start(f32[512]{0:T(512)} %param.8) | copy-start | bytes 6148
  25.3 9.9 %collective-permute-start.6 = (bf16[3,128,512]{2,1,0:T(8,128)(2,1)S(1)}, bf16[3,128,512]{2,1,0:T(8,128)(2,1)S(1)}, u32[]{:S(2)}, u32[]{:S(2)}) collective-permute-start(bf16[3,128,512]{2,1,0:T(8,128)(2,1)S(1)} %get-tuple-element.34), channel_id=1, source_target_pairs={{0,16},{16,0},{1,17},{17,1},{2,18},{18,2},{3,19},{19,3},{4,20},{20... | collective-permute-start | bytes 1179656 | tf_op jit(solution)/shard_map/ppermute | solution.py:438
  32.5 3.9 %collective-permute-start.7 = (bf16[2,128,512]{2,1,0:T(8,128)(2,1)S(1)}, bf16[2,128,512]{2,1,0:T(8,128)(2,1)S(1)}, u32[]{:S(2)}, u32[]{:S(2)}) collective-permute-start(bf16[2,128,512]{2,1,0:T(8,128)(2,1)S(1)} %collective-permute-done.4.refs_5_), channel_id=1, source_target_pairs={{0,1},{1,0},{2,3},{3,2},{4,5},{5,4},{6,7},{7,6},{8,9},{9,8},{10,11... | collective-permute-start | bytes 786440 | tf_op jit(solution)/shard_map/ppermute | solution.py:429
  35.2 1.5 %collective-permute-start.8 = (bf16[2,128,512]{2,1,0:T(8,128)(2,1)S(1)}, bf16[2,128,512]{2,1,0:T(8,128)(2,1)S(1)}, u32[]{:S(2)}, u32[]{:S(2)}) collective-permute-start(bf16[2,128,512]{2,1,0:T(8,128)(2,1)S(1)} %collective-permute-done.5.refs_7_), channel_id=1, source_target_pairs={{0,1},{1,0},{2,3},{3,2},{4,5},{5,4},{6,7},{7,6},{8,9},{9,8},{10,11... | collective-permute-start | bytes 786440 | tf_op jit(solution)/shard_map/ppermute | solution.py:429
  36.8 8.8 %copy-start.3 = (bf16[3,256,512]{2,1,0:T(8,128)(2,1)S(1)}, bf16[3,256,512]{2,1,0:T(8,128)(2,1)}, u32[]{:S(2)}) copy-start(bf16[3,256,512]{2,1,0:T(8,128)(2,1)} %refs_7_.1) | copy-start | bytes 2359300
  36.8 8.8 %copy-start.5 = (f32[512]{0:T(512)S(1)}, f32[512]{0:T(512)}, u32[]{:S(2)}) copy-start(f32[512]{0:T(512)} %param.9) | copy-start | bytes 6148
  41.5 4.1 %collective-permute-start.13 = (bf16[14,64,512]{2,1,0:T(8,128)(2,1)S(1)}, bf16[14,64,512]{2,1,0:T(8,128)(2,1)S(1)}, u32[]{:S(2)}, u32[]{:S(2)}) collective-permute-start(bf16[14,64,512]{2,1,0:T(8,128)(2,1)S(1)} %get-tuple-element.40.refs_2_), channel_id=1, source_target_pairs={{0,1},{1,0},{2,3},{3,2},{4,5},{5,4},{6,7},{7,6},{8,9},{9,8},{10,11... | collective-permute-start | bytes 2752520 | tf_op jit(solution)/shard_map/ppermute | solution.py:445
  41.9 3.5 %collective-permute-start.11 = (bf16[8,64,512]{2,1,0:T(8,128)(2,1)S(1)}, bf16[8,64,512]{2,1,0:T(8,128)(2,1)S(1)}, u32[]{:S(2)}, u32[]{:S(2)}) collective-permute-start(bf16[8,64,512]{2,1,0:T(8,128)(2,1)S(1)} %get-tuple-element.38.refs_0_), channel_id=1, source_target_pairs={{0,1},{1,0},{2,3},{3,2},{4,5},{5,4},{6,7},{7,6},{8,9},{9,8},{10,11... | collective-permute-start | bytes 1572872 | tf_op jit(solution)/shard_map/ppermute | solution.py:445
  42.0 3.5 %collective-permute-start.12 = (bf16[8,64,512]{2,1,0:T(8,128)(2,1)S(1)}, bf16[8,64,512]{2,1,0:T(8,128)(2,1)S(1)}, u32[]{:S(2)}, u32[]{:S(2)}) collective-permute-start(bf16[8,64,512]{2,1,0:T(8,128)(2,1)S(1)} %get-tuple-element.39.refs_1_), channel_id=1, source_target_pairs={{0,1},{1,0},{2,3},{3,2},{4,5},{5,4},{6,7},{7,6},{8,9},{9,8},{10,11... | collective-permute-start | bytes 1572872 | tf_op jit(solution)/shard_map/ppermute | solution.py:445
  42.4 15.2 %collective-permute-start.10 = (bf16[8,64,512]{2,1,0:T(8,128)(2,1)}, bf16[8,64,512]{2,1,0:T(8,128)(2,1)}, u32[]{:S(2)}, u32[]{:S(2)}) collective-permute-start(bf16[8,64,512]{2,1,0:T(8,128)(2,1)} %get-tuple-element.37.refs_0_), channel_id=1, source_target_pairs={{1,2},{2,1},{3,4},{4,3},{5,6},{6,5},{7,8},{8,7},{9,10},{10,9},{11,... | collective-permute-start | bytes 1572872 | tf_op jit(solution)/shard_map/ppermute | solution.py:444
  45.4 12.2 %collective-permute-start.9 = (bf16[8,64,512]{2,1,0:T(8,128)(2,1)}, bf16[8,64,512]{2,1,0:T(8,128)(2,1)}, u32[]{:S(2)}, u32[]{:S(2)}) collective-permute-start(bf16[8,64,512]{2,1,0:T(8,128)(2,1)} %get-tuple-element.37.refs_0_), channel_id=1, source_target_pairs={{0,1},{1,0},{2,3},{3,2},{4,5},{5,4},{6,7},{7,6},{8,9},{9,8},{10,11... | collective-permute-start | bytes 1572872 | tf_op jit(solution)/shard_map/ppermute | solution.py:445

commit v6 on v5

--- a/solution.py
+++ b/solution.py
@@ -412,7 +412,7 @@
         return mine(middle + relay_starts(relay)[0], relay)()
 
     unit = height // 32
-    blocks = tuple(unit * block for block in (8, 8, 8, 8))
+    blocks = tuple(unit * block for block in (9, 9, 6, 8))
     sent = height - blocks[-1] + 1
     taps = [(0, 3), (3, 2)]
     middle, relay = 5, 2

time: 61.6 us -> 61.6 us (level)
    ppermute x4, starting transfers between devices: 4.5 us -> 3.44 us  [both(): lax.ppermute(piece, 'tile', mates)]
    ppermute x4, starting transfers between devices: 1.02 us -> 2.02 us  [near_device(): mate = [lax.ppermute(block, 'tile', mates) for block in own]]
where the time goes in v6:
time: 61.6 us; the launch traced here: 60.9 us
  Pallas kernels  30.6 us (50%)
  starting transfers between devices  19 us (31%)
  waiting for transfers between devices  7.65 us (12%)
  local copies, waits for them, and re-layouts  3.27 us (5%)
    pallas_call x2, Pallas kernels, mix_call(): pl.pallas_call(functools.partial(mix_kernel, rows, begin, sizes, given, t...  15.2 us
    pallas_call x2, Pallas kernels, conv_call(): pl.pallas_call(functools.partial(conv_kernel, rows, taps, held), grid=(st...  8.89 us
    pallas_call x1, Pallas kernels, own_call(): pl.pallas_call(functools.partial(own_kernel, rows, blocks, taps), in_spec...  4.67 us
    ppermute x1, starting transfers between devices, near_device(): far = lax.ppermute(far, 'tile', across)  4.38 us
    ppermute x3, waiting for transfers between devices, near_device(): fetched = [lax.ppermute(piece, 'dp', swap) for piece in cut]  3.56 us
    ppermute x3, starting transfers between devices, near_device(): fetched = [lax.ppermute(piece, 'dp', swap) for piece in cut]  3.52 us
    ppermute x4, starting transfers between devices, both(): lax.ppermute(piece, 'tile', mates)  3.44 us
    unnamed x12, local copies, waits for them, and re-layouts  3.27 us
  transfers between devices with their start and end apart: 15, of which 5 were waited for; matrix products, arithmetic and copies ran while one was open for 0% of the time, Pallas kernels for 42%

profile of v6, /device:TPU:1, one launch (start us, length us, event | category | flops | bytes accessed | tf_op | source)
XLA Modules:
  0.0 60.9 jit_solution(10906238472864752074)
XLA Ops:
  0.0 1.9 %shard_map.55 = (bf16[3,128,512]{2,1,0:T(8,128)(2,1)S(1)}, bf16[2,128,512]{2,1,0:T(8,128)(2,1)S(1)}, bf16[2,128,512]{2,1,0:T(8,128)(2,1)S(1)}, bf16[3,128,512]{2,1,0:T(8,128)(2,1)S(1)}, bf16[25,64,512]{2,1,0:T(8,128)(2,1)S(1)}) custom-call(bf16[9,256,512]{2,1,0:T(8,128)(2,1)} %refs_0_.5, bf16[3,256,512]{2,1,0:T(8,128)(2,1)} %refs_7_.1, ...), custom_call_target="tpu_custom_call" | custom-call | flops 1000 | bytes 1000 | tf_op jit(solution)/shard_map/pallas_call | solution.py:80
  1.9 2.1 %collective-permute-start = (bf16[3,128,512]{2,1,0:T(8,128)(2,1)S(1)}, bf16[3,128,512]{2,1,0:T(8,128)(2,1)S(1)}, u32[]{:S(2)}, u32[]{:S(2)}) collective-permute-start(bf16[3,128,512]{2,1,0:T(8,128)(2,1)S(1)} %get-tuple-element.25), channel_id=1, source_target_pairs={{0,16},{16,0},{1,17},{17,1},{2,18},{18,2},{3,19},{19,3},{4,20},{20... | collective-permute-start | bytes 1179656 | tf_op jit(solution)/shard_map/ppermute | solution.py:426
  4.0 0.1 collective-permute-start.1
  4.1 4.4 %collective-permute-start.14 = (bf16[25,64,512]{2,1,0:T(8,128)(2,1)S(1)}, bf16[25,64,512]{2,1,0:T(8,128)(2,1)S(1)}, u32[]{:S(2)}, u32[]{:S(2)}) collective-permute-start(bf16[25,64,512]{2,1,0:T(8,128)(2,1)S(1)} %get-tuple-element.41), channel_id=1, source_target_pairs={{1,2},{2,1},{3,4},{4,3},{5,6},{6,5},{7,8},{8,7},{9,10},{10,9},{11,... | collective-permute-start | bytes 4915208 | tf_op jit(solution)/shard_map/ppermute | solution.py:425
  8.5 1.3 %collective-permute-start.4 = (bf16[2,128,512]{2,1,0:T(8,128)(2,1)S(1)}, bf16[2,128,512]{2,1,0:T(8,128)(2,1)S(1)}, u32[]{:S(2)}, u32[]{:S(2)}) collective-permute-start(bf16[2,128,512]{2,1,0:T(8,128)(2,1)S(1)} %get-tuple-element.31), channel_id=1, source_target_pairs={{0,16},{16,0},{1,17},{17,1},{2,18},{18,2},{3,19},{19,3},{4,20},{20... | collective-permute-start | bytes 786440 | tf_op jit(solution)/shard_map/ppermute | solution.py:426
  9.8 0.0 copy-start
  9.8 1.7 %copy-done = bf16[9,256,512]{2,1,0:T(8,128)(2,1)S(1)} copy-done((bf16[9,256,512]{2,1,0:T(8,128)(2,1)S(1)}, bf16[9,256,512]{2,1,0:T(8,128)(2,1)}, u32[]{:S(2)}) %copy-start) | copy-done | bytes 2359320
  11.5 0.0 copy-start.2
  11.5 1.6 %copy-done.2 = bf16[1,1,32,64,512]{4,3,2,1,0:T(8,128)(2,1)S(1)} copy-done((bf16[1,1,32,64,512]{4,3,2,1,0:T(8,128)(2,1)S(1)}, bf16[1,1,32,64,512]{4,3,2,1,0:T(8,128)(2,1)}, u32[]{:S(2)}) %copy-start.2) | copy-done | bytes 2097176
  13.1 5.5 %shard_map.56.refs_0_ = f32[32,64,512]{2,1,0:T(8,128)S(1)} custom-call(bf16[32,64,512]{2,1,0:T(8,128)(2,1)S(1)} %bitcast.6, bf16[9,256,512]{2,1,0:T(8,128)(2,1)S(1)} %copy-done), custom_call_target="tpu_custom_call" | custom-call | flops 1000 | bytes 1000 | tf_op jit(solution)/shard_map/pallas_call | solution.py:170
  18.6 0.0 collective-permute-done.1.refs_3_
  18.6 0.0 collective-permute-done.refs_1_
  18.6 2.0 %collective-permute-start.2 = (bf16[3,128,512]{2,1,0:T(8,128)(2,1)S(1)}, bf16[3,128,512]{2,1,0:T(8,128)(2,1)S(1)}, u32[]{:S(2)}, u32[]{:S(2)}) collective-permute-start(bf16[3,128,512]{2,1,0:T(8,128)(2,1)S(1)} %collective-permute-done.refs_1_), channel_id=1, source_target_pairs={{0,1},{1,0},{2,3},{3,2},{4,5},{5,4},{6,7},{7,6},{8,9},{9,8},{10,11... | collective-permute-start | bytes 1179656 | tf_op jit(solution)/shard_map/ppermute | solution.py:429
  20.5 0.0 collective-permute-start.3
  20.5 3.6 %collective-permute-done.4.refs_5_ = bf16[2,128,512]{2,1,0:T(8,128)(2,1)S(1)} collective-permute-done((bf16[2,128,512]{2,1,0:T(8,128)(2,1)S(1)}, bf16[2,128,512]{2,1,0:T(8,128)(2,1)S(1)}, u32[]{:S(2)}, u32[]{:S(2)}) %collective-permute-start.4) | collective-permute-done | bytes 262176 | tf_op jit(solution)/shard_map/ppermute | solution.py:426
  24.1 1.2 %collective-permute-start.5 = (bf16[2,128,512]{2,1,0:T(8,128)(2,1)S(1)}, bf16[2,128,512]{2,1,0:T(8,128)(2,1)S(1)}, u32[]{:S(2)}, u32[]{:S(2)}) collective-permute-start(bf16[2,128,512]{2,1,0:T(8,128)(2,1)S(1)} %collective-permute-done.4.refs_5_), channel_id=1, source_target_pairs={{0,4},{1,5},{2,6},{3,7},{4,0},{5,1},{6,2},{7,3},{8,12},{9,13},{10,... | collective-permute-start | bytes 786440 | tf_op jit(solution)/shard_map/ppermute | solution.py:435
  25.3 0.0 copy-start.1
  25.3 0.0 copy-start.4
  25.3 1.2 %collective-permute-start.6 = (bf16[3,128,512]{2,1,0:T(8,128)(2,1)S(1)}, bf16[3,128,512]{2,1,0:T(8,128)(2,1)S(1)}, u32[]{:S(2)}, u32[]{:S(2)}) collective-permute-start(bf16[3,128,512]{2,1,0:T(8,128)(2,1)S(1)} %get-tuple-element.34), channel_id=1, source_target_pairs={{0,16},{16,0},{1,17},{17,1},{2,18},{18,2},{3,19},{19,3},{4,20},{20... | collective-permute-start | bytes 1179656 | tf_op jit(solution)/shard_map/ppermute | solution.py:438
  26.5 0.0 collective-permute-done.3.refs_4_
  26.5 0.0 collective-permute-done.2.refs_2_
  26.6 3.4 %shard_map.57 = (f32[32,64,512]{2,1,0:T(8,128)S(1)}, bf16[34,64,256]{2,1,0:T(8,128)(2,1)S(1)}) custom-call(bf16[32,64,512]{2,1,0:T(8,128)(2,1)S(1)} %bitcast.7, f32[32,64,512]{2,1,0:T(8,128)S(1)} %shard_map.56.refs_0_, bf16[3,128,512]{2,1,0:T(8,128)(2,1)S(1)} %collective-permute-done.refs_1_, bf16[3,128,512]{2,1,0:T(8,128)(2,1)S(1)} %collective-permute-done.2.refs_2_, ...), custom_call_target="tpu_custom_call" | custom-call | flops 1000 | bytes 1000 | tf_op jit(solution)/shard_map/pallas_call | solution.py:170
  29.9 2.5 %collective-permute-done.5.refs_7_ = bf16[2,128,512]{2,1,0:T(8,128)(2,1)S(1)} collective-permute-done((bf16[2,128,512]{2,1,0:T(8,128)(2,1)S(1)}, bf16[2,128,512]{2,1,0:T(8,128)(2,1)S(1)}, u32[]{:S(2)}, u32[]{:S(2)}) %collective-permute-start.5) | collective-permute-done | bytes 262176 | tf_op jit(solution)/shard_map/ppermute | solution.py:435
  32.5 1.5 %collective-permute-start.7 = (bf16[2,128,512]{2,1,0:T(8,128)(2,1)S(1)}, bf16[2,128,512]{2,1,0:T(8,128)(2,1)S(1)}, u32[]{:S(2)}, u32[]{:S(2)}) collective-permute-start(bf16[2,128,512]{2,1,0:T(8,128)(2,1)S(1)} %collective-permute-done.4.refs_5_), channel_id=1, source_target_pairs={{0,1},{1,0},{2,3},{3,2},{4,5},{5,4},{6,7},{7,6},{8,9},{9,8},{10,11... | collective-permute-start | bytes 786440 | tf_op jit(solution)/shard_map/ppermute | solution.py:429
  34.0 0.0 collective-permute-start.8
  34.0 0.1 collective-permute-done.6.refs_8_
  34.1 1.0 %collective-permute-done.7.refs_6_ = bf16[2,128,512]{2,1,0:T(8,128)(2,1)S(1)} collective-permute-done((bf16[2,128,512]{2,1,0:T(8,128)(2,1)S(1)}, bf16[2,128,512]{2,1,0:T(8,128)(2,1)S(1)}, u32[]{:S(2)}, u32[]{:S(2)}) %collective-permute-start.7) | collective-permute-done | bytes 262176 | tf_op jit(solution)/shard_map/ppermute | solution.py:429
  35.1 0.4 collective-permute-done.8.refs_8_
  35.5 0.0 copy-done.1
  35.5 0.0 copy-done.4
  35.5 0.0 copy-start.3
  35.5 0.0 copy-start.5
  35.5 4.7 %shard_map.58 = (bf16[9,64,512]{2,1,0:T(8,128)(2,1)S(1)}, bf16[9,64,512]{2,1,0:T(8,128)(2,1)S(1)}, bf16[12,64,512]{2,1,0:T(8,128)(2,1)S(1)}, bf16[8,64,512]{2,1,0:T(8,128)(2,1)}, bf16[9,512,512]{2,1,0:T(8,128)(2,1)S(1)}) custom-call(bf16[34,64,256]{2,1,0:T(8,128)(2,1)S(1)} %get-tuple-element.30.padded, f32[32,64,512]{2,1,0:T(8,128)S(1)} %get-tuple-element.33.base, ...), custom_call_target="tpu_custom_call" | custom-call | flops 1000 | bytes 1000 | tf_op jit(solution)/shard_map/pallas_call | solution.py:240
  40.2 1.4 %collective-permute-start.13 = (bf16[12,64,512]{2,1,0:T(8,128)(2,1)S(1)}, bf16[12,64,512]{2,1,0:T(8,128)(2,1)S(1)}, u32[]{:S(2)}, u32[]{:S(2)}) collective-permute-start(bf16[12,64,512]{2,1,0:T(8,128)(2,1)S(1)} %get-tuple-element.40.refs_2_), channel_id=1, source_target_pairs={{0,1},{1,0},{2,3},{3,2},{4,5},{5,4},{6,7},{7,6},{8,9},{9,8},{10,11... | collective-permute-start | bytes 2359304 | tf_op jit(solution)/shard_map/ppermute | solution.py:445
  41.6 0.1 collective-permute-start.11
  41.7 0.4 collective-permute-start.12
  42.1 3.3 %collective-permute-start.10 = (bf16[8,64,512]{2,1,0:T(8,128)(2,1)}, bf16[8,64,512]{2,1,0:T(8,128)(2,1)}, u32[]{:S(2)}, u32[]{:S(2)}) collective-permute-start(bf16[8,64,512]{2,1,0:T(8,128)(2,1)} %get-tuple-element.37.refs_0_), channel_id=1, source_target_pairs={{1,2},{2,1},{3,4},{4,3},{5,6},{6,5},{7,8},{8,7},{9,10},{10,9},{11,... | collective-permute-start | bytes 1572872 | tf_op jit(solution)/shard_map/ppermute | solution.py:444
  45.4 0.0 collective-permute-done.14.refs_6_
  45.4 0.1 collective-permute-start.9
  45.5 0.0 collective-permute-done.11.refs_3_
  45.5 0.0 collective-permute-done.12.refs_4_
  45.5 0.0 collective-permute-done.13.refs_5_
  45.5 0.0 copy-done.3
  45.5 0.0 copy-done.5
  45.5 12.0 %shard_map.59 = (bf16[32,64,512]{2,1,0:T(8,128)(2,1)}, bf16[3,512,512]{2,1,0:T(8,128)(2,1)S(1)}) custom-call(bf16[9,64,512]{2,1,0:T(8,128)(2,1)S(1)} %get-tuple-element.38.refs_0_, bf16[9,64,512]{2,1,0:T(8,128)(2,1)S(1)} %get-tuple-element.39.refs_1_, bf16[12,64,512]{2,1,0:T(8,128)(2,1)S(1)} %get-tuple-element.40.refs_2_, ...), custom_call_target="tpu_custom_call" | custom-call | flops 999999995904 | bytes 1000 | tf_op jit(solution)/shard_map/pallas_call | solution.py:375
  57.6 0.0 collective-permute-done.10.refs_2_
  57.6 0.0 collective-permute-done.9.refs_1_
  57.6 3.1 %shard_map.60 = bf16[32,64,512]{2,1,0:T(8,128)(2,1)} custom-call(bf16[8,64,512]{2,1,0:T(8,128)(2,1)} %get-tuple-element.37.refs_0_, bf16[8,64,512]{2,1,0:T(8,128)(2,1)} %collective-permute-done.9.refs_1_, bf16[8,64,512]{2,1,0:T(8,128)(2,1)} %collective-permute-done.10.refs_2_, ...), custom_call_target="tpu_custom_call", output_to_operand_aliasing={{}: (6, {})} | custom-call | flops 1000 | bytes 1000 | tf_op jit(solution)/shard_map/pallas_call | solution.py:375
Async XLA Ops:
  1.9 16.7 %collective-permute-start = (bf16[3,128,512]{2,1,0:T(8,128)(2,1)S(1)}, bf16[3,128,512]{2,1,0:T(8,128)(2,1)S(1)}, u32[]{:S(2)}, u32[]{:S(2)}) collective-permute-start(bf16[3,128,512]{2,1,0:T(8,128)(2,1)S(1)} %get-tuple-element.25), channel_id=1, source_target_pairs={{0,16},{16,0},{1,17},{17,1},{2,18},{18,2},{3,19},{19,3},{4,20},{20... | collective-permute-start | bytes 1179656 | tf_op jit(solution)/shard_map/ppermute | solution.py:426
  4.0 14.5 %collective-permute-start.1 = (bf16[2,128,512]{2,1,0:T(8,128)(2,1)S(1)}, bf16[2,128,512]{2,1,0:T(8,128)(2,1)S(1)}, u32[]{:S(2)}, u32[]{:S(2)}) collective-permute-start(bf16[2,128,512]{2,1,0:T(8,128)(2,1)S(1)} %get-tuple-element.26), channel_id=1, source_target_pairs={{0,16},{16,0},{1,17},{17,1},{2,18},{18,2},{3,19},{19,3},{4,20},{20... | collective-permute-start | bytes 786440 | tf_op jit(solution)/shard_map/ppermute | solution.py:426
  4.1 41.3 %collective-permute-start.14 = (bf16[25,64,512]{2,1,0:T(8,128)(2,1)S(1)}, bf16[25,64,512]{2,1,0:T(8,128)(2,1)S(1)}, u32[]{:S(2)}, u32[]{:S(2)}) collective-permute-start(bf16[25,64,512]{2,1,0:T(8,128)(2,1)S(1)} %get-tuple-element.41), channel_id=1, source_target_pairs={{1,2},{2,1},{3,4},{4,3},{5,6},{6,5},{7,8},{8,7},{9,10},{10,9},{11,... | collective-permute-start | bytes 4915208 | tf_op jit(solution)/shard_map/ppermute | solution.py:425
  8.5 15.6 %collective-permute-start.4 = (bf16[2,128,512]{2,1,0:T(8,128)(2,1)S(1)}, bf16[2,128,512]{2,1,0:T(8,128)(2,1)S(1)}, u32[]{:S(2)}, u32[]{:S(2)}) collective-permute-start(bf16[2,128,512]{2,1,0:T(8,128)(2,1)S(1)} %get-tuple-element.31), channel_id=1, source_target_pairs={{0,16},{16,0},{1,17},{17,1},{2,18},{18,2},{3,19},{19,3},{4,20},{20... | collective-permute-start | bytes 786440 | tf_op jit(solution)/shard_map/ppermute | solution.py:426
  9.8 1.7 %copy-start = (bf16[9,256,512]{2,1,0:T(8,128)(2,1)S(1)}, bf16[9,256,512]{2,1,0:T(8,128)(2,1)}, u32[]{:S(2)}) copy-start(bf16[9,256,512]{2,1,0:T(8,128)(2,1)} %refs_0_.5) | copy-start | bytes 7077892
  11.5 1.6 %copy-start.2 = (bf16[1,1,32,64,512]{4,3,2,1,0:T(8,128)(2,1)S(1)}, bf16[1,1,32,64,512]{4,3,2,1,0:T(8,128)(2,1)}, u32[]{:S(2)}) copy-start(bf16[1,1,32,64,512]{4,3,2,1,0:T(8,128)(2,1)} %param.5) | copy-start | bytes 6291460
  18.6 8.0 %collective-permute-start.2 = (bf16[3,128,512]{2,1,0:T(8,128)(2,1)S(1)}, bf16[3,128,512]{2,1,0:T(8,128)(2,1)S(1)}, u32[]{:S(2)}, u32[]{:S(2)}) collective-permute-start(bf16[3,128,512]{2,1,0:T(8,128)(2,1)S(1)} %collective-permute-done.refs_1_), channel_id=1, source_target_pairs={{0,1},{1,0},{2,3},{3,2},{4,5},{5,4},{6,7},{7,6},{8,9},{9,8},{10,11... | collective-permute-start | bytes 1179656 | tf_op jit(solution)/shard_map/ppermute | solution.py:429
  20.5 6.0 %collective-permute-start.3 = (bf16[2,128,512]{2,1,0:T(8,128)(2,1)S(1)}, bf16[2,128,512]{2,1,0:T(8,128)(2,1)S(1)}, u32[]{:S(2)}, u32[]{:S(2)}) collective-permute-start(bf16[2,128,512]{2,1,0:T(8,128)(2,1)S(1)} %collective-permute-done.1.refs_3_), channel_id=1, source_target_pairs={{0,1},{1,0},{2,3},{3,2},{4,5},{5,4},{6,7},{7,6},{8,9},{9,8},{10,11... | collective-permute-start | bytes 786440 | tf_op jit(solution)/shard_map/ppermute | solution.py:429
  24.1 8.4 %collective-permute-start.5 = (bf16[2,128,512]{2,1,0:T(8,128)(2,1)S(1)}, bf16[2,128,512]{2,1,0:T(8,128)(2,1)S(1)}, u32[]{:S(2)}, u32[]{:S(2)}) collective-permute-start(bf16[2,128,512]{2,1,0:T(8,128)(2,1)S(1)} %collective-permute-done.4.refs_5_), channel_id=1, source_target_pairs={{0,4},{1,5},{2,6},{3,7},{4,0},{5,1},{6,2},{7,3},{8,12},{9,13},{10,... | collective-permute-start | bytes 786440 | tf_op jit(solution)/shard_map/ppermute | solution.py:435
  25.3 10.2 %copy-start.1 = (bf16[9,256,512]{2,1,0:T(8,128)(2,1)S(1)}, bf16[9,256,512]{2,1,0:T(8,128)(2,1)}, u32[]{:S(2)}) copy-start(bf16[9,256,512]{2,1,0:T(8,128)(2,1)} %refs_0_.5) | copy-start | bytes 7077892
  25.3 10.2 %copy-start.4 = (f32[512]{0:T(512)S(1)}, f32[512]{0:T(512)}, u32[]{:S(2)}) copy-start(f32[512]{0:T(512)} %param.8) | copy-start | bytes 6148
  25.3 8.8 %collective-permute-start.6 = (bf16[3,128,512]{2,1,0:T(8,128)(2,1)S(1)}, bf16[3,128,512]{2,1,0:T(8,128)(2,1)S(1)}, u32[]{:S(2)}, u32[]{:S(2)}) collective-permute-start(bf16[3,128,512]{2,1,0:T(8,128)(2,1)S(1)} %get-tuple-element.34), channel_id=1, source_target_pairs={{0,16},{16,0},{1,17},{17,1},{2,18},{18,2},{3,19},{19,3},{4,20},{20... | collective-permute-start | bytes 1179656 | tf_op jit(solution)/shard_map/ppermute | solution.py:438
  32.5 2.6 %collective-permute-start.7 = (bf16[2,128,512]{2,1,0:T(8,128)(2,1)S(1)}, bf16[2,128,512]{2,1,0:T(8,128)(2,1)S(1)}, u32[]{:S(2)}, u32[]{:S(2)}) collective-permute-start(bf16[2,128,512]{2,1,0:T(8,128)(2,1)S(1)} %collective-permute-done.4.refs_5_), channel_id=1, source_target_pairs={{0,1},{1,0},{2,3},{3,2},{4,5},{5,4},{6,7},{7,6},{8,9},{9,8},{10,11... | collective-permute-start | bytes 786440 | tf_op jit(solution)/shard_map/ppermute | solution.py:429
  34.0 1.5 %collective-permute-start.8 = (bf16[2,128,512]{2,1,0:T(8,128)(2,1)S(1)}, bf16[2,128,512]{2,1,0:T(8,128)(2,1)S(1)}, u32[]{:S(2)}, u32[]{:S(2)}) collective-permute-start(bf16[2,128,512]{2,1,0:T(8,128)(2,1)S(1)} %collective-permute-done.5.refs_7_), channel_id=1, source_target_pairs={{0,1},{1,0},{2,3},{3,2},{4,5},{5,4},{6,7},{7,6},{8,9},{9,8},{10,11... | collective-permute-start | bytes 786440 | tf_op jit(solution)/shard_map/ppermute | solution.py:429
  35.5 10.0 %copy-start.3 = (bf16[3,256,512]{2,1,0:T(8,128)(2,1)S(1)}, bf16[3,256,512]{2,1,0:T(8,128)(2,1)}, u32[]{:S(2)}) copy-start(bf16[3,256,512]{2,1,0:T(8,128)(2,1)} %refs_7_.1) | copy-start | bytes 2359300
  35.5 10.0 %copy-start.5 = (f32[512]{0:T(512)S(1)}, f32[512]{0:T(512)}, u32[]{:S(2)}) copy-start(f32[512]{0:T(512)} %param.9) | copy-start | bytes 6148
  40.2 5.3 %collective-permute-start.13 = (bf16[12,64,512]{2,1,0:T(8,128)(2,1)S(1)}, bf16[12,64,512]{2,1,0:T(8,128)(2,1)S(1)}, u32[]{:S(2)}, u32[]{:S(2)}) collective-permute-start(bf16[12,64,512]{2,1,0:T(8,128)(2,1)S(1)} %get-tuple-element.40.refs_2_), channel_id=1, source_target_pairs={{0,1},{1,0},{2,3},{3,2},{4,5},{5,4},{6,7},{7,6},{8,9},{9,8},{10,11... | collective-permute-start | bytes 2359304 | tf_op jit(solution)/shard_map/ppermute | solution.py:445
  41.6 3.9 %collective-permute-start.11 = (bf16[9,64,512]{2,1,0:T(8,128)(2,1)S(1)}, bf16[9,64,512]{2,1,0:T(8,128)(2,1)S(1)}, u32[]{:S(2)}, u32[]{:S(2)}) collective-permute-start(bf16[9,64,512]{2,1,0:T(8,128)(2,1)S(1)} %get-tuple-element.38.refs_0_), channel_id=1, source_target_pairs={{0,1},{1,0},{2,3},{3,2},{4,5},{5,4},{6,7},{7,6},{8,9},{9,8},{10,11... | collective-permute-start | bytes 1769480 | tf_op jit(solution)/shard_map/ppermute | solution.py:445
  41.7 3.8 %collective-permute-start.12 = (bf16[9,64,512]{2,1,0:T(8,128)(2,1)S(1)}, bf16[9,64,512]{2,1,0:T(8,128)(2,1)S(1)}, u32[]{:S(2)}, u32[]{:S(2)}) collective-permute-start(bf16[9,64,512]{2,1,0:T(8,128)(2,1)S(1)} %get-tuple-element.39.refs_1_), channel_id=1, source_target_pairs={{0,1},{1,0},{2,3},{3,2},{4,5},{5,4},{6,7},{7,6},{8,9},{9,8},{10,11... | collective-permute-start | bytes 1769480 | tf_op jit(solution)/shard_map/ppermute | solution.py:445
  42.1 15.4 %collective-permute-start.10 = (bf16[8,64,512]{2,1,0:T(8,128)(2,1)}, bf16[8,64,512]{2,1,0:T(8,128)(2,1)}, u32[]{:S(2)}, u32[]{:S(2)}) collective-permute-start(bf16[8,64,512]{2,1,0:T(8,128)(2,1)} %get-tuple-element.37.refs_0_), channel_id=1, source_target_pairs={{1,2},{2,1},{3,4},{4,3},{5,6},{6,5},{7,8},{8,7},{9,10},{10,9},{11,... | collective-permute-start | bytes 1572872 | tf_op jit(solution)/shard_map/ppermute | solution.py:444
  45.4 12.2 %collective-permute-start.9 = (bf16[8,64,512]{2,1,0:T(8,128)(2,1)}, bf16[8,64,512]{2,1,0:T(8,128)(2,1)}, u32[]{:S(2)}, u32[]{:S(2)}) collective-permute-start(bf16[8,64,512]{2,1,0:T(8,128)(2,1)} %get-tuple-element.37.refs_0_), channel_id=1, source_target_pairs={{0,1},{1,0},{2,3},{3,2},{4,5},{5,4},{6,7},{7,6},{8,9},{9,8},{10,11... | collective-permute-start | bytes 1572872 | tf_op jit(solution)/shard_map/ppermute | solution.py:445

commit v7 on v6

--- a/solution.py
+++ b/solution.py
@@ -438,7 +438,7 @@
     c_y = lax.ppermute(c_y, "dp", swap)
     tail = c_y.reshape(-1, breadth, width)
     parts = [spatial_filter, *early, *late]
-    *own, spatial = own_call(padded, base, biases[0], tail, parts, range(middle, 9), 16, blocks, light)
+    *own, spatial = own_call(padded, base, biases[0], tail, parts, range(middle, 9), 8, blocks, light)
     temporal_parts = [temporal_filter, c_y]
 
     last = lax.ppermute(own[-1], "tile", across)

time: 61.6 us -> 61.3 us (level)
  no operation moved by 1% of the time
where the time goes in v7:
time: 61.3 us; the launch traced here: 60.7 us
  Pallas kernels  30.4 us (50%)
  starting transfers between devices  19 us (31%)
  waiting for transfers between devices  7.65 us (12%)
  local copies, waits for them, and re-layouts  3.27 us (5%)
    pallas_call x2, Pallas kernels, mix_call(): pl.pallas_call(functools.partial(mix_kernel, rows, begin, sizes, given, t...  15.2 us
    pallas_call x2, Pallas kernels, conv_call(): pl.pallas_call(functools.partial(conv_kernel, rows, taps, held), grid=(st...  8.89 us
    pallas_call x1, Pallas kernels, own_call(): pl.pallas_call(functools.partial(own_kernel, rows, blocks, taps), in_spec...  4.45 us
    ppermute x1, starting transfers between devices, near_device(): far = lax.ppermute(far, 'tile', across)  4.38 us
    ppermute x3, waiting for transfers between devices, near_device(): fetched = [lax.ppermute(piece, 'dp', swap) for piece in cut]  3.56 us
    ppermute x3, starting transfers between devices, near_device(): fetched = [lax.ppermute(piece, 'dp', swap) for piece in cut]  3.52 us
    ppermute x4, starting transfers between devices, both(): lax.ppermute(piece, 'tile', mates)  3.44 us
    unnamed x12, local copies, waits for them, and re-layouts  3.27 us
  transfers between devices with their start and end apart: 15, of which 5 were waited for; matrix products, arithmetic and copies ran while one was open for 0% of the time, Pallas kernels for 42%

profile of v7, /device:TPU:1, one launch (start us, length us, event | category | flops | bytes accessed | tf_op | source)
XLA Modules:
  0.0 60.7 jit_solution(7089209448714834468)
XLA Ops:
  0.0 1.9 %shard_map.55 = (bf16[3,128,512]{2,1,0:T(8,128)(2,1)S(1)}, bf16[2,128,512]{2,1,0:T(8,128)(2,1)S(1)}, bf16[2,128,512]{2,1,0:T(8,128)(2,1)S(1)}, bf16[3,128,512]{2,1,0:T(8,128)(2,1)S(1)}, bf16[25,64,512]{2,1,0:T(8,128)(2,1)S(1)}) custom-call(bf16[9,256,512]{2,1,0:T(8,128)(2,1)} %refs_0_.5, bf16[3,256,512]{2,1,0:T(8,128)(2,1)} %refs_7_.1, ...), custom_call_target="tpu_custom_call" | custom-call | flops 1000 | bytes 1000 | tf_op jit(solution)/shard_map/pallas_call | solution.py:80
  1.9 2.1 %collective-permute-start = (bf16[3,128,512]{2,1,0:T(8,128)(2,1)S(1)}, bf16[3,128,512]{2,1,0:T(8,128)(2,1)S(1)}, u32[]{:S(2)}, u32[]{:S(2)}) collective-permute-start(bf16[3,128,512]{2,1,0:T(8,128)(2,1)S(1)} %get-tuple-element.25), channel_id=1, source_target_pairs={{0,16},{16,0},{1,17},{17,1},{2,18},{18,2},{3,19},{19,3},{4,20},{20... | collective-permute-start | bytes 1179656 | tf_op jit(solution)/shard_map/ppermute | solution.py:426
  4.0 0.1 collective-permute-start.1
  4.1 4.4 %collective-permute-start.14 = (bf16[25,64,512]{2,1,0:T(8,128)(2,1)S(1)}, bf16[25,64,512]{2,1,0:T(8,128)(2,1)S(1)}, u32[]{:S(2)}, u32[]{:S(2)}) collective-permute-start(bf16[25,64,512]{2,1,0:T(8,128)(2,1)S(1)} %get-tuple-element.41), channel_id=1, source_target_pairs={{1,2},{2,1},{3,4},{4,3},{5,6},{6,5},{7,8},{8,7},{9,10},{10,9},{11,... | collective-permute-start | bytes 4915208 | tf_op jit(solution)/shard_map/ppermute | solution.py:425
  8.5 1.3 %collective-permute-start.4 = (bf16[2,128,512]{2,1,0:T(8,128)(2,1)S(1)}, bf16[2,128,512]{2,1,0:T(8,128)(2,1)S(1)}, u32[]{:S(2)}, u32[]{:S(2)}) collective-permute-start(bf16[2,128,512]{2,1,0:T(8,128)(2,1)S(1)} %get-tuple-element.31), channel_id=1, source_target_pairs={{0,16},{16,0},{1,17},{17,1},{2,18},{18,2},{3,19},{19,3},{4,20},{20... | collective-permute-start | bytes 786440 | tf_op jit(solution)/shard_map/ppermute | solution.py:426
  9.8 0.0 copy-start
  9.8 1.7 %copy-done = bf16[9,256,512]{2,1,0:T(8,128)(2,1)S(1)} copy-done((bf16[9,256,512]{2,1,0:T(8,128)(2,1)S(1)}, bf16[9,256,512]{2,1,0:T(8,128)(2,1)}, u32[]{:S(2)}) %copy-start) | copy-done | bytes 2359320
  11.5 0.0 copy-start.2
  11.5 1.6 %copy-done.2 = bf16[1,1,32,64,512]{4,3,2,1,0:T(8,128)(2,1)S(1)} copy-done((bf16[1,1,32,64,512]{4,3,2,1,0:T(8,128)(2,1)S(1)}, bf16[1,1,32,64,512]{4,3,2,1,0:T(8,128)(2,1)}, u32[]{:S(2)}) %copy-start.2) | copy-done | bytes 2097176
  13.1 5.5 %shard_map.56.refs_0_ = f32[32,64,512]{2,1,0:T(8,128)S(1)} custom-call(bf16[32,64,512]{2,1,0:T(8,128)(2,1)S(1)} %bitcast.6, bf16[9,256,512]{2,1,0:T(8,128)(2,1)S(1)} %copy-done), custom_call_target="tpu_custom_call" | custom-call | flops 1000 | bytes 1000 | tf_op jit(solution)/shard_map/pallas_call | solution.py:170
  18.6 0.0 collective-permute-done.1.refs_3_
  18.6 0.0 collective-permute-done.refs_1_
  18.6 2.0 %collective-permute-start.2 = (bf16[3,128,512]{2,1,0:T(8,128)(2,1)S(1)}, bf16[3,128,512]{2,1,0:T(8,128)(2,1)S(1)}, u32[]{:S(2)}, u32[]{:S(2)}) collective-permute-start(bf16[3,128,512]{2,1,0:T(8,128)(2,1)S(1)} %collective-permute-done.refs_1_), channel_id=1, source_target_pairs={{0,1},{1,0},{2,3},{3,2},{4,5},{5,4},{6,7},{7,6},{8,9},{9,8},{10,11... | collective-permute-start | bytes 1179656 | tf_op jit(solution)/shard_map/ppermute | solution.py:429
  20.5 0.0 collective-permute-start.3
  20.5 3.6 %collective-permute-done.4.refs_5_ = bf16[2,128,512]{2,1,0:T(8,128)(2,1)S(1)} collective-permute-done((bf16[2,128,512]{2,1,0:T(8,128)(2,1)S(1)}, bf16[2,128,512]{2,1,0:T(8,128)(2,1)S(1)}, u32[]{:S(2)}, u32[]{:S(2)}) %collective-permute-start.4) | collective-permute-done | bytes 262176 | tf_op jit(solution)/shard_map/ppermute | solution.py:426
  24.1 1.2 %collective-permute-start.5 = (bf16[2,128,512]{2,1,0:T(8,128)(2,1)S(1)}, bf16[2,128,512]{2,1,0:T(8,128)(2,1)S(1)}, u32[]{:S(2)}, u32[]{:S(2)}) collective-permute-start(bf16[2,128,512]{2,1,0:T(8,128)(2,1)S(1)} %collective-permute-done.4.refs_5_), channel_id=1, source_target_pairs={{0,4},{1,5},{2,6},{3,7},{4,0},{5,1},{6,2},{7,3},{8,12},{9,13},{10,... | collective-permute-start | bytes 786440 | tf_op jit(solution)/shard_map/ppermute | solution.py:435
  25.3 0.0 copy-start.1
  25.3 0.0 copy-start.4
  25.3 1.2 %collective-permute-start.6 = (bf16[3,128,512]{2,1,0:T(8,128)(2,1)S(1)}, bf16[3,128,512]{2,1,0:T(8,128)(2,1)S(1)}, u32[]{:S(2)}, u32[]{:S(2)}) collective-permute-start(bf16[3,128,512]{2,1,0:T(8,128)(2,1)S(1)} %get-tuple-element.34), channel_id=1, source_target_pairs={{0,16},{16,0},{1,17},{17,1},{2,18},{18,2},{3,19},{19,3},{4,20},{20... | collective-permute-start | bytes 1179656 | tf_op jit(solution)/shard_map/ppermute | solution.py:438
  26.5 0.0 collective-permute-done.3.refs_4_
  26.5 0.0 collective-permute-done.2.refs_2_
  26.6 3.4 %shard_map.57 = (f32[32,64,512]{2,1,0:T(8,128)S(1)}, bf16[34,64,256]{2,1,0:T(8,128)(2,1)S(1)}) custom-call(bf16[32,64,512]{2,1,0:T(8,128)(2,1)S(1)} %bitcast.7, f32[32,64,512]{2,1,0:T(8,128)S(1)} %shard_map.56.refs_0_, bf16[3,128,512]{2,1,0:T(8,128)(2,1)S(1)} %collective-permute-done.refs_1_, bf16[3,128,512]{2,1,0:T(8,128)(2,1)S(1)} %collective-permute-done.2.refs_2_, ...), custom_call_target="tpu_custom_call" | custom-call | flops 1000 | bytes 1000 | tf_op jit(solution)/shard_map/pallas_call | solution.py:170
  29.9 2.5 %collective-permute-done.5.refs_7_ = bf16[2,128,512]{2,1,0:T(8,128)(2,1)S(1)} collective-permute-done((bf16[2,128,512]{2,1,0:T(8,128)(2,1)S(1)}, bf16[2,128,512]{2,1,0:T(8,128)(2,1)S(1)}, u32[]{:S(2)}, u32[]{:S(2)}) %collective-permute-start.5) | collective-permute-done | bytes 262176 | tf_op jit(solution)/shard_map/ppermute | solution.py:435
  32.5 1.5 %collective-permute-start.7 = (bf16[2,128,512]{2,1,0:T(8,128)(2,1)S(1)}, bf16[2,128,512]{2,1,0:T(8,128)(2,1)S(1)}, u32[]{:S(2)}, u32[]{:S(2)}) collective-permute-start(bf16[2,128,512]{2,1,0:T(8,128)(2,1)S(1)} %collective-permute-done.4.refs_5_), channel_id=1, source_target_pairs={{0,1},{1,0},{2,3},{3,2},{4,5},{5,4},{6,7},{7,6},{8,9},{9,8},{10,11... | collective-permute-start | bytes 786440 | tf_op jit(solution)/shard_map/ppermute | solution.py:429
  34.0 0.0 collective-permute-start.8
  34.0 0.1 collective-permute-done.6.refs_8_
  34.1 1.0 %collective-permute-done.7.refs_6_ = bf16[2,128,512]{2,1,0:T(8,128)(2,1)S(1)} collective-permute-done((bf16[2,128,512]{2,1,0:T(8,128)(2,1)S(1)}, bf16[2,128,512]{2,1,0:T(8,128)(2,1)S(1)}, u32[]{:S(2)}, u32[]{:S(2)}) %collective-permute-start.7) | collective-permute-done | bytes 262176 | tf_op jit(solution)/shard_map/ppermute | solution.py:429
  35.1 0.4 collective-permute-done.8.refs_8_
  35.5 0.0 copy-done.1
  35.5 0.0 copy-done.4
  35.5 0.0 copy-start.3
  35.5 0.0 copy-start.5
  35.5 4.4 %shard_map.58 = (bf16[9,64,512]{2,1,0:T(8,128)(2,1)S(1)}, bf16[9,64,512]{2,1,0:T(8,128)(2,1)S(1)}, bf16[12,64,512]{2,1,0:T(8,128)(2,1)S(1)}, bf16[8,64,512]{2,1,0:T(8,128)(2,1)}, bf16[9,512,512]{2,1,0:T(8,128)(2,1)S(1)}) custom-call(bf16[34,64,256]{2,1,0:T(8,128)(2,1)S(1)} %get-tuple-element.30.padded, f32[32,64,512]{2,1,0:T(8,128)S(1)} %get-tuple-element.33.base, ...), custom_call_target="tpu_custom_call" | custom-call | flops 1000 | bytes 1000 | tf_op jit(solution)/shard_map/pallas_call | solution.py:240
  40.0 1.4 %collective-permute-start.13 = (bf16[12,64,512]{2,1,0:T(8,128)(2,1)S(1)}, bf16[12,64,512]{2,1,0:T(8,128)(2,1)S(1)}, u32[]{:S(2)}, u32[]{:S(2)}) collective-permute-start(bf16[12,64,512]{2,1,0:T(8,128)(2,1)S(1)} %get-tuple-element.40.refs_2_), channel_id=1, source_target_pairs={{0,1},{1,0},{2,3},{3,2},{4,5},{5,4},{6,7},{7,6},{8,9},{9,8},{10,11... | collective-permute-start | bytes 2359304 | tf_op jit(solution)/shard_map/ppermute | solution.py:445
  41.4 0.1 collective-permute-start.11
  41.5 0.4 collective-permute-start.12
  41.9 3.3 %collective-permute-start.10 = (bf16[8,64,512]{2,1,0:T(8,128)(2,1)}, bf16[8,64,512]{2,1,0:T(8,128)(2,1)}, u32[]{:S(2)}, u32[]{:S(2)}) collective-permute-start(bf16[8,64,512]{2,1,0:T(8,128)(2,1)} %get-tuple-element.37.refs_0_), channel_id=1, source_target_pairs={{1,2},{2,1},{3,4},{4,3},{5,6},{6,5},{7,8},{8,7},{9,10},{10,9},{11,... | collective-permute-start | bytes 1572872 | tf_op jit(solution)/shard_map/ppermute | solution.py:444
  45.2 0.0 collective-permute-done.14.refs_6_
  45.2 0.1 collective-permute-start.9
  45.3 0.0 collective-permute-done.11.refs_3_
  45.3 0.0 collective-permute-done.12.refs_4_
  45.3 0.0 collective-permute-done.13.refs_5_
  45.3 0.0 copy-done.3
  45.3 0.0 copy-done.5
  45.3 12.0 %shard_map.59 = (bf16[32,64,512]{2,1,0:T(8,128)(2,1)}, bf16[3,512,512]{2,1,0:T(8,128)(2,1)S(1)}) custom-call(bf16[9,64,512]{2,1,0:T(8,128)(2,1)S(1)} %get-tuple-element.38.refs_0_, bf16[9,64,512]{2,1,0:T(8,128)(2,1)S(1)} %get-tuple-element.39.refs_1_, bf16[12,64,512]{2,1,0:T(8,128)(2,1)S(1)} %get-tuple-element.40.refs_2_, ...), custom_call_target="tpu_custom_call" | custom-call | flops 999999995904 | bytes 1000 | tf_op jit(solution)/shard_map/pallas_call | solution.py:375
  57.3 0.0 collective-permute-done.10.refs_2_
  57.4 0.0 collective-permute-done.9.refs_1_
  57.4 3.1 %shard_map.60 = bf16[32,64,512]{2,1,0:T(8,128)(2,1)} custom-call(bf16[8,64,512]{2,1,0:T(8,128)(2,1)} %get-tuple-element.37.refs_0_, bf16[8,64,512]{2,1,0:T(8,128)(2,1)} %collective-permute-done.9.refs_1_, bf16[8,64,512]{2,1,0:T(8,128)(2,1)} %collective-permute-done.10.refs_2_, ...), custom_call_target="tpu_custom_call", output_to_operand_aliasing={{}: (6, {})} | custom-call | flops 1000 | bytes 1000 | tf_op jit(solution)/shard_map/pallas_call | solution.py:375
Async XLA Ops:
  1.9 16.7 %collective-permute-start = (bf16[3,128,512]{2,1,0:T(8,128)(2,1)S(1)}, bf16[3,128,512]{2,1,0:T(8,128)(2,1)S(1)}, u32[]{:S(2)}, u32[]{:S(2)}) collective-permute-start(bf16[3,128,512]{2,1,0:T(8,128)(2,1)S(1)} %get-tuple-element.25), channel_id=1, source_target_pairs={{0,16},{16,0},{1,17},{17,1},{2,18},{18,2},{3,19},{19,3},{4,20},{20... | collective-permute-start | bytes 1179656 | tf_op jit(solution)/shard_map/ppermute | solution.py:426
  4.0 14.5 %collective-permute-start.1 = (bf16[2,128,512]{2,1,0:T(8,128)(2,1)S(1)}, bf16[2,128,512]{2,1,0:T(8,128)(2,1)S(1)}, u32[]{:S(2)}, u32[]{:S(2)}) collective-permute-start(bf16[2,128,512]{2,1,0:T(8,128)(2,1)S(1)} %get-tuple-element.26), channel_id=1, source_target_pairs={{0,16},{16,0},{1,17},{17,1},{2,18},{18,2},{3,19},{19,3},{4,20},{20... | collective-permute-start | bytes 786440 | tf_op jit(solution)/shard_map/ppermute | solution.py:426
  4.1 41.1 %collective-permute-start.14 = (bf16[25,64,512]{2,1,0:T(8,128)(2,1)S(1)}, bf16[25,64,512]{2,1,0:T(8,128)(2,1)S(1)}, u32[]{:S(2)}, u32[]{:S(2)}) collective-permute-start(bf16[25,64,512]{2,1,0:T(8,128)(2,1)S(1)} %get-tuple-element.41), channel_id=1, source_target_pairs={{1,2},{2,1},{3,4},{4,3},{5,6},{6,5},{7,8},{8,7},{9,10},{10,9},{11,... | collective-permute-start | bytes 4915208 | tf_op jit(solution)/shard_map/ppermute | solution.py:425
  8.5 15.6 %collective-permute-start.4 = (bf16[2,128,512]{2,1,0:T(8,128)(2,1)S(1)}, bf16[2,128,512]{2,1,0:T(8,128)(2,1)S(1)}, u32[]{:S(2)}, u32[]{:S(2)}) collective-permute-start(bf16[2,128,512]{2,1,0:T(8,128)(2,1)S(1)} %get-tuple-element.31), channel_id=1, source_target_pairs={{0,16},{16,0},{1,17},{17,1},{2,18},{18,2},{3,19},{19,3},{4,20},{20... | collective-permute-start | bytes 786440 | tf_op jit(solution)/shard_map/ppermute | solution.py:426
  9.8 1.7 %copy-start = (bf16[9,256,512]{2,1,0:T(8,128)(2,1)S(1)}, bf16[9,256,512]{2,1,0:T(8,128)(2,1)}, u32[]{:S(2)}) copy-start(bf16[9,256,512]{2,1,0:T(8,128)(2,1)} %refs_0_.5) | copy-start | bytes 7077892
  11.5 1.6 %copy-start.2 = (bf16[1,1,32,64,512]{4,3,2,1,0:T(8,128)(2,1)S(1)}, bf16[1,1,32,64,512]{4,3,2,1,0:T(8,128)(2,1)}, u32[]{:S(2)}) copy-start(bf16[1,1,32,64,512]{4,3,2,1,0:T(8,128)(2,1)} %param.5) | copy-start | bytes 6291460
  18.6 8.0 %collective-permute-start.2 = (bf16[3,128,512]{2,1,0:T(8,128)(2,1)S(1)}, bf16[3,128,512]{2,1,0:T(8,128)(2,1)S(1)}, u32[]{:S(2)}, u32[]{:S(2)}) collective-permute-start(bf16[3,128,512]{2,1,0:T(8,128)(2,1)S(1)} %collective-permute-done.refs_1_), channel_id=1, source_target_pairs={{0,1},{1,0},{2,3},{3,2},{4,5},{5,4},{6,7},{7,6},{8,9},{9,8},{10,11... | collective-permute-start | bytes 1179656 | tf_op jit(solution)/shard_map/ppermute | solution.py:429
  20.5 6.0 %collective-permute-start.3 = (bf16[2,128,512]{2,1,0:T(8,128)(2,1)S(1)}, bf16[2,128,512]{2,1,0:T(8,128)(2,1)S(1)}, u32[]{:S(2)}, u32[]{:S(2)}) collective-permute-start(bf16[2,128,512]{2,1,0:T(8,128)(2,1)S(1)} %collective-permute-done.1.refs_3_), channel_id=1, source_target_pairs={{0,1},{1,0},{2,3},{3,2},{4,5},{5,4},{6,7},{7,6},{8,9},{9,8},{10,11... | collective-permute-start | bytes 786440 | tf_op jit(solution)/shard_map/ppermute | solution.py:429
  24.1 8.4 %collective-permute-start.5 = (bf16[2,128,512]{2,1,0:T(8,128)(2,1)S(1)}, bf16[2,128,512]{2,1,0:T(8,128)(2,1)S(1)}, u32[]{:S(2)}, u32[]{:S(2)}) collective-permute-start(bf16[2,128,512]{2,1,0:T(8,128)(2,1)S(1)} %collective-permute-done.4.refs_5_), channel_id=1, source_target_pairs={{0,4},{1,5},{2,6},{3,7},{4,0},{5,1},{6,2},{7,3},{8,12},{9,13},{10,... | collective-permute-start | bytes 786440 | tf_op jit(solution)/shard_map/ppermute | solution.py:435
  25.3 10.2 %copy-start.1 = (bf16[9,256,512]{2,1,0:T(8,128)(2,1)S(1)}, bf16[9,256,512]{2,1,0:T(8,128)(2,1)}, u32[]{:S(2)}) copy-start(bf16[9,256,512]{2,1,0:T(8,128)(2,1)} %refs_0_.5) | copy-start | bytes 7077892
  25.3 10.2 %copy-start.4 = (f32[512]{0:T(512)S(1)}, f32[512]{0:T(512)}, u32[]{:S(2)}) copy-start(f32[512]{0:T(512)} %param.8) | copy-start | bytes 6148
  25.3 8.8 %collective-permute-start.6 = (bf16[3,128,512]{2,1,0:T(8,128)(2,1)S(1)}, bf16[3,128,512]{2,1,0:T(8,128)(2,1)S(1)}, u32[]{:S(2)}, u32[]{:S(2)}) collective-permute-start(bf16[3,128,512]{2,1,0:T(8,128)(2,1)S(1)} %get-tuple-element.34), channel_id=1, source_target_pairs={{0,16},{16,0},{1,17},{17,1},{2,18},{18,2},{3,19},{19,3},{4,20},{20... | collective-permute-start | bytes 1179656 | tf_op jit(solution)/shard_map/ppermute | solution.py:438
  32.5 2.6 %collective-permute-start.7 = (bf16[2,128,512]{2,1,0:T(8,128)(2,1)S(1)}, bf16[2,128,512]{2,1,0:T(8,128)(2,1)S(1)}, u32[]{:S(2)}, u32[]{:S(2)}) collective-permute-start(bf16[2,128,512]{2,1,0:T(8,128)(2,1)S(1)} %collective-permute-done.4.refs_5_), channel_id=1, source_target_pairs={{0,1},{1,0},{2,3},{3,2},{4,5},{5,4},{6,7},{7,6},{8,9},{9,8},{10,11... | collective-permute-start | bytes 786440 | tf_op jit(solution)/shard_map/ppermute | solution.py:429
  34.0 1.5 %collective-permute-start.8 = (bf16[2,128,512]{2,1,0:T(8,128)(2,1)S(1)}, bf16[2,128,512]{2,1,0:T(8,128)(2,1)S(1)}, u32[]{:S(2)}, u32[]{:S(2)}) collective-permute-start(bf16[2,128,512]{2,1,0:T(8,128)(2,1)S(1)} %collective-permute-done.5.refs_7_), channel_id=1, source_target_pairs={{0,1},{1,0},{2,3},{3,2},{4,5},{5,4},{6,7},{7,6},{8,9},{9,8},{10,11... | collective-permute-start | bytes 786440 | tf_op jit(solution)/shard_map/ppermute | solution.py:429
  35.5 9.8 %copy-start.3 = (bf16[3,256,512]{2,1,0:T(8,128)(2,1)S(1)}, bf16[3,256,512]{2,1,0:T(8,128)(2,1)}, u32[]{:S(2)}) copy-start(bf16[3,256,512]{2,1,0:T(8,128)(2,1)} %refs_7_.1) | copy-start | bytes 2359300
  35.5 9.8 %copy-start.5 = (f32[512]{0:T(512)S(1)}, f32[512]{0:T(512)}, u32[]{:S(2)}) copy-start(f32[512]{0:T(512)} %param.9) | copy-start | bytes 6148
  40.0 5.3 %collective-permute-start.13 = (bf16[12,64,512]{2,1,0:T(8,128)(2,1)S(1)}, bf16[12,64,512]{2,1,0:T(8,128)(2,1)S(1)}, u32[]{:S(2)}, u32[]{:S(2)}) collective-permute-start(bf16[12,64,512]{2,1,0:T(8,128)(2,1)S(1)} %get-tuple-element.40.refs_2_), channel_id=1, source_target_pairs={{0,1},{1,0},{2,3},{3,2},{4,5},{5,4},{6,7},{7,6},{8,9},{9,8},{10,11... | collective-permute-start | bytes 2359304 | tf_op jit(solution)/shard_map/ppermute | solution.py:445
  41.4 3.9 %collective-permute-start.11 = (bf16[9,64,512]{2,1,0:T(8,128)(2,1)S(1)}, bf16[9,64,512]{2,1,0:T(8,128)(2,1)S(1)}, u32[]{:S(2)}, u32[]{:S(2)}) collective-permute-start(bf16[9,64,512]{2,1,0:T(8,128)(2,1)S(1)} %get-tuple-element.38.refs_0_), channel_id=1, source_target_pairs={{0,1},{1,0},{2,3},{3,2},{4,5},{5,4},{6,7},{7,6},{8,9},{9,8},{10,11... | collective-permute-start | bytes 1769480 | tf_op jit(solution)/shard_map/ppermute | solution.py:445
  41.5 3.8 %collective-permute-start.12 = (bf16[9,64,512]{2,1,0:T(8,128)(2,1)S(1)}, bf16[9,64,512]{2,1,0:T(8,128)(2,1)S(1)}, u32[]{:S(2)}, u32[]{:S(2)}) collective-permute-start(bf16[9,64,512]{2,1,0:T(8,128)(2,1)S(1)} %get-tuple-element.39.refs_1_), channel_id=1, source_target_pairs={{0,1},{1,0},{2,3},{3,2},{4,5},{5,4},{6,7},{7,6},{8,9},{9,8},{10,11... | collective-permute-start | bytes 1769480 | tf_op jit(solution)/shard_map/ppermute | solution.py:445
  41.9 15.4 %collective-permute-start.10 = (bf16[8,64,512]{2,1,0:T(8,128)(2,1)}, bf16[8,64,512]{2,1,0:T(8,128)(2,1)}, u32[]{:S(2)}, u32[]{:S(2)}) collective-permute-start(bf16[8,64,512]{2,1,0:T(8,128)(2,1)} %get-tuple-element.37.refs_0_), channel_id=1, source_target_pairs={{1,2},{2,1},{3,4},{4,3},{5,6},{6,5},{7,8},{8,7},{9,10},{10,9},{11,... | collective-permute-start | bytes 1572872 | tf_op jit(solution)/shard_map/ppermute | solution.py:444
  45.2 12.2 %collective-permute-start.9 = (bf16[8,64,512]{2,1,0:T(8,128)(2,1)}, bf16[8,64,512]{2,1,0:T(8,128)(2,1)}, u32[]{:S(2)}, u32[]{:S(2)}) collective-permute-start(bf16[8,64,512]{2,1,0:T(8,128)(2,1)} %get-tuple-element.37.refs_0_), channel_id=1, source_target_pairs={{0,1},{1,0},{2,3},{3,2},{4,5},{5,4},{6,7},{7,6},{8,9},{9,8},{10,11... | collective-permute-start | bytes 1572872 | tf_op jit(solution)/shard_map/ppermute | solution.py:445
